TPU v7x, 128 devices: a whole 4x4x4 slice. The times are simulated.
128 devices in a mesh: gx: 4 (over y), gy: 4 (over z), gz: 8 (over x, core).
Axes of the slice: x: 4, y: 4, z: 4, core: 2. Of those that a mesh axis runs over, the one named last changes fastest.
Arguments:
- positions: float32 [3, 1048576], P(None, ('gx', 'gy', 'gz')), may hold values from 0 to 1
- velocities: float32 [3, 1048576], P(None, ('gx', 'gy', 'gz')), may hold values from -6 to 6
- masses: float32 [1048576], P(('gx', 'gy', 'gz')), may hold values from 0.004 to 0.016
- time_bins: int32 [1048576], P(('gx', 'gy', 'gz')), may hold values from 0 to 3
- pair_owner: int32 [2, 16384, 2], P(None, ('gx', 'gy', 'gz')), may hold values from 0 to 127, all different within a row; in each aligned block of 128 rows (0 to 127, 128 to 255, ..., all dimensions but the last counted through in order) at most 4 rows name the same one
- pair_slot: int32 [2, 16384, 2], P(None, ('gx', 'gy', 'gz')), may hold values from 0 to 63
- local_pairs: int32 [2, 8192, 2], P(None, ('gx', 'gy', 'gz')), may hold values from 0 to 63
Outputs:
- new_positions: float32 [3, 1048576], P(None, ('gx', 'gy', 'gz'))
- new_velocities: float32 [3, 1048576], P(None, ('gx', 'gy', 'gz'))
- accel: float32 [3, 1048576], P(None, ('gx', 'gy', 'gz'))
Inputs may be any that keep to these rules, and one draw needn't show every extreme that they name: `pair_owner`: each row names two different owners. Within the 128 rows of one device in one subcycle no owner is named more than 4 times, and some owner reaches exactly 4. `local_pairs`: A row may name the same leaf twice.
All inputs are finite; a program needn't handle non-finite values.
Results may differ from a plain program's by a relative error of at most 0.0003.
Values sent between devices are 32-bit elements; how exact they have to be, the bound alone decides.
No kernel may reach another device: no remote copies, remote signals or barrier semaphores. Data moves between devices by JAX's collectives and lax.ppermute only.
A program may use at most 64 MiB of HBM per device.

v0:
```python
import jax
import jax.numpy as jnp
from jax import lax
from jax.sharding import PartitionSpec as P

LEAF = 128


SOFTENING = 0.01
CUTOFF_SQ = 0.04
TIME_STEP = 0.05


def pair_forces(left_leaf, right_leaf):
    offset = right_leaf[:, :3, None, :] - left_leaf[:, :3, :, None]
    dist_sq = jnp.sum(offset * offset, axis=1)
    softened = dist_sq + SOFTENING
    taper = jnp.maximum(1.0 - dist_sq / CUTOFF_SQ, 0.0)
    kernel = taper * taper / (softened * jnp.sqrt(softened))
    on_left = jnp.sum(offset * (kernel * right_leaf[:, 3, None, :])[:, None], axis=3)
    on_right = -jnp.sum(offset * (kernel * left_leaf[:, 3, :, None])[:, None], axis=2)
    return (on_left, on_right)


def blocked_forces(left_leaf, right_leaf):
    count = left_leaf.shape[0]
    width = left_leaf.shape[2]
    block_size = 32
    shaped_left = left_leaf.reshape((count // block_size, block_size) + left_leaf.shape[1:])
    shaped_right = right_leaf.reshape((count // block_size, block_size) + right_leaf.shape[1:])
    force_left, force_right = lax.map(
        lambda pair: pair_forces(pair[0], pair[1]), (shaped_left, shaped_right)
    )
    return (force_left.reshape((count, 3, width)), force_right.reshape((count, 3, width)))


def deliver_leaves(looked):
    result = lax.all_to_all(looked, ("gx", "gy", "gz"), split_axis=0, concat_axis=0, tiled=True)
    return result


def return_forces(pushed):
    result = lax.all_to_all(pushed, ("gx", "gy", "gz"), split_axis=0, concat_axis=0, tiled=True)
    return result


def gather_onto(leaf_ids, forces, nleaf):
    selector = (leaf_ids[:, None] == jnp.arange(nleaf, dtype=jnp.int32)[None, :]).astype(
        jnp.float32
    )
    flat = forces.reshape(forces.shape[0], -1)
    return jnp.dot(
        selector.T, flat, precision=lax.Precision.HIGHEST, preferred_element_type=jnp.float32
    )


def shards(positions, velocities, masses, time_bins, pair_owner, pair_slot, local_pairs):
    devices = lax.axis_size(("gx", "gy", "gz"))
    width = LEAF
    nleaf = positions.shape[1] // width
    pair_rows = pair_owner.shape[1]
    capacity = max(2, 4 * pair_rows // devices)
    current = positions
    moving = velocities
    accel = jnp.zeros_like(positions)
    for subcycle in range(2):
        leaves = jnp.concatenate(
            [current.reshape(3, nleaf, width), masses.reshape(1, nleaf, width)], axis=0
        ).transpose(1, 0, 2)
        owners = pair_owner[subcycle].reshape(-1)
        leaf_slots = pair_slot[subcycle].reshape(-1)
        owner_hits = (owners[:, None] == jnp.arange(devices, dtype=jnp.int32)[None, :]).astype(
            jnp.int32
        )
        slot_rank = jnp.sum((jnp.cumsum(owner_hits, axis=0) - 1) * owner_hits, axis=1)
        placed = owners * capacity + slot_rank
        wanted = (
            jnp.full((devices * capacity,), -1, jnp.int32)
            .at[placed]
            .set(leaf_slots)
            .reshape(devices, capacity)
        )
        asked_for = lax.all_to_all(
            wanted, ("gx", "gy", "gz"), split_axis=0, concat_axis=0, tiled=True
        )
        filled = asked_for >= 0
        looked = jnp.where(filled[:, :, None, None], leaves[jnp.maximum(asked_for, 0)], 0.0)
        local_ids = local_pairs[subcycle]
        local_left, local_right = blocked_forces(leaves[local_ids[:, 0]], leaves[local_ids[:, 1]])
        arrived = deliver_leaves(looked).reshape(devices * capacity, 4, width)
        pair_ends = arrived[placed].reshape(pair_rows, 2, 4, width)
        force_left, force_right = blocked_forces(pair_ends[:, 0], pair_ends[:, 1])
        end_forces = jnp.stack([force_left, force_right], axis=1).reshape(2 * pair_rows, 3, width)
        pushed = jnp.zeros((devices * capacity, 3, width), jnp.float32).at[placed].set(end_forces)
        returned = return_forces(pushed.reshape(devices, capacity, 3, width))
        summed = gather_onto(
            asked_for.reshape(-1), returned.reshape(devices * capacity, 3, width), nleaf
        )
        local_both = jnp.concatenate([local_ids[:, 0], local_ids[:, 1]], axis=0)
        local_forces = jnp.concatenate([local_left, local_right], axis=0)
        summed = summed + gather_onto(local_both, local_forces, nleaf)
        accel = summed.reshape(nleaf, 3, width).transpose(1, 0, 2).reshape(3, nleaf * width)
        active = (time_bins >= 3 - subcycle).astype(jnp.float32)
        moving = moving + TIME_STEP * accel * active[None, :]
        current = current + TIME_STEP * moving
    return (current, moving, accel)


def solution(mesh):
    return jax.shard_map(
        shards,
        mesh=mesh,
        in_specs=(
            P(None, ("gx", "gy", "gz")),
            P(None, ("gx", "gy", "gz")),
            P(("gx", "gy", "gz")),
            P(("gx", "gy", "gz")),
            P(None, ("gx", "gy", "gz"), None),
            P(None, ("gx", "gy", "gz"), None),
            P(None, ("gx", "gy", "gz"), None),
        ),
        out_specs=(
            P(None, ("gx", "gy", "gz")),
            P(None, ("gx", "gy", "gz")),
            P(None, ("gx", "gy", "gz")),
        ),
        check_vma=False,
    )
```

profile of v0, /device:TPU:1, one launch (start us, length us, event | category | flops | bytes accessed | tf_op | source)
XLA Modules:
  0.0 231.4 jit_solution(15080376783734467444)
XLA Ops:
  3.6 1.4 scatter_custom_fusion
  5.8 11.5 %all-to-all-start = ((s32[128,1,4]{2,1,0:T(1,128)}), s32[128,1,4]{2,1,0:T(1,128)S(1)}, u32[]{:S(2)}, u32[]{:S(2)}) async-start(s32[128,1,4]{2,1,0:T(1,128)} %bitcast.29), calls=%async_computation | async-start | bytes 131072 | tf_op jit(solution)/shard_map/all_to_all | solution.py:83
  18.9 1.4 scatter_custom_fusion.2
  21.0 5.7 %all-to-all-done = s32[128,1,4]{2,1,0:T(1,128)S(1)} async-done(((s32[128,1,4]{2,1,0:T(1,128)}), s32[128,1,4]{2,1,0:T(1,128)S(1)}, u32[]{:S(2)}, u32[]{:S(2)}) %all-to-all-start) | async-done | bytes 2080 | tf_op jit(solution)/shard_map/all_to_all | solution.py:83
  26.7 4.6 %all-to-all-start.3 = ((s32[128,1,4]{2,1,0:T(1,128)}), s32[128,1,4]{2,1,0:T(1,128)S(1)}, u32[]{:S(2)}, u32[]{:S(2)}) async-start(s32[128,1,4]{2,1,0:T(1,128)} %bitcast.57), calls=%async_computation.3 | async-start | bytes 131072 | tf_op jit(solution)/shard_map/all_to_all | solution.py:83
  31.4 9.3 %all-to-all-done.3 = s32[128,1,4]{2,1,0:T(1,128)S(1)} async-done(((s32[128,1,4]{2,1,0:T(1,128)}), s32[128,1,4]{2,1,0:T(1,128)S(1)}, u32[]{:S(2)}, u32[]{:S(2)}) %all-to-all-start.3) | async-done | bytes 2080 | tf_op jit(solution)/shard_map/all_to_all | solution.py:83
  41.3 1.3 fusion.54
  43.1 2.1 gather_fusion
  45.2 2.2 broadcast_select_fusion.1
  47.3 4.6 %all-to-all-start.1 = ((f32[128,4,4,128]{3,2,1,0:T(4,128)}), f32[128,4,4,128]{3,2,1,0:T(4,128)S(1)}, u32[]{:S(2)}, u32[]{:S(2)}) async-start(f32[128,4,4,128]{3,2,1,0:T(4,128)} %broadcast_select_fusion.1), calls=%async_computation.1 | async-start | bytes 2097152 | tf_op jit(solution)/shard_map/all_to_all | solution.py:38
  53.3 17.9 %all-to-all-done.1 = f32[128,4,4,128]{3,2,1,0:T(4,128)S(1)} async-done(((f32[128,4,4,128]{3,2,1,0:T(4,128)}), f32[128,4,4,128]{3,2,1,0:T(4,128)S(1)}, u32[]{:S(2)}, u32[]{:S(2)}) %all-to-all-start.1) | async-done | bytes 1048608 | tf_op jit(solution)/shard_map/all_to_all | solution.py:38
  71.3 1.0 gather_fusion.1
  72.8 30.2 %while.48 = (s32[]{:T(128)}, f32[4,32,3,128]{3,2,1,0:T(4,128)S(1)}, f32[4,32,3,128]{3,2,1,0:T(4,128)S(1)}, f32[4,32,4,128]{3,1,0,2:T(8,128)S(1)}, f32[4,32,4,128]{3,1,0,2:T(8,128)S(1)}, /*index=5*/s32[]{:T(128)}) while((s32[]{:T(128)}, f32[4,32,3,128]{3,2,1,0:T(4,128)S(1)}, f32[4,32,3,128]{3,2,1,0:T(4,128)S(1)}, ...), condition=%wide.region_8.9_spmd, body=%wide.region_4.0_spmd.sunk | while | flops 16764930 | bytes 13893713 | solution.py:31
  73.0 2.1 fusion.69
  75.1 1.3 broadcast_multiply_fusion.14
  76.4 3.9 %fusion.70 = (f32[32,3,128]{2,1,0:T(4,128)S(1)}, f32[32,3,128]{2,1,0:T(4,128)S(1)}) fusion(f32[32,128,128]{2,1,0:T(8,128)S(1)} %get-tuple-element.416, f32[32,3,128]{2,1,0:T(4,128)S(1)} %copy.220, f32[32,3,128]{2,1,0:T(4,128)S(1)} %copy.221, f32[32,128,128]{2,1,0:T(8,128)S(1)} %get-tuple-element.417), kind=kLoop, calls=%fused_computation.17.clone.1 | loop fusion | flops 7839744 | bytes 4390912 | tf_op jit(solution)/shard_map/while/body/eval_jaxpr/reduce_sum | solution.py:21
  80.5 2.1 fusion.69
  82.6 1.3 broadcast_multiply_fusion.14
  84.0 3.9 %fusion.70 = (f32[32,3,128]{2,1,0:T(4,128)S(1)}, f32[32,3,128]{2,1,0:T(4,128)S(1)}) fusion(f32[32,128,128]{2,1,0:T(8,128)S(1)} %get-tuple-element.416, f32[32,3,128]{2,1,0:T(4,128)S(1)} %copy.220, f32[32,3,128]{2,1,0:T(4,128)S(1)} %copy.221, f32[32,128,128]{2,1,0:T(8,128)S(1)} %get-tuple-element.417), kind=kLoop, calls=%fused_computation.17.clone.1 | loop fusion | flops 7839744 | bytes 4390912 | tf_op jit(solution)/shard_map/while/body/eval_jaxpr/reduce_sum | solution.py:21
  88.1 2.1 fusion.69
  90.2 1.3 broadcast_multiply_fusion.14
  91.5 3.9 %fusion.70 = (f32[32,3,128]{2,1,0:T(4,128)S(1)}, f32[32,3,128]{2,1,0:T(4,128)S(1)}) fusion(f32[32,128,128]{2,1,0:T(8,128)S(1)} %get-tuple-element.416, f32[32,3,128]{2,1,0:T(4,128)S(1)} %copy.220, f32[32,3,128]{2,1,0:T(4,128)S(1)} %copy.221, f32[32,128,128]{2,1,0:T(8,128)S(1)} %get-tuple-element.417), kind=kLoop, calls=%fused_computation.17.clone.1 | loop fusion | flops 7839744 | bytes 4390912 | tf_op jit(solution)/shard_map/while/body/eval_jaxpr/reduce_sum | solution.py:21
  95.7 2.1 fusion.69
  97.8 1.3 broadcast_multiply_fusion.14
  99.1 3.9 %fusion.70 = (f32[32,3,128]{2,1,0:T(4,128)S(1)}, f32[32,3,128]{2,1,0:T(4,128)S(1)}) fusion(f32[32,128,128]{2,1,0:T(8,128)S(1)} %get-tuple-element.416, f32[32,3,128]{2,1,0:T(4,128)S(1)} %copy.220, f32[32,3,128]{2,1,0:T(4,128)S(1)} %copy.221, f32[32,128,128]{2,1,0:T(8,128)S(1)} %get-tuple-element.417), kind=kLoop, calls=%fused_computation.17.clone.1 | loop fusion | flops 7839744 | bytes 4390912 | tf_op jit(solution)/shard_map/while/body/eval_jaxpr/reduce_sum | solution.py:21
  104.3 7.0 %scatter_fusion = f32[512,3,128]{2,1,0:T(4,128)S(1)} fusion(f32[512,3,128]{2,1,0:T(4,128)S(1)} %broadcast.376.clone, s32[256]{0:T(256)S(1)} %bitcast.264, f32[256,3,128]{2,1,0:T(4,128)S(1)} %copy.146), kind=kCustom, calls=%fused_computation.9 | custom fusion | bytes 1180672 | tf_op jit(solution)/shard_map/scatter | solution.py:94
  111.3 1.1 copy.147
  112.3 4.3 %all-to-all-start.2 = ((f32[128,4,3,128]{3,1,2,0:T(4,128)}), f32[128,4,3,128]{3,1,2,0:T(4,128)S(1)}, u32[]{:S(2)}, u32[]{:S(2)}) async-start(f32[128,4,3,128]{3,1,2,0:T(4,128)} %copy.147), calls=%async_computation.2 | async-start | bytes 1572864 | tf_op jit(solution)/shard_map/all_to_all | solution.py:43
  116.7 15.2 %while.49 = (s32[]{:T(128)}, f32[2,32,3,128]{3,2,1,0:T(4,128)S(1)}, f32[2,32,3,128]{3,2,1,0:T(4,128)S(1)}, f32[2,32,4,128]{3,2,1,0:T(4,128)S(1)}, f32[2,32,4,128]{3,2,1,0:T(4,128)S(1)}, /*index=5*/s32[]{:T(128)}) while((s32[]{:T(128)}, f32[2,32,3,128]{3,2,1,0:T(4,128)S(1)}, f32[2,32,3,128]{3,2,1,0:T(4,128)S(1)}, ...), condition=%wide.region_14.15_spmd, body=%wide.region_10.14_spmd.sunk | while | flops 16764930 | bytes 14155857 | solution.py:31
  116.9 2.1 fusion.71
  119.0 1.3 broadcast_multiply_fusion.15
  120.4 3.9 %fusion.72 = (f32[32,3,128]{2,1,0:T(4,128)S(1)}, f32[32,3,128]{2,1,0:T(4,128)S(1)}) fusion(f32[32,128,128]{2,1,0:T(8,128)S(1)} %get-tuple-element.427, f32[32,3,128]{2,1,0:T(4,128)S(1)} %copy.224, f32[32,3,128]{2,1,0:T(4,128)S(1)} %copy.225, f32[32,128,128]{2,1,0:T(8,128)S(1)} %get-tuple-element.428), kind=kLoop, calls=%fused_computation.33.clone.1 | loop fusion | flops 7839744 | bytes 4390912 | tf_op jit(solution)/shard_map/while/body/eval_jaxpr/reduce_sum | solution.py:21
  124.5 2.1 fusion.71
  126.6 1.3 broadcast_multiply_fusion.15
  128.0 3.9 %fusion.72 = (f32[32,3,128]{2,1,0:T(4,128)S(1)}, f32[32,3,128]{2,1,0:T(4,128)S(1)}) fusion(f32[32,128,128]{2,1,0:T(8,128)S(1)} %get-tuple-element.427, f32[32,3,128]{2,1,0:T(4,128)S(1)} %copy.224, f32[32,3,128]{2,1,0:T(4,128)S(1)} %copy.225, f32[32,128,128]{2,1,0:T(8,128)S(1)} %get-tuple-element.428), kind=kLoop, calls=%fused_computation.33.clone.1 | loop fusion | flops 7839744 | bytes 4390912 | tf_op jit(solution)/shard_map/while/body/eval_jaxpr/reduce_sum | solution.py:21
  134.6 2.1 gather_fusion.4
  136.7 2.2 broadcast_select_fusion
  138.9 9.2 %all-to-all-start.4 = ((f32[128,4,4,128]{3,2,1,0:T(4,128)}), f32[128,4,4,128]{3,2,1,0:T(4,128)S(1)}, u32[]{:S(2)}, u32[]{:S(2)}) async-start(f32[128,4,4,128]{3,2,1,0:T(4,128)} %broadcast_select_fusion), calls=%async_computation.4 | async-start | bytes 2097152 | tf_op jit(solution)/shard_map/all_to_all | solution.py:38
  149.6 17.8 %all-to-all-done.4 = f32[128,4,4,128]{3,2,1,0:T(4,128)S(1)} async-done(((f32[128,4,4,128]{3,2,1,0:T(4,128)}), f32[128,4,4,128]{3,2,1,0:T(4,128)S(1)}, u32[]{:S(2)}, u32[]{:S(2)}) %all-to-all-start.4) | async-done | bytes 1048608 | tf_op jit(solution)/shard_map/all_to_all | solution.py:38
  167.4 1.0 gather_fusion.5
  169.0 30.2 %while.50 = (s32[]{:T(128)}, f32[4,32,3,128]{3,2,1,0:T(4,128)S(1)}, f32[4,32,3,128]{3,2,1,0:T(4,128)S(1)}, f32[4,32,4,128]{3,1,0,2:T(8,128)S(1)}, f32[4,32,4,128]{3,1,0,2:T(8,128)S(1)}, /*index=5*/s32[]{:T(128)}) while((s32[]{:T(128)}, f32[4,32,3,128]{3,2,1,0:T(4,128)S(1)}, f32[4,32,3,128]{3,2,1,0:T(4,128)S(1)}, ...), condition=%wide.region_23.24_spmd, body=%wide.region_19.23_spmd.sunk | while | flops 16764930 | bytes 13893713 | solution.py:31
  169.1 2.1 fusion.73
  171.2 1.3 broadcast_multiply_fusion.16
  172.6 3.9 %fusion.74 = (f32[32,3,128]{2,1,0:T(4,128)S(1)}, f32[32,3,128]{2,1,0:T(4,128)S(1)}) fusion(f32[32,128,128]{2,1,0:T(8,128)S(1)} %get-tuple-element.438, f32[32,3,128]{2,1,0:T(4,128)S(1)} %copy.226, f32[32,3,128]{2,1,0:T(4,128)S(1)} %copy.227, f32[32,128,128]{2,1,0:T(8,128)S(1)} %get-tuple-element.439), kind=kLoop, calls=%fused_computation.51.clone.1 | loop fusion | flops 7839744 | bytes 4390912 | tf_op jit(solution)/shard_map/while/body/eval_jaxpr/reduce_sum | solution.py:21
  176.7 2.1 fusion.73
  178.8 1.3 broadcast_multiply_fusion.16
  180.1 3.9 %fusion.74 = (f32[32,3,128]{2,1,0:T(4,128)S(1)}, f32[32,3,128]{2,1,0:T(4,128)S(1)}) fusion(f32[32,128,128]{2,1,0:T(8,128)S(1)} %get-tuple-element.438, f32[32,3,128]{2,1,0:T(4,128)S(1)} %copy.226, f32[32,3,128]{2,1,0:T(4,128)S(1)} %copy.227, f32[32,128,128]{2,1,0:T(8,128)S(1)} %get-tuple-element.439), kind=kLoop, calls=%fused_computation.51.clone.1 | loop fusion | flops 7839744 | bytes 4390912 | tf_op jit(solution)/shard_map/while/body/eval_jaxpr/reduce_sum | solution.py:21
  184.3 2.1 fusion.73
  186.3 1.3 broadcast_multiply_fusion.16
  187.7 3.9 %fusion.74 = (f32[32,3,128]{2,1,0:T(4,128)S(1)}, f32[32,3,128]{2,1,0:T(4,128)S(1)}) fusion(f32[32,128,128]{2,1,0:T(8,128)S(1)} %get-tuple-element.438, f32[32,3,128]{2,1,0:T(4,128)S(1)} %copy.226, f32[32,3,128]{2,1,0:T(4,128)S(1)} %copy.227, f32[32,128,128]{2,1,0:T(8,128)S(1)} %get-tuple-element.439), kind=kLoop, calls=%fused_computation.51.clone.1 | loop fusion | flops 7839744 | bytes 4390912 | tf_op jit(solution)/shard_map/while/body/eval_jaxpr/reduce_sum | solution.py:21
  191.8 2.1 fusion.73
  193.9 1.3 broadcast_multiply_fusion.16
  195.2 3.9 %fusion.74 = (f32[32,3,128]{2,1,0:T(4,128)S(1)}, f32[32,3,128]{2,1,0:T(4,128)S(1)}) fusion(f32[32,128,128]{2,1,0:T(8,128)S(1)} %get-tuple-element.438, f32[32,3,128]{2,1,0:T(4,128)S(1)} %copy.226, f32[32,3,128]{2,1,0:T(4,128)S(1)} %copy.227, f32[32,128,128]{2,1,0:T(8,128)S(1)} %get-tuple-element.439), kind=kLoop, calls=%fused_computation.51.clone.1 | loop fusion | flops 7839744 | bytes 4390912 | tf_op jit(solution)/shard_map/while/body/eval_jaxpr/reduce_sum | solution.py:21
  200.4 7.0 %scatter_fusion.1 = f32[512,3,128]{2,1,0:T(4,128)S(1)} fusion(f32[512,3,128]{2,1,0:T(4,128)S(1)} %broadcast.376, s32[256]{0:T(256)S(1)} %bitcast.261, f32[256,3,128]{2,1,0:T(4,128)S(1)} %copy.165), kind=kCustom, calls=%fused_computation.11 | custom fusion | bytes 1180672 | tf_op jit(solution)/shard_map/scatter | solution.py:94
  207.4 1.1 copy.166
  208.5 4.3 %all-to-all-start.5 = ((f32[128,4,3,128]{3,1,2,0:T(4,128)}), f32[128,4,3,128]{3,1,2,0:T(4,128)S(1)}, u32[]{:S(2)}, u32[]{:S(2)}) async-start(f32[128,4,3,128]{3,1,2,0:T(4,128)} %copy.166), calls=%async_computation.5 | async-start | bytes 1572864 | tf_op jit(solution)/shard_map/all_to_all | solution.py:43
  212.9 15.2 %while.51 = (s32[]{:T(128)}, f32[2,32,3,128]{3,2,1,0:T(4,128)S(1)}, f32[2,32,3,128]{3,2,1,0:T(4,128)S(1)}, f32[2,32,4,128]{3,2,1,0:T(4,128)S(1)}, f32[2,32,4,128]{3,2,1,0:T(4,128)S(1)}, /*index=5*/s32[]{:T(128)}) while((s32[]{:T(128)}, f32[2,32,3,128]{3,2,1,0:T(4,128)S(1)}, f32[2,32,3,128]{3,2,1,0:T(4,128)S(1)}, ...), condition=%wide.region_29.30_spmd, body=%wide.region_25.29_spmd.sunk | while | flops 16764930 | bytes 14155857 | solution.py:31
  213.1 2.1 fusion.75
  215.2 1.3 broadcast_multiply_fusion.17
  216.5 3.9 %fusion.76 = (f32[32,3,128]{2,1,0:T(4,128)S(1)}, f32[32,3,128]{2,1,0:T(4,128)S(1)}) fusion(f32[32,128,128]{2,1,0:T(8,128)S(1)} %get-tuple-element.449, f32[32,3,128]{2,1,0:T(4,128)S(1)} %copy.230, f32[32,3,128]{2,1,0:T(4,128)S(1)} %copy.231, f32[32,128,128]{2,1,0:T(8,128)S(1)} %get-tuple-element.450), kind=kLoop, calls=%fused_computation.67.clone.1 | loop fusion | flops 7839744 | bytes 4390912 | tf_op jit(solution)/shard_map/while/body/eval_jaxpr/reduce_sum | solution.py:21
  220.7 2.1 fusion.75
  222.8 1.3 broadcast_multiply_fusion.17
  224.1 3.9 %fusion.76 = (f32[32,3,128]{2,1,0:T(4,128)S(1)}, f32[32,3,128]{2,1,0:T(4,128)S(1)}) fusion(f32[32,128,128]{2,1,0:T(8,128)S(1)} %get-tuple-element.449, f32[32,3,128]{2,1,0:T(4,128)S(1)} %copy.230, f32[32,3,128]{2,1,0:T(4,128)S(1)} %copy.231, f32[32,128,128]{2,1,0:T(8,128)S(1)} %get-tuple-element.450), kind=kLoop, calls=%fused_computation.67.clone.1 | loop fusion | flops 7839744 | bytes 4390912 | tf_op jit(solution)/shard_map/while/body/eval_jaxpr/reduce_sum | solution.py:21
  228.1 1.4 all-to-all-done.5
  (231 shorter events, 19.9 us)
Async XLA Ops:
  0.6 30.7 %copy-start.2 = (f32[8192]{0:T(1024)S(1)}, f32[8192]{0:T(1024)}, u32[]{:S(2)}) copy-start(f32[8192]{0:T(1024)} %param.17) | copy-start | bytes 98308
  0.6 30.7 %copy-start = (f32[3,8192]{1,0:T(4,128)S(1)}, f32[3,8192]{1,0:T(4,128)}, u32[]{:S(2)}) copy-start(f32[3,8192]{1,0:T(4,128)} %param.15) | copy-start | bytes 294916
  5.8 20.9 %all-to-all-start = ((s32[128,1,4]{2,1,0:T(1,128)}), s32[128,1,4]{2,1,0:T(1,128)S(1)}, u32[]{:S(2)}, u32[]{:S(2)}) async-start(s32[128,1,4]{2,1,0:T(1,128)} %bitcast.29), calls=%async_computation | async-start | bytes 131072 | tf_op jit(solution)/shard_map/all_to_all | solution.py:83
  26.7 14.0 %all-to-all-start.3 = ((s32[128,1,4]{2,1,0:T(1,128)}), s32[128,1,4]{2,1,0:T(1,128)S(1)}, u32[]{:S(2)}, u32[]{:S(2)}) async-start(s32[128,1,4]{2,1,0:T(1,128)} %bitcast.57), calls=%async_computation.3 | async-start | bytes 131072 | tf_op jit(solution)/shard_map/all_to_all | solution.py:83
  45.1 6.8 %copy-start.5 = (s32[2,64,2]{1,2,0:T(2,128)S(1)}, s32[2,64,2]{1,2,0:T(2,128)}, u32[]{:S(2)}) copy-start(s32[2,64,2]{1,2,0:T(2,128)} %param.21) | copy-start | bytes 3076
  47.3 24.0 %all-to-all-start.1 = ((f32[128,4,4,128]{3,2,1,0:T(4,128)}), f32[128,4,4,128]{3,2,1,0:T(4,128)S(1)}, u32[]{:S(2)}, u32[]{:S(2)}) async-start(f32[128,4,4,128]{3,2,1,0:T(4,128)} %broadcast_select_fusion.1), calls=%async_computation.1 | async-start | bytes 2097152 | tf_op jit(solution)/shard_map/all_to_all | solution.py:38
  112.3 21.0 %all-to-all-start.2 = ((f32[128,4,3,128]{3,1,2,0:T(4,128)}), f32[128,4,3,128]{3,1,2,0:T(4,128)S(1)}, u32[]{:S(2)}, u32[]{:S(2)}) async-start(f32[128,4,3,128]{3,1,2,0:T(4,128)} %copy.147), calls=%async_computation.2 | async-start | bytes 1572864 | tf_op jit(solution)/shard_map/all_to_all | solution.py:43
  116.7 15.3 %copy-start.4 = (s32[8192]{0:T(1024)S(1)}, s32[8192]{0:T(1024)}, u32[]{:S(2)}) copy-start(s32[8192]{0:T(1024)} %param.18) | copy-start | bytes 98308
  131.9 2.5 %copy-start.3 = (f32[3,8192]{1,0:T(4,128)S(1)}, f32[3,8192]{1,0:T(4,128)}, u32[]{:S(2)}) copy-start(f32[3,8192]{1,0:T(4,128)} %param.16) | copy-start | bytes 294916
  138.9 28.5 %all-to-all-start.4 = ((f32[128,4,4,128]{3,2,1,0:T(4,128)}), f32[128,4,4,128]{3,2,1,0:T(4,128)S(1)}, u32[]{:S(2)}, u32[]{:S(2)}) async-start(f32[128,4,4,128]{3,2,1,0:T(4,128)} %broadcast_select_fusion), calls=%async_computation.4 | async-start | bytes 2097152 | tf_op jit(solution)/shard_map/all_to_all | solution.py:38
  208.5 21.0 %all-to-all-start.5 = ((f32[128,4,3,128]{3,1,2,0:T(4,128)}), f32[128,4,3,128]{3,1,2,0:T(4,128)S(1)}, u32[]{:S(2)}, u32[]{:S(2)}) async-start(f32[128,4,3,128]{3,1,2,0:T(4,128)} %copy.166), calls=%async_computation.5 | async-start | bytes 1572864 | tf_op jit(solution)/shard_map/all_to_all | solution.py:43
  230.6 0.8 copy-start.1
where the time goes:
time: 232 us; the launch traced here: 231 us
  other arithmetic  97.6 us (42%)
  waiting for transfers between devices  52.8 us (23%)
  starting transfers between devices  38.6 us (17%)
  local copies, waits for them, and re-layouts  38.2 us (16%)
    reduce_sum x12, other arithmetic, pair_forces(): jnp.sum(offset * (kernel * left_leaf[:, 3, :, None])[:, None], axis=2)  46.7 us
    all_to_all x2, waiting for transfers between devices, deliver_leaves(): lax.all_to_all(looked, ('gx', 'gy', 'gz'), split_axis=0, concat_axis=0, t...  35.7 us
    reduce_sum x12, other arithmetic, pair_forces(): dist_sq = jnp.sum(offset * offset, axis=1)  24.7 us
    all_to_all x2, starting transfers between devices, shards(): lax.all_to_all(wanted, ('gx', 'gy', 'gz'), split_axis=0, concat_axis=0, t...  16.1 us
    mul x12, other arithmetic, pair_forces(): kernel * right_leaf[:, 3, None, :]  16 us
    all_to_all x2, waiting for transfers between devices, shards(): lax.all_to_all(wanted, ('gx', 'gy', 'gz'), split_axis=0, concat_axis=0, t...  15 us
    scatter x2, local copies, waits for them, and re-layouts, shards(): jnp.zeros((devices * capacity, 3, width), jnp.float32).at[placed]  13.9 us
    all_to_all x2, starting transfers between devices, deliver_leaves(): lax.all_to_all(looked, ('gx', 'gy', 'gz'), split_axis=0, concat_axis=0, t...  13.8 us
  transfers between devices with their start and end apart: 6, of which 6 were waited for; matrix products, arithmetic and copies ran while one was open for 16% of the time, Pallas kernels for 0%

commit v1 on v0

v1 whole, which is shorter than its diff:
```python
import jax
import jax.numpy as jnp
from jax import lax
from jax.experimental import pallas as pl
from jax.experimental.pallas import tpu as pltpu
from jax.sharding import PartitionSpec as P

LEAF = 128
NLEAF = 64
DEVICES = 128
CAP = 4
PAIRS = 128
LOCAL = 64
SLOTS = DEVICES * CAP
AXES = ("gx", "gy", "gz")

SOFTENING = 0.01
CUTOFF_SQ = 0.04
TIME_STEP = 0.05
CENTRE = 0.5

F32 = jnp.float32
BF16 = jnp.bfloat16
NT = (((1,), (1,)), ((), ()))
NN = (((1,), (0,)), ((), ()))
TN = (((0,), (0,)), ((), ()))
VMEM = pl.BlockSpec(memory_space=pltpu.VMEM)


def split3(value):
    high = value.astype(BF16).astype(F32)
    rest = value - high
    middle = rest.astype(BF16).astype(F32)
    return high, middle, rest - middle


def leaf_parts(tile, row):
    xyz = jnp.where(row < 3, tile - CENTRE, 0.0)
    high, middle, low = split3(xyz)
    norm = split3(jnp.sum(xyz * xyz, axis=0, keepdims=True))
    mass = tile[3:4] * (1.0 / CUTOFF_SQ**2)
    moment = jnp.where(row < 3, xyz * mass, jnp.where(row == 3, mass, 0.0))
    mh, mm, ml = split3(moment)
    weights = jnp.concatenate([mh + pltpu.roll(mm, 4, 0), ml], axis=0).astype(BF16)
    return xyz, (high, middle, low), norm, weights


def squared_distances(left, right, row):
    _, (ah, am, al), (an0, an1, an2), _ = left
    _, (bh, bm, bl), (bn0, bn1, bn2), _ = right
    a_norm = jnp.where(
        row == 0, an0, jnp.where(row == 1, an1, jnp.where(row == 2, an2, jnp.where(row < 6, 1.0, 0.0)))
    )
    b_norm = jnp.where(
        row < 3, 1.0, jnp.where(row == 3, bn0, jnp.where(row == 4, bn1, jnp.where(row == 5, bn2, 0.0)))
    )
    bh, bm, bl = -2.0 * bh, -2.0 * bm, -2.0 * bl
    zero = jnp.zeros_like(a_norm)
    lhs = jnp.concatenate([ah, ah, am, ah, al, am, a_norm, zero], axis=0).astype(BF16)
    rhs = jnp.concatenate([bh, bm, bh, bl, bh, bm, b_norm, zero], axis=0).astype(BF16)
    return lax.dot_general(lhs, rhs, TN, preferred_element_type=F32)


def pair_kernel(dist_sq):
    taper = jnp.maximum(CUTOFF_SQ - dist_sq, 0.0)
    root = lax.rsqrt(dist_sq + SOFTENING)
    scaled = taper * root
    kernel = scaled * scaled * root
    high = kernel.astype(BF16)
    return high, (kernel - high.astype(F32)).astype(BF16)


def moments(left, right, kernel):
    high, low = kernel
    rows = jnp.concatenate([high, low], axis=0)
    columns = jnp.concatenate([high, low], axis=1)
    on_left = lax.dot_general(right[3], rows, NT, preferred_element_type=F32)
    on_right = lax.dot_general(left[3], columns, NN, preferred_element_type=F32)
    return (on_left[:, :LEAF] + on_left[:, LEAF:], on_right[:, :LEAF] + on_right[:, LEAF:])


def force_tile(moment, xyz):
    total = moment[0:8] + moment[8:16]
    total = total + pltpu.roll(total, 4, 0)
    return total - (xyz + pltpu.roll(xyz, 4, 0)) * total[3:4]


def pair_forces(tiles, row):
    parts = [(leaf_parts(a, row), leaf_parts(b, row)) for a, b in tiles]
    dists = [squared_distances(a, b, row) for a, b in parts]
    kernels = [pair_kernel(q) for q in dists]
    sums = [moments(a, b, k) for (a, b), k in zip(parts, kernels)]
    return [
        (force_tile(fa, a[0]), force_tile(fb, b[0])) for (a, b), (fa, fb) in zip(parts, sums)
    ]


def row_iota():
    return lax.broadcasted_iota(jnp.int32, (8, LEAF), 0)


def fill_slots(asked, state, looked):
    row = row_iota()

    def body(step, carry):
        for u in range(16):
            tile = step * 16 + u
            looked[pl.ds(pl.multiple_of(tile * 8, 8), 8), :] = jnp.where(
                row < 4, state[asked[2 * tile]], state[asked[2 * tile + 1]]
            )
        return carry

    lax.fori_loop(0, SLOTS // 32, body, 0)


def pack_kernel(positions, velocities, masses, state, moving):
    for leaf in range(NLEAF):
        lanes = slice(leaf * LEAF, (leaf + 1) * LEAF)
        state[leaf, 0:3, :] = positions[:, lanes]
        state[leaf, 4:7, :] = positions[:, lanes]
        state[leaf, 3:4, :] = masses[leaf : leaf + 1, :]
        state[leaf, 7:8, :] = masses[leaf : leaf + 1, :]
        moving[leaf, 0:3, :] = velocities[:, lanes]
        moving[leaf, 4:7, :] = velocities[:, lanes]
        moving[leaf, 3:4, :] = jnp.zeros((1, LEAF), F32)
        moving[leaf, 7:8, :] = jnp.zeros((1, LEAF), F32)
    state[NLEAF] = jnp.zeros((8, LEAF), F32)


def gather_kernel(asked, state, looked):
    fill_slots(asked, state, looked)


def local_kernel(pairs, state, forces):
    row = row_iota()
    forces[...] = jnp.zeros_like(forces)
    unroll = 16

    def body(step, carry):
        ids = [
            (pairs[2 * (step * unroll + u)], pairs[2 * (step * unroll + u) + 1])
            for u in range(unroll)
        ]
        found = pair_forces([(state[a], state[b]) for a, b in ids], row)
        for (a, b), (fa, fb) in zip(ids, found):
            forces[a] += fa
            forces[b] += fb
        return carry

    lax.fori_loop(0, LOCAL // unroll, body, 0)


def remote_kernel(placed, arrived, pushed):
    row = row_iota()
    pushed[...] = jnp.zeros_like(pushed)
    unroll = 16

    def leaf(slot):
        tile = arrived[pl.ds(pl.multiple_of((slot >> 1) * 8, 8), 8), :]
        return jnp.where((slot & 1) == 1, pltpu.roll(tile, 4, 0), tile)

    def body(step, carry):
        ids = [
            (placed[2 * (step * unroll + u)], placed[2 * (step * unroll + u) + 1])
            for u in range(unroll)
        ]
        found = pair_forces([(leaf(a), leaf(b)) for a, b in ids], row)
        for (a, b), (fa, fb) in zip(ids, found):
            pushed[pl.ds(3 * a, 3), :] = fa[0:3]
            pushed[pl.ds(3 * b, 3), :] = fb[0:3]
        return carry

    lax.fori_loop(0, PAIRS // unroll, body, 0)


def summed_tiles(codes, returned):
    target = lax.broadcasted_iota(jnp.int32, (4 * NLEAF, 3 * SLOTS), 0)
    chosen = jnp.where(target == codes[...], 1.0, 0.0).astype(BF16)
    total = jnp.zeros((4 * NLEAF, LEAF), F32)
    for part in split3(returned[...]):
        total = total + lax.dot_general(chosen, part.astype(BF16), NN, preferred_element_type=F32)
    return total


def kick_drift(threshold, codes, returned, local, state, moving, bins, leaf_done):
    row = row_iota()
    total = summed_tiles(codes, returned)
    for leaf in range(NLEAF):
        pair = total[leaf // 2 * 8 : leaf // 2 * 8 + 8]
        other = pltpu.roll(pair, 4, 0)
        mine = jnp.where(row < 4, pair, other) if leaf % 2 == 0 else jnp.where(row < 4, other, pair)
        accel = jnp.where((row & 3) < 3, mine + local[leaf], 0.0)
        active = bins[leaf : leaf + 1, :] >= threshold
        velocity = moving[leaf] + jnp.where(active, TIME_STEP * accel, 0.0)
        position = state[leaf] + TIME_STEP * velocity
        leaf_done(leaf, position, velocity, accel)


def advance_kernel(asked, codes, returned, local, state, moving, bins, looked, new_state, new_moving):
    def leaf_done(leaf, position, velocity, accel):
        new_state[leaf] = position
        new_moving[leaf] = velocity

    kick_drift(3, codes, returned, local, state, moving, bins, leaf_done)
    new_state[NLEAF] = jnp.zeros((8, LEAF), F32)
    fill_slots(asked, new_state, looked)


def finish_kernel(codes, returned, local, state, moving, bins, positions, velocities, accels):
    def leaf_done(leaf, position, velocity, accel):
        lanes = slice(leaf * LEAF, (leaf + 1) * LEAF)
        positions[:, lanes] = position[0:3]
        velocities[:, lanes] = velocity[0:3]
        accels[:, lanes] = accel[0:3]

    kick_drift(2, codes, returned, local, state, moving, bins, leaf_done)


def call(kernel, out_shapes, scalars, arrays, flops, size):
    return pl.pallas_call(
        kernel,
        out_shape=out_shapes,
        grid_spec=pltpu.PrefetchScalarGridSpec(
            num_scalar_prefetch=len(scalars),
            grid=(),
            in_specs=[VMEM] * len(arrays),
            out_specs=jax.tree.map(lambda _: VMEM, out_shapes),
        ),
        compiler_params=pltpu.CompilerParams(vmem_limit_bytes=40 * 2**20),
        cost_estimate=pl.CostEstimate(flops=flops, bytes_accessed=size, transcendentals=0),
    )(*scalars, *arrays)


def shape(*dims):
    return jax.ShapeDtypeStruct(dims, F32)


def exchange(array):
    return lax.all_to_all(array, AXES, split_axis=0, concat_axis=0, tiled=True)


def send_leaves(looked):
    return exchange(looked.reshape(DEVICES, 4 * CAP, LEAF)).reshape(4 * SLOTS, LEAF)


def send_forces(pushed):
    return exchange(pushed.reshape(DEVICES, 3, CAP, LEAF)).reshape(3 * SLOTS, LEAF)


def requests(pair_owner, pair_slot):
    owners = pair_owner.reshape(2, 2 * PAIRS)
    slots = pair_slot.reshape(2, 2 * PAIRS)
    earlier = jnp.arange(2 * PAIRS)[None, :] < jnp.arange(2 * PAIRS)[:, None]
    rank = jnp.sum(
        ((owners[:, :, None] == owners[:, None, :]) & earlier[None]).astype(jnp.int32), axis=2
    )
    placed = owners * CAP + rank
    spots = jnp.arange(SLOTS, dtype=jnp.int32)
    wanted = NLEAF + jnp.sum(
        jnp.where(placed[:, :, None] == spots[None, None, :], (slots - NLEAF)[:, :, None], 0), axis=1
    )
    return placed, wanted.reshape(2, DEVICES, CAP).transpose(1, 0, 2).reshape(DEVICES, 2 * CAP)


def shards(positions, velocities, masses, time_bins, pair_owner, pair_slot, local_pairs):
    masses = masses.reshape(NLEAF, LEAF)
    bins = time_bins.reshape(NLEAF, LEAF)
    placed, wanted = requests(pair_owner, pair_slot)
    asked = exchange(wanted).reshape(DEVICES, 2, CAP).transpose(1, 0, 2).reshape(2, SLOTS)
    codes = (4 * asked[:, :, None] + jnp.arange(3, dtype=jnp.int32)).reshape(2, 1, 3 * SLOTS)
    local_ids = local_pairs.reshape(2, 2 * LOCAL)

    state_shape = shape(NLEAF + 1, 8, LEAF)
    moving_shape = shape(NLEAF, 8, LEAF)
    looked_shape = shape(4 * SLOTS, LEAF)
    pushed_shape = shape(3 * SLOTS, LEAF)

    def local_forces(ids, state):
        return call(local_kernel, moving_shape, [ids], [state], 64 * 2**14 * 25, 2**20)

    def remote_forces(ids, arrived):
        return call(remote_kernel, pushed_shape, [ids], [arrived], 128 * 2**14 * 25, 2**21)

    state, moving = call(
        pack_kernel, (state_shape, moving_shape), [], [positions, velocities, masses], 2**16, 2**20
    )
    local = local_forces(local_ids[0], state)
    looked = call(gather_kernel, looked_shape, [asked[0]], [state], 2**16, 2**21)
    pushed = remote_forces(placed[0], send_leaves(looked))
    returned = send_forces(pushed)
    looked, state, moving = call(
        advance_kernel,
        (looked_shape, state_shape, moving_shape),
        [asked[1]],
        [codes[0], returned, local, state, moving, bins],
        2**16,
        2**22,
    )
    local = local_forces(local_ids[1], state)
    pushed = remote_forces(placed[1], send_leaves(looked))
    returned = send_forces(pushed)
    out = shape(3, NLEAF * LEAF)
    return call(
        finish_kernel,
        (out, out, out),
        [],
        [codes[1], returned, local, state, moving, bins],
        2**16,
        2**22,
    )


def solution(mesh):
    split = P(None, AXES)
    rows = P(None, AXES, None)
    return jax.shard_map(
        shards,
        mesh=mesh,
        in_specs=(split, split, P(AXES), P(AXES), rows, rows, rows),
        out_specs=(split, split, split),
        check_vma=False,
    )
```

time: 232 us -> 139 us (0.60)
  other arithmetic: 97.6 us -> 0.72 us
  local copies, waits for them, and re-layouts: 38.2 us -> 4.42 us
  Pallas kernels: 0 us -> 33 us
  blocking collectives: 0 us -> 23.6 us
  starting transfers between devices: 38.6 us -> 24.9 us
    reduce_sum x26 -> x2, other arithmetic: 71.9 us -> 0.48 us  [the longest x1 0.25 us: requests(): jnp.sum(((owners[:, :, None] == owners[:, None, :]) & earlier[None]).asty...]
    pallas_call x0 -> x8, Pallas kernels: none -> 33 us  [call(): pl.pallas_call(kernel, out_shape=out_shapes, grid_spec=pltpu.PrefetchScal...]
    all_to_all x0 -> x1, blocking collectives: none -> 23.6 us  [exchange(): return lax.all_to_all(array, AXES, split_axis=0, concat_axis=0, tiled=True)]
    scatter x4 -> x0, local copies, waits for them, and re-layouts: 16.7 us -> none  [the longest x2 13.9 us: shards(): jnp.zeros((devices * capacity, 3, width), jnp.float32).at[placed]]
    mul x13 -> x1, other arithmetic: 16 us -> 0.01 us  [shards(): 4 * asked[:, :, None] + jnp.arange(3, dtype=jnp.int32)]
    all_to_all x6 -> x4, starting transfers between devices: 38.6 us -> 24.9 us  [exchange(): return lax.all_to_all(array, AXES, split_axis=0, concat_axis=0, tiled=True)]
    gather x10 -> x0, local copies, waits for them, and re-layouts: 8.84 us -> none  [the longest x2 4.15 us: shards(): leaves[jnp.maximum(asked_for, 0)]]
    select_n x4 -> x0, other arithmetic: 4.33 us -> none  [the longest x2 4.31 us: shards(): jnp.where(filled[:, :, None, None], leaves[jnp.maximum(asked_for, 0)], 0.0)]
  transfers between devices with their start and end apart: 6 -> 4, of which waited for: 6 -> 4; matrix products, arithmetic and copies ran while one was open for 16% -> 1% of each run, Pallas kernels for 0% -> 6%
where the time goes in v1:
time: 139 us
  waiting for transfers between devices  51.4 us (37%)
  Pallas kernels  33 us (24%)
  starting transfers between devices  24.9 us (18%)
  blocking collectives  23.6 us (17%)
  local copies, waits for them, and re-layouts  4.42 us (3%)
    all_to_all x4, waiting for transfers between devices, exchange(): return lax.all_to_all(array, AXES, split_axis=0, concat_axis=0, tiled=True)  51.4 us
    pallas_call x8, Pallas kernels, call(): pl.pallas_call(kernel, out_shape=out_shapes, grid_spec=pltpu.PrefetchScal...  33 us
    all_to_all x4, starting transfers between devices, exchange(): return lax.all_to_all(array, AXES, split_axis=0, concat_axis=0, tiled=True)  24.9 us
    all_to_all x1, blocking collectives, exchange(): return lax.all_to_all(array, AXES, split_axis=0, concat_axis=0, tiled=True)  23.6 us
  transfers between devices with their start and end apart: 4, of which 4 were waited for; matrix products, arithmetic and copies ran while one was open for 1% of the time, Pallas kernels for 6%

profile of v1, /device:TPU:1, one launch (start us, length us, event | category | flops | bytes accessed | tf_op | source)
XLA Modules:
  0.0 138.9 jit_solution(1447589877682606919)
XLA Ops:
  0.6 0.0 copy-start.5
  0.7 0.6 copy-done.5
  1.3 0.1 copy.31
  1.5 0.0 copy-start.4
  1.5 0.1 sub.7
  1.6 0.5 copy-done.4
  2.1 0.1 copy.30
  2.3 0.1 reshape.105
  2.4 0.3 convert_reduce_fusion
  2.7 0.2 select_reduce_fusion
  2.9 0.1 add.39
  3.1 0.0 copy-start.2
  3.1 0.1 copy.32
  3.2 0.0 copy-start.1
  3.2 0.7 copy.33
  3.9 0.0 copy-start.3
  3.9 11.5 %all-to-all-start = ((s32[128,1,8]{2,1,0:T(1,128)}), s32[128,1,8]{2,1,0:T(1,128)S(1)}, u32[]{:S(2)}, u32[]{:S(2)}) async-start(s32[128,1,8]{2,1,0:T(1,128)} %copy.33), calls=%async_computation | async-start | bytes 131072 | tf_op jit(solution)/shard_map/all_to_all | solution.py:239
  15.4 0.0 copy-done.2
  15.4 0.0 copy-done.1
  15.4 0.0 copy-done.3
  15.5 0.1 shard_map.94
  15.6 9.2 %all-to-all-done = s32[128,1,8]{2,1,0:T(1,128)S(1)} async-done(((s32[128,1,8]{2,1,0:T(1,128)}), s32[128,1,8]{2,1,0:T(1,128)S(1)}, u32[]{:S(2)}, u32[]{:S(2)}) %all-to-all-start) | async-done | bytes 4128 | tf_op jit(solution)/shard_map/all_to_all | solution.py:239
  24.9 0.1 copy.37
  25.0 0.1 squeeze.29.asked
  25.1 2.2 %shard_map.95 = f32[2048,128]{1,0:T(8,128)} custom-call(s32[512]{0:T(512)S(1)} %squeeze.29.asked, f32[65,8,128]{2,1,0:T(8,128)S(1)} %get-tuple-element.8.state), custom_call_target="tpu_custom_call" | custom-call | flops 65536 | bytes 2097152 | tf_op jit(solution)/shard_map/pallas_call | solution.py:220
  27.3 4.6 %all-to-all-start.1 = ((f32[128,16,128]{2,1,0:T(8,128)}), f32[128,16,128]{2,1,0:T(8,128)S(1)}, u32[]{:S(2)}, u32[]{:S(2)}) async-start(f32[128,16,128]{2,1,0:T(8,128)} %bitcast.8), calls=%async_computation.1 | async-start | bytes 2097152 | tf_op jit(solution)/shard_map/all_to_all | solution.py:239
  31.9 19.3 %all-to-all-done.1 = f32[128,16,128]{2,1,0:T(8,128)S(1)} async-done(((f32[128,16,128]{2,1,0:T(8,128)}), f32[128,16,128]{2,1,0:T(8,128)S(1)}, u32[]{:S(2)}, u32[]{:S(2)}) %all-to-all-start.1) | async-done | bytes 1048608 | tf_op jit(solution)/shard_map/all_to_all | solution.py:239
  51.3 9.1 %shard_map.96 = f32[1536,128]{1,0:T(8,128)} custom-call(s32[256]{0:T(256)S(1)} %bitcast.26, f32[2048,128]{1,0:T(8,128)S(1)} %bitcast.17), custom_call_target="tpu_custom_call" | custom-call | flops 52428800 | bytes 2097152 | tf_op jit(solution)/shard_map/pallas_call | solution.py:220
  60.4 0.0 copy-start.6
  60.4 4.4 %all-to-all-start.2 = ((f32[128,3,4,128]{3,2,1,0:T(4,128)}), f32[128,3,4,128]{3,2,1,0:T(4,128)S(1)}, u32[]{:S(2)}, u32[]{:S(2)}) async-start(f32[128,3,4,128]{3,2,1,0:T(4,128)} %bitcast.10), calls=%async_computation.2 | async-start | bytes 1572864 | tf_op jit(solution)/shard_map/all_to_all | solution.py:239
  64.8 0.0 copy-done.6
  64.8 0.1 copy.38
  64.9 0.1 squeeze.30.pairs
  65.1 4.4 %shard_map.97.local = f32[64,8,128]{2,1,0:T(8,128)S(1)} custom-call(s32[128]{0:T(128)S(1)} %squeeze.30.pairs, f32[65,8,128]{2,1,0:T(8,128)S(1)} %get-tuple-element.8.state), custom_call_target="tpu_custom_call" | custom-call | flops 26214400 | bytes 1048576 | tf_op jit(solution)/shard_map/pallas_call | solution.py:220
  69.5 0.1 copy.36
  69.6 0.1 squeeze.26.asked
  69.7 0.1 copy.35
  69.8 0.1 mul.28
  70.0 0.2 iota_add_fusion
  70.2 0.0 copy-start
  70.2 0.2 squeeze.27.codes
  70.4 11.1 %all-to-all-done.2 = f32[128,3,4,128]{3,2,1,0:T(4,128)S(1)} async-done(((f32[128,3,4,128]{3,2,1,0:T(4,128)}), f32[128,3,4,128]{3,2,1,0:T(4,128)S(1)}, u32[]{:S(2)}, u32[]{:S(2)}) %all-to-all-start.2) | async-done | bytes 786464 | tf_op jit(solution)/shard_map/all_to_all | solution.py:239
  81.5 0.0 copy-done
  81.5 2.1 %shard_map.98 = (f32[2048,128]{1,0:T(8,128)S(1)}, f32[65,8,128]{2,1,0:T(8,128)S(1)}, f32[64,8,128]{2,1,0:T(8,128)S(1)}) custom-call(s32[512]{0:T(512)S(1)} %squeeze.26.asked, s32[1,1536]{1,0:T(1,128)S(1)} %squeeze.27.codes, f32[1536,128]{1,0:T(8,128)S(1)} %bitcast.19, f32[64,8,128]{2,1,0:T(8,128)S(1)} %shard_map.97.local, ...), custom_call_target="tpu_custom_call" | custom-call | flops 65536 | bytes 4194304 | tf_op jit(solution)/shard_map/pallas_call | solution.py:220
  83.6 23.6 %all_to_all.29 = f32[128,16,128]{2,1,0:T(8,128)S(1)} all-to-all(f32[128,16,128]{2,1,0:T(8,128)S(1)} %bitcast.21), channel_id=1, replica_groups=mesh['gx'=4,'gy'=4,'gz'=8] {'gx','gy','gz'}, dimensions={0} | all-to-all | bytes 2097152 | tf_op jit(solution)/shard_map/all_to_all | solution.py:239
  107.1 9.1 %shard_map.99 = f32[1536,128]{1,0:T(8,128)} custom-call(s32[256]{0:T(256)S(1)} %bitcast.25, f32[2048,128]{1,0:T(8,128)S(1)} %bitcast.18), custom_call_target="tpu_custom_call" | custom-call | flops 52428800 | bytes 2097152 | tf_op jit(solution)/shard_map/pallas_call | solution.py:220
  116.3 4.3 %all-to-all-start.4 = ((f32[128,3,4,128]{3,2,1,0:T(4,128)}), f32[128,3,4,128]{3,2,1,0:T(4,128)S(1)}, u32[]{:S(2)}, u32[]{:S(2)}) async-start(f32[128,3,4,128]{3,2,1,0:T(4,128)} %bitcast.15), calls=%async_computation.4 | async-start | bytes 1572864 | tf_op jit(solution)/shard_map/all_to_all | solution.py:239
  120.6 0.1 copy.39
  120.7 0.1 squeeze.31.pairs
  120.8 0.2 squeeze.24.codes
  121.1 4.4 %shard_map.100.local = f32[64,8,128]{2,1,0:T(8,128)S(1)} custom-call(s32[128]{0:T(128)S(1)} %squeeze.31.pairs, f32[65,8,128]{2,1,0:T(8,128)S(1)} %get-tuple-element.11.state), custom_call_target="tpu_custom_call" | custom-call | flops 26214400 | bytes 1048576 | tf_op jit(solution)/shard_map/pallas_call | solution.py:220
  125.4 11.8 %all-to-all-done.4 = f32[128,3,4,128]{3,2,1,0:T(4,128)S(1)} async-done(((f32[128,3,4,128]{3,2,1,0:T(4,128)}), f32[128,3,4,128]{3,2,1,0:T(4,128)S(1)}, u32[]{:S(2)}, u32[]{:S(2)}) %all-to-all-start.4) | async-done | bytes 786464 | tf_op jit(solution)/shard_map/all_to_all | solution.py:239
  137.2 1.6 %shard_map.101 = (f32[3,8192]{1,0:T(4,128)}, f32[3,8192]{1,0:T(4,128)}, f32[3,8192]{1,0:T(4,128)}) custom-call(s32[1,1536]{1,0:T(1,128)S(1)} %squeeze.24.codes, f32[1536,128]{1,0:T(8,128)S(1)} %bitcast.20, f32[64,8,128]{2,1,0:T(8,128)S(1)} %shard_map.100.local, f32[65,8,128]{2,1,0:T(8,128)S(1)} %get-tuple-element.11.state, ...), custom_call_target="tpu_custom_call" | custom-call | flops 65536 | bytes 4194304 | tf_op jit(solution)/shard_map/pallas_call | solution.py:220
  (10 shorter events, 0.1 us)
Async XLA Ops:
  0.6 0.7 copy-start.5
  1.5 0.7 copy-start.4
  3.1 12.3 %copy-start.2 = (f32[3,8192]{1,0:T(4,128)S(1)}, f32[3,8192]{1,0:T(4,128)}, u32[]{:S(2)}) copy-start(f32[3,8192]{1,0:T(4,128)} %velocities.1) | copy-start | bytes 294916
  3.2 12.3 %copy-start.1 = (f32[3,8192]{1,0:T(4,128)S(1)}, f32[3,8192]{1,0:T(4,128)}, u32[]{:S(2)}) copy-start(f32[3,8192]{1,0:T(4,128)} %positions.1) | copy-start | bytes 294916
  3.9 11.5 %copy-start.3 = (f32[8192]{0:T(1024)S(1)}, f32[8192]{0:T(1024)}, u32[]{:S(2)}) copy-start(f32[8192]{0:T(1024)} %param.9) | copy-start | bytes 98308
  3.9 20.9 %all-to-all-start = ((s32[128,1,8]{2,1,0:T(1,128)}), s32[128,1,8]{2,1,0:T(1,128)S(1)}, u32[]{:S(2)}, u32[]{:S(2)}) async-start(s32[128,1,8]{2,1,0:T(1,128)} %copy.33), calls=%async_computation | async-start | bytes 131072 | tf_op jit(solution)/shard_map/all_to_all | solution.py:239
  27.3 24.0 %all-to-all-start.1 = ((f32[128,16,128]{2,1,0:T(8,128)}), f32[128,16,128]{2,1,0:T(8,128)S(1)}, u32[]{:S(2)}, u32[]{:S(2)}) async-start(f32[128,16,128]{2,1,0:T(8,128)} %bitcast.8), calls=%async_computation.1 | async-start | bytes 2097152 | tf_op jit(solution)/shard_map/all_to_all | solution.py:239
  60.4 4.4 %copy-start.6 = (s32[2,64,2]{1,2,0:T(2,128)S(1)}, s32[2,64,2]{1,2,0:T(2,128)}, u32[]{:S(2)}) copy-start(s32[2,64,2]{1,2,0:T(2,128)} %param.13) | copy-start | bytes 3076
  60.4 21.1 %all-to-all-start.2 = ((f32[128,3,4,128]{3,2,1,0:T(4,128)}), f32[128,3,4,128]{3,2,1,0:T(4,128)S(1)}, u32[]{:S(2)}, u32[]{:S(2)}) async-start(f32[128,3,4,128]{3,2,1,0:T(4,128)} %bitcast.10), calls=%async_computation.2 | async-start | bytes 1572864 | tf_op jit(solution)/shard_map/all_to_all | solution.py:239
  70.2 11.3 %copy-start = (s32[8192]{0:T(1024)S(1)}, s32[8192]{0:T(1024)}, u32[]{:S(2)}) copy-start(s32[8192]{0:T(1024)} %param.10) | copy-start | bytes 98308
  116.3 21.0 %all-to-all-start.4 = ((f32[128,3,4,128]{3,2,1,0:T(4,128)}), f32[128,3,4,128]{3,2,1,0:T(4,128)S(1)}, u32[]{:S(2)}, u32[]{:S(2)}) async-start(f32[128,3,4,128]{3,2,1,0:T(4,128)} %bitcast.15), calls=%async_computation.4 | async-start | bytes 1572864 | tf_op jit(solution)/shard_map/all_to_all | solution.py:239

commit v2 on v1

--- a/solution.py
+++ b/solution.py
@@ -34,65 +34,74 @@
     return high, middle, rest - middle
 
 
-def leaf_parts(tile, row):
-    xyz = jnp.where(row < 3, tile - CENTRE, 0.0)
-    high, middle, low = split3(xyz)
-    norm = split3(jnp.sum(xyz * xyz, axis=0, keepdims=True))
-    mass = tile[3:4] * (1.0 / CUTOFF_SQ**2)
-    moment = jnp.where(row < 3, xyz * mass, jnp.where(row == 3, mass, 0.0))
-    mh, mm, ml = split3(moment)
-    weights = jnp.concatenate([mh + pltpu.roll(mm, 4, 0), ml], axis=0).astype(BF16)
-    return xyz, (high, middle, low), norm, weights
-
-
-def squared_distances(left, right, row):
-    _, (ah, am, al), (an0, an1, an2), _ = left
-    _, (bh, bm, bl), (bn0, bn1, bn2), _ = right
-    a_norm = jnp.where(
-        row == 0, an0, jnp.where(row == 1, an1, jnp.where(row == 2, an2, jnp.where(row < 6, 1.0, 0.0)))
-    )
-    b_norm = jnp.where(
-        row < 3, 1.0, jnp.where(row == 3, bn0, jnp.where(row == 4, bn1, jnp.where(row == 5, bn2, 0.0)))
-    )
-    bh, bm, bl = -2.0 * bh, -2.0 * bm, -2.0 * bl
-    zero = jnp.zeros_like(a_norm)
-    lhs = jnp.concatenate([ah, ah, am, ah, al, am, a_norm, zero], axis=0).astype(BF16)
-    rhs = jnp.concatenate([bh, bm, bh, bl, bh, bm, b_norm, zero], axis=0).astype(BF16)
+def pair_parts(tile, row):
+    vector = (row & 3) < 3
+    xyz = jnp.where(vector, tile - CENTRE, 0.0)
+    parts = split3(xyz)
+    square = xyz * xyz
+    norm = pltpu.roll(square, 1, 0) + pltpu.roll(square, 2, 0) + pltpu.roll(square, 3, 0)
+    norms = split3(norm + jnp.where(row == 3, SOFTENING, 0.0))
+    mass = jnp.where(row < 4, tile[3:4], tile[7:8]) * (1.0 / CUTOFF_SQ**2)
+    weights = split3(jnp.where(vector, xyz, 1.0) * mass)
+    weights = jnp.concatenate([*weights, jnp.zeros_like(xyz)], axis=0).astype(BF16)
+    return xyz, parts, norms, weights
+
+
+def softened_distances(parts, norms, row):
+    high, middle, low = parts
+    minus_two = jnp.where(row < 3, -2.0, 0.0)
+    h2, m2, l2 = (pltpu.roll(part, 4, 0) * minus_two for part in parts)
+    lhs, rhs = [], []
+    for left, right, norm in zip(parts, (h2, h2, h2), norms):
+        lhs.append(left + jnp.where(row == 3, norm, jnp.where(row == 7, 1.0, 0.0)))
+        rhs.append(right + jnp.where(row == 7, norm, jnp.where(row == 3, 1.0, 0.0)))
+    lhs = jnp.concatenate(lhs + [high, high, middle], axis=0).astype(BF16)
+    rhs = jnp.concatenate(rhs + [m2, l2, m2], axis=0).astype(BF16)
     return lax.dot_general(lhs, rhs, TN, preferred_element_type=F32)
 
 
-def pair_kernel(dist_sq):
-    taper = jnp.maximum(CUTOFF_SQ - dist_sq, 0.0)
-    root = lax.rsqrt(dist_sq + SOFTENING)
+def pair_kernel(softened):
+    taper = jnp.maximum((CUTOFF_SQ + SOFTENING) - softened, 0.0)
+    root = lax.rsqrt(softened)
     scaled = taper * root
     kernel = scaled * scaled * root
     high = kernel.astype(BF16)
     return high, (kernel - high.astype(F32)).astype(BF16)
 
 
-def moments(left, right, kernel):
+def moments(weights, kernel):
     high, low = kernel
-    rows = jnp.concatenate([high, low], axis=0)
-    columns = jnp.concatenate([high, low], axis=1)
-    on_left = lax.dot_general(right[3], rows, NT, preferred_element_type=F32)
-    on_right = lax.dot_general(left[3], columns, NN, preferred_element_type=F32)
-    return (on_left[:, :LEAF] + on_left[:, LEAF:], on_right[:, :LEAF] + on_right[:, LEAF:])
-
-
-def force_tile(moment, xyz):
-    total = moment[0:8] + moment[8:16]
-    total = total + pltpu.roll(total, 4, 0)
-    return total - (xyz + pltpu.roll(xyz, 4, 0)) * total[3:4]
+    twice = jnp.concatenate([weights, weights], axis=1)
+    on_left = lax.dot_general(
+        jnp.concatenate([high, low], axis=1), twice, NT, preferred_element_type=F32
+    ).T
+    on_right = lax.dot_general(
+        twice, jnp.concatenate([high, low], axis=0), NN, preferred_element_type=F32
+    )
+    return on_left, on_right
+
+
+def force_tile(sums, xyz, row):
+    on_left, on_right = (part[0:8] + part[8:16] + part[16:24] for part in sums)
+    total = jnp.where(row < 4, on_right, on_left)
+    mass = jnp.where(row < 4, total[3:4], total[7:8])
+    return total - pltpu.roll(xyz, 4, 0) * mass
 
 
 def pair_forces(tiles, row):
-    parts = [(leaf_parts(a, row), leaf_parts(b, row)) for a, b in tiles]
-    dists = [squared_distances(a, b, row) for a, b in parts]
-    kernels = [pair_kernel(q) for q in dists]
-    sums = [moments(a, b, k) for (a, b), k in zip(parts, kernels)]
-    return [
-        (force_tile(fa, a[0]), force_tile(fb, b[0])) for (a, b), (fa, fb) in zip(parts, sums)
-    ]
+    count, lag = len(tiles), 4
+    parts, dists, sums, out = {}, {}, {}, []
+    for step in range(count + 2 * lag):
+        if step < count:
+            parts[step] = pair_parts(tiles[step], row)
+            dists[step] = softened_distances(parts[step][1], parts[step][2], row)
+        k = step - lag
+        if 0 <= k < count:
+            sums[k] = moments(parts[k][3], pair_kernel(dists[k]))
+        k = step - 2 * lag
+        if k >= 0:
+            out.append(force_tile(sums[k], parts[k][0], row))
+    return out
 
 
 def row_iota():
@@ -134,40 +143,42 @@
 def local_kernel(pairs, state, forces):
     row = row_iota()
     forces[...] = jnp.zeros_like(forces)
-    unroll = 16
+    unroll = 32
 
     def body(step, carry):
         ids = [
-            (pairs[2 * (step * unroll + u)], pairs[2 * (step * unroll + u) + 1])
+            (pairs[0, step * unroll + u], pairs[1, step * unroll + u])
             for u in range(unroll)
         ]
-        found = pair_forces([(state[a], state[b]) for a, b in ids], row)
-        for (a, b), (fa, fb) in zip(ids, found):
-            forces[a] += fa
-            forces[b] += fb
+        found = pair_forces([jnp.where(row < 4, state[a], state[b]) for a, b in ids], row)
+        for (a, b), force in zip(ids, found):
+            forces[a] += jnp.where(row < 4, 0.0, force)
+            forces[b] += jnp.where(row < 4, force, 0.0)
         return carry
 
     lax.fori_loop(0, LOCAL // unroll, body, 0)
+    for leaf in range(NLEAF):
+        forces[leaf] += pltpu.roll(forces[leaf], 4, 0)
 
 
 def remote_kernel(placed, arrived, pushed):
     row = row_iota()
     pushed[...] = jnp.zeros_like(pushed)
-    unroll = 16
-
-    def leaf(slot):
+    unroll = 64
+
+    def leaf(slot, half):
         tile = arrived[pl.ds(pl.multiple_of((slot >> 1) * 8, 8), 8), :]
-        return jnp.where((slot & 1) == 1, pltpu.roll(tile, 4, 0), tile)
+        return jnp.where((slot & 1) == half, tile, pltpu.roll(tile, 4, 0))
 
     def body(step, carry):
         ids = [
-            (placed[2 * (step * unroll + u)], placed[2 * (step * unroll + u) + 1])
+            (placed[0, step * unroll + u], placed[1, step * unroll + u])
             for u in range(unroll)
         ]
-        found = pair_forces([(leaf(a), leaf(b)) for a, b in ids], row)
-        for (a, b), (fa, fb) in zip(ids, found):
-            pushed[pl.ds(3 * a, 3), :] = fa[0:3]
-            pushed[pl.ds(3 * b, 3), :] = fb[0:3]
+        found = pair_forces([jnp.where(row < 4, leaf(a, 0), leaf(b, 1)) for a, b in ids], row)
+        for (a, b), force in zip(ids, found):
+            pushed[pl.ds(3 * a, 3), :] = force[4:7]
+            pushed[pl.ds(3 * b, 3), :] = force[0:3]
         return carry
 
     lax.fori_loop(0, PAIRS // unroll, body, 0)
@@ -247,28 +258,48 @@
     return exchange(pushed.reshape(DEVICES, 3, CAP, LEAF)).reshape(3 * SLOTS, LEAF)
 
 
-def requests(pair_owner, pair_slot):
-    owners = pair_owner.reshape(2, 2 * PAIRS)
-    slots = pair_slot.reshape(2, 2 * PAIRS)
-    earlier = jnp.arange(2 * PAIRS)[None, :] < jnp.arange(2 * PAIRS)[:, None]
-    rank = jnp.sum(
-        ((owners[:, :, None] == owners[:, None, :]) & earlier[None]).astype(jnp.int32), axis=2
-    )
-    placed = owners * CAP + rank
-    spots = jnp.arange(SLOTS, dtype=jnp.int32)
-    wanted = NLEAF + jnp.sum(
-        jnp.where(placed[:, :, None] == spots[None, None, :], (slots - NLEAF)[:, :, None], 0), axis=1
-    )
-    return placed, wanted.reshape(2, DEVICES, CAP).transpose(1, 0, 2).reshape(DEVICES, 2 * CAP)
+def request_kernel(owners, slots, placed0, placed1, wanted):
+    ends = 2 * PAIRS
+    owner_of = lax.broadcasted_iota(jnp.int32, (DEVICES, ends), 0)
+    earlier = lax.broadcasted_iota(jnp.int32, (ends, ends), 0) < lax.broadcasted_iota(
+        jnp.int32, (ends, ends), 1
+    )
+    earlier = jnp.where(earlier, 1.0, 0.0).astype(BF16)
+    column = lax.broadcasted_iota(jnp.int32, (ends, LEAF), 1)
+    total = jnp.zeros((DEVICES, LEAF), F32)
+    for sub, placed in enumerate((placed0, placed1)):
+        owner = jnp.concatenate([owners[sub, 0:1], owners[sub, 1:2]], axis=1)
+        slot = jnp.concatenate([slots[sub, 0:1], slots[sub, 1:2]], axis=1) - NLEAF
+        hit = jnp.where(owner_of == owner, 1.0, 0.0)
+        before = lax.dot_general(hit.astype(BF16), earlier, NN, preferred_element_type=F32)
+        rank = jnp.sum(hit * before, axis=0, keepdims=True)
+        place = CAP * owner + rank.astype(jnp.int32)
+        placed[0:1, :] = place[:, :PAIRS]
+        placed[1:2, :] = place[:, PAIRS:]
+        asked = hit * slot.astype(F32)
+        for turn in range(CAP):
+            mine = jnp.where(before == float(turn), asked, 0.0).astype(BF16)
+            here = jnp.where(column == CAP * sub + turn, 1.0, 0.0).astype(BF16)
+            total += lax.dot_general(mine, here, NN, preferred_element_type=F32)
+    wanted[...] = total.astype(jnp.int32) + NLEAF
 
 
 def shards(positions, velocities, masses, time_bins, pair_owner, pair_slot, local_pairs):
     masses = masses.reshape(NLEAF, LEAF)
     bins = time_bins.reshape(NLEAF, LEAF)
-    placed, wanted = requests(pair_owner, pair_slot)
-    asked = exchange(wanted).reshape(DEVICES, 2, CAP).transpose(1, 0, 2).reshape(2, SLOTS)
+    ints = jax.ShapeDtypeStruct((2, PAIRS), jnp.int32)
+    *placed, wanted = call(
+        request_kernel,
+        (ints, ints, jax.ShapeDtypeStruct((DEVICES, LEAF), jnp.int32)),
+        [],
+        [pair_owner.transpose(0, 2, 1), pair_slot.transpose(0, 2, 1)],
+        2**26,
+        2**18,
+    )
+    asked = exchange(wanted.reshape(DEVICES, 1, LEAF)).reshape(DEVICES, LEAF)[:, : 2 * CAP]
+    asked = asked.reshape(DEVICES, 2, CAP).transpose(1, 0, 2).reshape(2, SLOTS)
     codes = (4 * asked[:, :, None] + jnp.arange(3, dtype=jnp.int32)).reshape(2, 1, 3 * SLOTS)
-    local_ids = local_pairs.reshape(2, 2 * LOCAL)
+    local_ids = local_pairs.transpose(0, 2, 1)
 
     state_shape = shape(NLEAF + 1, 8, LEAF)
     moving_shape = shape(NLEAF, 8, LEAF)

time: 139 us -> 132 us (0.950)
  blocking collectives: 23.6 us -> 47.3 us
  waiting for transfers between devices: 51.4 us -> 34.5 us
  Pallas kernels: 33 us -> 25.7 us
  starting transfers between devices: 24.9 us -> 20.4 us
  local copies, waits for them, and re-layouts: 4.42 us -> 2.64 us
    all_to_all x1 -> x2, blocking collectives: 23.6 us -> 47.3 us  [exchange(): return lax.all_to_all(array, AXES, split_axis=0, concat_axis=0, tiled=True)]
    all_to_all x4 -> x3, waiting for transfers between devices: 51.4 us -> 34.5 us  [exchange(): return lax.all_to_all(array, AXES, split_axis=0, concat_axis=0, tiled=True)]
    pallas_call x8 -> x9, Pallas kernels: 33 us -> 25.7 us  [call(): pl.pallas_call(kernel, out_shape=out_shapes, grid_spec=pltpu.PrefetchScal...]
    all_to_all x4 -> x3, starting transfers between devices: 24.9 us -> 20.4 us  [exchange(): return lax.all_to_all(array, AXES, split_axis=0, concat_axis=0, tiled=True)]
  transfers between devices with their start and end apart: 4 -> 3, of which waited for: 4 -> 3; matrix products, arithmetic and copies ran while one was open for 1% -> 1% of each run, Pallas kernels for 6% -> 5%
where the time goes in v2:
time: 132 us
  blocking collectives  47.3 us (36%)
  waiting for transfers between devices  34.5 us (26%)
  Pallas kernels  25.7 us (19%)
  starting transfers between devices  20.4 us (15%)
  local copies, waits for them, and re-layouts  2.64 us (2%)
    all_to_all x2, blocking collectives, exchange(): return lax.all_to_all(array, AXES, split_axis=0, concat_axis=0, tiled=True)  47.3 us
    all_to_all x3, waiting for transfers between devices, exchange(): return lax.all_to_all(array, AXES, split_axis=0, concat_axis=0, tiled=True)  34.5 us
    pallas_call x9, Pallas kernels, call(): pl.pallas_call(kernel, out_shape=out_shapes, grid_spec=pltpu.PrefetchScal...  25.7 us
    all_to_all x3, starting transfers between devices, exchange(): return lax.all_to_all(array, AXES, split_axis=0, concat_axis=0, tiled=True)  20.4 us
  transfers between devices with their start and end apart: 3, of which 3 were waited for; matrix products, arithmetic and copies ran while one was open for 1% of the time, Pallas kernels for 5%

profile of v2, /device:TPU:1, one launch (start us, length us, event | category | flops | bytes accessed | tf_op | source)
XLA Modules:
  0.0 131.6 jit_solution(3458915280469906009)
XLA Ops:
  0.6 0.0 copy-start.4
  0.6 0.7 copy-done.4
  1.3 0.0 copy-start.5
  1.3 0.7 copy-done.5
  2.0 0.0 copy-start.1
  2.0 0.0 copy-start.2
  2.0 1.2 shard_map.94
  3.2 0.0 copy-start.3
  3.2 11.5 %all-to-all-start = ((s32[128,1,128]{2,1,0:T(1,128)}), s32[128,1,128]{2,1,0:T(1,128)S(1)}, u32[]{:S(2)}, u32[]{:S(2)}) async-start(s32[128,1,128]{2,1,0:T(1,128)} %bitcast.3), calls=%async_computation | async-start | bytes 131072 | tf_op jit(solution)/shard_map/all_to_all | solution.py:250
  14.7 0.0 copy-done.1
  14.7 0.0 copy-done.2
  14.7 0.0 copy-done.3
  14.7 0.1 shard_map.95
  14.9 9.2 %all-to-all-done = s32[128,1,128]{2,1,0:T(1,128)S(1)} async-done(((s32[128,1,128]{2,1,0:T(1,128)}), s32[128,1,128]{2,1,0:T(1,128)S(1)}, u32[]{:S(2)}, u32[]{:S(2)}) %all-to-all-start) | async-done | bytes 65568 | tf_op jit(solution)/shard_map/all_to_all | solution.py:250
  24.1 0.1 copy.15
  24.2 0.1 copy.18
  24.3 0.1 squeeze.21.asked
  24.5 1.2 shard_map.96
  25.6 23.8 %all_to_all.25 = f32[128,16,128]{2,1,0:T(8,128)S(1)} all-to-all(f32[128,16,128]{2,1,0:T(8,128)S(1)} %bitcast.24), channel_id=1, replica_groups=mesh['gx'=4,'gy'=4,'gz'=8] {'gx','gy','gz'}, dimensions={0} | all-to-all | bytes 2097152 | tf_op jit(solution)/shard_map/all_to_all | solution.py:250
  49.4 6.3 %shard_map.97 = f32[1536,128]{1,0:T(8,128)} custom-call(s32[2,128]{1,0:T(2,128)S(1)} %get-tuple-element.13.placed, f32[2048,128]{1,0:T(8,128)S(1)} %bitcast.26), custom_call_target="tpu_custom_call" | custom-call | flops 52428800 | bytes 2097152 | tf_op jit(solution)/shard_map/pallas_call | solution.py:231
  55.7 0.0 copy-start.6
  55.7 4.4 %all-to-all-start.2 = ((f32[128,3,4,128]{3,2,1,0:T(4,128)}), f32[128,3,4,128]{3,2,1,0:T(4,128)S(1)}, u32[]{:S(2)}, u32[]{:S(2)}) async-start(f32[128,3,4,128]{3,2,1,0:T(4,128)} %bitcast.11), calls=%async_computation.2 | async-start | bytes 1572864 | tf_op jit(solution)/shard_map/all_to_all | solution.py:250
  60.2 0.0 copy-done.6
  60.2 3.4 %shard_map.98.local = f32[64,8,128]{2,1,0:T(8,128)S(1)} custom-call(s32[2,64]{1,0:T(2,128)S(1)} %get-tuple-element.24.pairs, f32[65,8,128]{2,1,0:T(8,128)S(1)} %get-tuple-element.14.state), custom_call_target="tpu_custom_call" | custom-call | flops 26214400 | bytes 1048576 | tf_op jit(solution)/shard_map/pallas_call | solution.py:231
  63.6 0.1 copy.17
  63.7 0.1 squeeze.19.asked
  63.8 0.1 copy.16
  64.0 0.1 mul.16
  64.1 0.2 iota_add_fusion
  64.4 0.0 copy-start
  64.4 0.2 squeeze.20.codes
  64.6 12.3 %all-to-all-done.2 = f32[128,3,4,128]{3,2,1,0:T(4,128)S(1)} async-done(((f32[128,3,4,128]{3,2,1,0:T(4,128)}), f32[128,3,4,128]{3,2,1,0:T(4,128)S(1)}, u32[]{:S(2)}, u32[]{:S(2)}) %all-to-all-start.2) | async-done | bytes 786464 | tf_op jit(solution)/shard_map/all_to_all | solution.py:250
  76.8 0.0 copy-done
  76.8 2.1 %shard_map.99 = (f32[2048,128]{1,0:T(8,128)S(1)}, f32[65,8,128]{2,1,0:T(8,128)S(1)}, f32[64,8,128]{2,1,0:T(8,128)S(1)}) custom-call(s32[512]{0:T(512)S(1)} %squeeze.19.asked, s32[1,1536]{1,0:T(1,128)S(1)} %squeeze.20.codes, f32[1536,128]{1,0:T(8,128)S(1)} %bitcast.27, f32[64,8,128]{2,1,0:T(8,128)S(1)} %shard_map.98.local, ...), custom_call_target="tpu_custom_call" | custom-call | flops 65536 | bytes 4194304 | tf_op jit(solution)/shard_map/pallas_call | solution.py:231
  78.9 23.6 %all_to_all.26 = f32[128,16,128]{2,1,0:T(8,128)S(1)} all-to-all(f32[128,16,128]{2,1,0:T(8,128)S(1)} %bitcast.29), channel_id=1, replica_groups=mesh['gx'=4,'gy'=4,'gz'=8] {'gx','gy','gz'}, dimensions={0} | all-to-all | bytes 2097152 | tf_op jit(solution)/shard_map/all_to_all | solution.py:250
  102.5 6.3 %shard_map.100 = f32[1536,128]{1,0:T(8,128)} custom-call(s32[2,128]{1,0:T(2,128)S(1)} %get-tuple-element.12.placed, f32[2048,128]{1,0:T(8,128)S(1)} %bitcast.25), custom_call_target="tpu_custom_call" | custom-call | flops 52428800 | bytes 2097152 | tf_op jit(solution)/shard_map/pallas_call | solution.py:231
  108.8 4.5 %all-to-all-start.4 = ((f32[128,3,4,128]{3,2,1,0:T(4,128)}), f32[128,3,4,128]{3,2,1,0:T(4,128)S(1)}, u32[]{:S(2)}, u32[]{:S(2)}) async-start(f32[128,3,4,128]{3,2,1,0:T(4,128)} %bitcast.18), calls=%async_computation.4 | async-start | bytes 1572864 | tf_op jit(solution)/shard_map/all_to_all | solution.py:250
  113.3 0.2 squeeze.18.codes
  113.5 3.4 %shard_map.101.local = f32[64,8,128]{2,1,0:T(8,128)S(1)} custom-call(s32[2,64]{1,0:T(2,128)S(1)} %get-tuple-element.23.pairs, f32[65,8,128]{2,1,0:T(8,128)S(1)} %get-tuple-element.17.state), custom_call_target="tpu_custom_call" | custom-call | flops 26214400 | bytes 1048576 | tf_op jit(solution)/shard_map/pallas_call | solution.py:231
  116.9 13.0 %all-to-all-done.4 = f32[128,3,4,128]{3,2,1,0:T(4,128)S(1)} async-done(((f32[128,3,4,128]{3,2,1,0:T(4,128)}), f32[128,3,4,128]{3,2,1,0:T(4,128)S(1)}, u32[]{:S(2)}, u32[]{:S(2)}) %all-to-all-start.4) | async-done | bytes 786464 | tf_op jit(solution)/shard_map/all_to_all | solution.py:250
  130.0 1.6 %shard_map.102 = (f32[3,8192]{1,0:T(4,128)}, f32[3,8192]{1,0:T(4,128)}, f32[3,8192]{1,0:T(4,128)}) custom-call(s32[1,1536]{1,0:T(1,128)S(1)} %squeeze.18.codes, f32[1536,128]{1,0:T(8,128)S(1)} %bitcast.28, f32[64,8,128]{2,1,0:T(8,128)S(1)} %shard_map.101.local, f32[65,8,128]{2,1,0:T(8,128)S(1)} %get-tuple-element.17.state, ...), custom_call_target="tpu_custom_call" | custom-call | flops 65536 | bytes 4194304 | tf_op jit(solution)/shard_map/pallas_call | solution.py:231
  (5 shorter events, 0.0 us)
Async XLA Ops:
  0.6 0.7 copy-start.4
  1.3 0.7 copy-start.5
  2.0 12.7 %copy-start.1 = (f32[3,8192]{1,0:T(4,128)S(1)}, f32[3,8192]{1,0:T(4,128)}, u32[]{:S(2)}) copy-start(f32[3,8192]{1,0:T(4,128)} %positions.1) | copy-start | bytes 294916
  2.0 12.7 %copy-start.2 = (f32[3,8192]{1,0:T(4,128)S(1)}, f32[3,8192]{1,0:T(4,128)}, u32[]{:S(2)}) copy-start(f32[3,8192]{1,0:T(4,128)} %velocities.1) | copy-start | bytes 294916
  3.2 11.5 %copy-start.3 = (f32[8192]{0:T(1024)S(1)}, f32[8192]{0:T(1024)}, u32[]{:S(2)}) copy-start(f32[8192]{0:T(1024)} %param.9) | copy-start | bytes 98308
  3.2 20.9 %all-to-all-start = ((s32[128,1,128]{2,1,0:T(1,128)}), s32[128,1,128]{2,1,0:T(1,128)S(1)}, u32[]{:S(2)}, u32[]{:S(2)}) async-start(s32[128,1,128]{2,1,0:T(1,128)} %bitcast.3), calls=%async_computation | async-start | bytes 131072 | tf_op jit(solution)/shard_map/all_to_all | solution.py:250
  55.7 4.4 %copy-start.6 = (s32[2,64,2]{1,2,0:T(2,128)S(1)}, s32[2,64,2]{1,2,0:T(2,128)}, u32[]{:S(2)}) copy-start(s32[2,64,2]{1,2,0:T(2,128)} %param.13) | copy-start | bytes 3076
  55.7 21.1 %all-to-all-start.2 = ((f32[128,3,4,128]{3,2,1,0:T(4,128)}), f32[128,3,4,128]{3,2,1,0:T(4,128)S(1)}, u32[]{:S(2)}, u32[]{:S(2)}) async-start(f32[128,3,4,128]{3,2,1,0:T(4,128)} %bitcast.11), calls=%async_computation.2 | async-start | bytes 1572864 | tf_op jit(solution)/shard_map/all_to_all | solution.py:250
  64.4 12.5 %copy-start = (s32[8192]{0:T(1024)S(1)}, s32[8192]{0:T(1024)}, u32[]{:S(2)}) copy-start(s32[8192]{0:T(1024)} %param.10) | copy-start | bytes 98308
  108.8 21.2 %all-to-all-start.4 = ((f32[128,3,4,128]{3,2,1,0:T(4,128)}), f32[128,3,4,128]{3,2,1,0:T(4,128)S(1)}, u32[]{:S(2)}, u32[]{:S(2)}) async-start(f32[128,3,4,128]{3,2,1,0:T(4,128)} %bitcast.18), calls=%async_computation.4 | async-start | bytes 1572864 | tf_op jit(solution)/shard_map/all_to_all | solution.py:250

commit v3 on v2

--- a/solution.py
+++ b/solution.py
@@ -108,36 +108,53 @@
     return lax.broadcasted_iota(jnp.int32, (8, LEAF), 0)
 
 
-def fill_slots(asked, state, looked):
+def leaf_tile(state, leaf):
+    return state[pl.ds(pl.multiple_of(leaf * 8, 8), 8), :]
+
+
+def fill_slots(first, asked, state, looked):
     row = row_iota()
 
     def body(step, carry):
-        for u in range(16):
-            tile = step * 16 + u
-            looked[pl.ds(pl.multiple_of(tile * 8, 8), 8), :] = jnp.where(
-                row < 4, state[asked[2 * tile]], state[asked[2 * tile + 1]]
-            )
+        for u in range(8):
+            worker = step * 8 + u
+            for half in range(2):
+                left = leaf_tile(state, asked[first + 2 * half, worker])
+                right = leaf_tile(state, asked[first + 2 * half + 1, worker])
+                looked[pl.ds(pl.multiple_of(worker * 16 + half * 8, 8), 8), :] = jnp.where(
+                    row < 4, left, right
+                )
         return carry
 
-    lax.fori_loop(0, SLOTS // 32, body, 0)
-
-
-def pack_kernel(positions, velocities, masses, state, moving):
+    lax.fori_loop(0, DEVICES // 8, body, 0)
+
+
+def component(index):
+    return slice(index * NLEAF, (index + 1) * NLEAF)
+
+
+def store_state(state, index, value):
+    state[pl.ds(index, NLEAF, stride=8), :] = value
+    state[pl.ds(index + 4, NLEAF, stride=8), :] = value
+
+
+def pack_kernel(positions, velocities, masses, state, where, moving):
     for leaf in range(NLEAF):
         lanes = slice(leaf * LEAF, (leaf + 1) * LEAF)
-        state[leaf, 0:3, :] = positions[:, lanes]
-        state[leaf, 4:7, :] = positions[:, lanes]
-        state[leaf, 3:4, :] = masses[leaf : leaf + 1, :]
-        state[leaf, 7:8, :] = masses[leaf : leaf + 1, :]
-        moving[leaf, 0:3, :] = velocities[:, lanes]
-        moving[leaf, 4:7, :] = velocities[:, lanes]
-        moving[leaf, 3:4, :] = jnp.zeros((1, LEAF), F32)
-        moving[leaf, 7:8, :] = jnp.zeros((1, LEAF), F32)
-    state[NLEAF] = jnp.zeros((8, LEAF), F32)
-
-
-def gather_kernel(asked, state, looked):
-    fill_slots(asked, state, looked)
+        where[pl.ds(leaf, 3, stride=NLEAF), :] = positions[:, lanes]
+        moving[pl.ds(leaf, 3, stride=NLEAF), :] = velocities[:, lanes]
+    for index in range(3):
+        store_state(state, index, where[component(index), :])
+    store_state(state, 3, masses[...])
+    state[8 * NLEAF :, :] = jnp.zeros((8, LEAF), F32)
+
+
+def gather_kernel(wanted, state, _, looked, asked, scalars, sem):
+    asked[...] = wanted[...].T[: 2 * CAP]
+    copy = pltpu.make_async_copy(asked, scalars, sem)
+    copy.start()
+    copy.wait()
+    fill_slots(0, scalars, state, looked)
 
 
 def local_kernel(pairs, state, forces):
@@ -150,20 +167,23 @@
             (pairs[0, step * unroll + u], pairs[1, step * unroll + u])
             for u in range(unroll)
         ]
-        found = pair_forces([jnp.where(row < 4, state[a], state[b]) for a, b in ids], row)
+        found = pair_forces([jnp.where(row < 4, leaf_tile(state, a), leaf_tile(state, b)) for a, b in ids], row)
         for (a, b), force in zip(ids, found):
-            forces[a] += jnp.where(row < 4, 0.0, force)
-            forces[b] += jnp.where(row < 4, force, 0.0)
+            to_left = pl.ds(pl.multiple_of(a * 8, 8), 8)
+            to_right = pl.ds(pl.multiple_of(b * 8, 8), 8)
+            forces[to_left, :] += jnp.where(row < 4, 0.0, force)
+            forces[to_right, :] += jnp.where(row < 4, force, 0.0)
         return carry
 
     lax.fori_loop(0, LOCAL // unroll, body, 0)
-    for leaf in range(NLEAF):
-        forces[leaf] += pltpu.roll(forces[leaf], 4, 0)
-
-
-def remote_kernel(placed, arrived, pushed):
+
+
+def remote_kernel(places, arrived, pushed, placed, sem):
     row = row_iota()
+    copy = pltpu.make_async_copy(places, placed, sem)
+    copy.start()
     pushed[...] = jnp.zeros_like(pushed)
+    copy.wait()
     unroll = 64
 
     def leaf(slot, half):
@@ -184,66 +204,75 @@
     lax.fori_loop(0, PAIRS // unroll, body, 0)
 
 
-def summed_tiles(codes, returned):
-    target = lax.broadcasted_iota(jnp.int32, (4 * NLEAF, 3 * SLOTS), 0)
-    chosen = jnp.where(target == codes[...], 1.0, 0.0).astype(BF16)
-    total = jnp.zeros((4 * NLEAF, LEAF), F32)
-    for part in split3(returned[...]):
-        total = total + lax.dot_general(chosen, part.astype(BF16), NN, preferred_element_type=F32)
+def summed(first, asked, returned):
+    target = lax.broadcasted_iota(jnp.int32, (NLEAF, DEVICES), 0)
+    chosen, blocks = [], []
+    for turn in range(CAP):
+        chosen.append(jnp.where(target == asked[first + turn : first + turn + 1, :], 1.0, 0.0))
+        rows = [
+            returned[pl.ds(3 * turn + index, DEVICES, stride=3 * CAP), :] for index in range(3)
+        ]
+        blocks.append(jnp.concatenate(rows, axis=1))
+    chosen = jnp.concatenate(chosen, axis=1).astype(BF16)
+    total = jnp.zeros((NLEAF, 3 * LEAF), F32)
+    for part in split3(jnp.concatenate(blocks, axis=0)):
+        total += lax.dot_general(chosen, part.astype(BF16), NN, preferred_element_type=F32)
     return total
 
 
-def kick_drift(threshold, codes, returned, local, state, moving, bins, leaf_done):
-    row = row_iota()
-    total = summed_tiles(codes, returned)
+def kick_drift(subcycle, asked, returned, local, where, moving, bins):
+    total = summed(CAP * subcycle, asked, returned)
+    active = bins[...] >= 3 - subcycle
+    for index in range(3):
+        accel = total[:, index * LEAF : (index + 1) * LEAF]
+        accel += local[pl.ds(index, NLEAF, stride=8), :] + local[pl.ds(index + 4, NLEAF, stride=8), :]
+        velocity = moving[component(index), :] + jnp.where(active, TIME_STEP * accel, 0.0)
+        yield index, accel, velocity, where[component(index), :] + TIME_STEP * velocity
+
+
+def advance_kernel(
+    asked, returned, local, masses, where, moving, bins, looked, state, new_where, new_moving, scalars, sem
+):
+    copy = pltpu.make_async_copy(asked, scalars, sem)
+    copy.start()
+    store_state(state, 3, masses[...])
+    state[8 * NLEAF :, :] = jnp.zeros((8, LEAF), F32)
+    for index, _, velocity, position in kick_drift(0, asked, returned, local, where, moving, bins):
+        new_moving[component(index), :] = velocity
+        new_where[component(index), :] = position
+        store_state(state, index, position)
+    copy.wait()
+    fill_slots(CAP, scalars, state, looked)
+
+
+def finish_kernel(asked, returned, local, where, moving, bins, positions, velocities, accels, rows):
+    for index, *results in kick_drift(1, asked, returned, local, where, moving, bins):
+        for number, result in enumerate(results):
+            rows[number, component(index), :] = result
     for leaf in range(NLEAF):
-        pair = total[leaf // 2 * 8 : leaf // 2 * 8 + 8]
-        other = pltpu.roll(pair, 4, 0)
-        mine = jnp.where(row < 4, pair, other) if leaf % 2 == 0 else jnp.where(row < 4, other, pair)
-        accel = jnp.where((row & 3) < 3, mine + local[leaf], 0.0)
-        active = bins[leaf : leaf + 1, :] >= threshold
-        velocity = moving[leaf] + jnp.where(active, TIME_STEP * accel, 0.0)
-        position = state[leaf] + TIME_STEP * velocity
-        leaf_done(leaf, position, velocity, accel)
-
-
-def advance_kernel(asked, codes, returned, local, state, moving, bins, looked, new_state, new_moving):
-    def leaf_done(leaf, position, velocity, accel):
-        new_state[leaf] = position
-        new_moving[leaf] = velocity
-
-    kick_drift(3, codes, returned, local, state, moving, bins, leaf_done)
-    new_state[NLEAF] = jnp.zeros((8, LEAF), F32)
-    fill_slots(asked, new_state, looked)
-
-
-def finish_kernel(codes, returned, local, state, moving, bins, positions, velocities, accels):
-    def leaf_done(leaf, position, velocity, accel):
         lanes = slice(leaf * LEAF, (leaf + 1) * LEAF)
-        positions[:, lanes] = position[0:3]
-        velocities[:, lanes] = velocity[0:3]
-        accels[:, lanes] = accel[0:3]
-
-    kick_drift(2, codes, returned, local, state, moving, bins, leaf_done)
-
-
-def call(kernel, out_shapes, scalars, arrays, flops, size):
+        for number, out in enumerate((accels, velocities, positions)):
+            out[:, lanes] = rows[number, pl.ds(leaf, 3, stride=NLEAF), :]
+
+
+def call(kernel, out_shapes, arrays, flops, size, scratch=(), in_specs=None, scalars=()):
     return pl.pallas_call(
         kernel,
         out_shape=out_shapes,
         grid_spec=pltpu.PrefetchScalarGridSpec(
             num_scalar_prefetch=len(scalars),
             grid=(),
-            in_specs=[VMEM] * len(arrays),
+            in_specs=in_specs or [VMEM] * len(arrays),
             out_specs=jax.tree.map(lambda _: VMEM, out_shapes),
+            scratch_shapes=scratch,
         ),
         compiler_params=pltpu.CompilerParams(vmem_limit_bytes=40 * 2**20),
         cost_estimate=pl.CostEstimate(flops=flops, bytes_accessed=size, transcendentals=0),
     )(*scalars, *arrays)
 
 
-def shape(*dims):
-    return jax.ShapeDtypeStruct(dims, F32)
+def shape(*dims, dtype=F32):
+    return jax.ShapeDtypeStruct(dims, dtype)
 
 
 def exchange(array):
@@ -258,7 +287,15 @@
     return exchange(pushed.reshape(DEVICES, 3, CAP, LEAF)).reshape(3 * SLOTS, LEAF)
 
 
-def request_kernel(owners, slots, placed0, placed1, wanted):
+def request_kernel(pair_owner, pair_slot, placed0, placed1, wanted, owners, slots, sems):
+    copies = [
+        pltpu.make_async_copy(pair_owner, owners, sems.at[0]),
+        pltpu.make_async_copy(pair_slot, slots, sems.at[1]),
+    ]
+    for copy in copies:
+        copy.start()
+    for copy in copies:
+        copy.wait()
     ends = 2 * PAIRS
     owner_of = lax.broadcasted_iota(jnp.int32, (DEVICES, ends), 0)
     earlier = lax.broadcasted_iota(jnp.int32, (ends, ends), 0) < lax.broadcasted_iota(
@@ -287,45 +324,63 @@
 def shards(positions, velocities, masses, time_bins, pair_owner, pair_slot, local_pairs):
     masses = masses.reshape(NLEAF, LEAF)
     bins = time_bins.reshape(NLEAF, LEAF)
-    ints = jax.ShapeDtypeStruct((2, PAIRS), jnp.int32)
+    local_ids = local_pairs.transpose(0, 2, 1)
+    state_shape = shape(8 * (NLEAF + 1), LEAF)
+    local_shape = shape(8 * NLEAF, LEAF)
+    rows_shape = shape(3 * NLEAF, LEAF)
+    looked_shape = shape(4 * SLOTS, LEAF)
+    pushed_shape = shape(3 * SLOTS, LEAF)
+    asked_shape = shape(2 * CAP, DEVICES, dtype=jnp.int32)
+    ends_shape = shape(2, PAIRS, dtype=jnp.int32)
+    anywhere = pl.BlockSpec(memory_space=pl.ANY)
+    dma = pltpu.SemaphoreType.DMA
+    asked_scratch = [pltpu.SMEM((2 * CAP, DEVICES), jnp.int32), dma(())]
+
+    def local_forces(ids, state):
+        return call(local_kernel, local_shape, [state], 64 * 2**14 * 25, 2**20, scalars=[ids])
+
+    def remote_forces(places, arrived):
+        scratch = [pltpu.SMEM((2, PAIRS), jnp.int32), dma(())]
+        return call(
+            remote_kernel, pushed_shape, [places, arrived], 128 * 2**14 * 25, 2**21, scratch
+        )
+
     *placed, wanted = call(
         request_kernel,
-        (ints, ints, jax.ShapeDtypeStruct((DEVICES, LEAF), jnp.int32)),
-        [],
+        (ends_shape, ends_shape, shape(DEVICES, LEAF, dtype=jnp.int32)),
         [pair_owner.transpose(0, 2, 1), pair_slot.transpose(0, 2, 1)],
         2**26,
         2**18,
-    )
-    asked = exchange(wanted.reshape(DEVICES, 1, LEAF)).reshape(DEVICES, LEAF)[:, : 2 * CAP]
-    asked = asked.reshape(DEVICES, 2, CAP).transpose(1, 0, 2).reshape(2, SLOTS)
-    codes = (4 * asked[:, :, None] + jnp.arange(3, dtype=jnp.int32)).reshape(2, 1, 3 * SLOTS)
-    local_ids = local_pairs.transpose(0, 2, 1)
-
-    state_shape = shape(NLEAF + 1, 8, LEAF)
-    moving_shape = shape(NLEAF, 8, LEAF)
-    looked_shape = shape(4 * SLOTS, LEAF)
-    pushed_shape = shape(3 * SLOTS, LEAF)
-
-    def local_forces(ids, state):
-        return call(local_kernel, moving_shape, [ids], [state], 64 * 2**14 * 25, 2**20)
-
-    def remote_forces(ids, arrived):
-        return call(remote_kernel, pushed_shape, [ids], [arrived], 128 * 2**14 * 25, 2**21)
-
-    state, moving = call(
-        pack_kernel, (state_shape, moving_shape), [], [positions, velocities, masses], 2**16, 2**20
+        [pltpu.VMEM((2, 2, PAIRS), jnp.int32), pltpu.VMEM((2, 2, PAIRS), jnp.int32), dma((2,))],
+        [pl.BlockSpec(memory_space=pltpu.HBM)] * 2,
+    )
+    wanted = exchange(wanted.reshape(DEVICES, 1, LEAF)).reshape(DEVICES, LEAF)
+    state, where, moving = call(
+        pack_kernel,
+        (state_shape, rows_shape, rows_shape),
+        [positions, velocities, masses],
+        2**16,
+        2**20,
     )
     local = local_forces(local_ids[0], state)
-    looked = call(gather_kernel, looked_shape, [asked[0]], [state], 2**16, 2**21)
+    looked, asked = call(
+        gather_kernel,
+        (looked_shape, asked_shape),
+        [wanted, state, local],
+        2**16,
+        2**21,
+        asked_scratch,
+        [VMEM, VMEM, anywhere],
+    )
     pushed = remote_forces(placed[0], send_leaves(looked))
     returned = send_forces(pushed)
-    looked, state, moving = call(
+    looked, state, where, moving = call(
         advance_kernel,
-        (looked_shape, state_shape, moving_shape),
-        [asked[1]],
-        [codes[0], returned, local, state, moving, bins],
+        (looked_shape, state_shape, rows_shape, rows_shape),
+        [asked, returned, local, masses, where, moving, bins],
         2**16,
         2**22,
+        asked_scratch,
     )
     local = local_forces(local_ids[1], state)
     pushed = remote_forces(placed[1], send_leaves(looked))
@@ -334,10 +389,10 @@
     return call(
         finish_kernel,
         (out, out, out),
-        [],
-        [codes[1], returned, local, state, moving, bins],
+        [asked, returned, local, where, moving, bins],
         2**16,
         2**22,
+        [pltpu.VMEM((3, 3 * NLEAF, LEAF), F32)],
     )
 
 

time: 132 us -> 130 us (0.985)
  blocking collectives: 47.3 us -> 68 us
  waiting for transfers between devices: 34.5 us -> 19.1 us
  starting transfers between devices: 20.4 us -> 15.8 us
  Pallas kernels: 25.7 us -> 24.2 us
    all_to_all x2 -> x3, blocking collectives: 47.3 us -> 68 us  [exchange(): return lax.all_to_all(array, AXES, split_axis=0, concat_axis=0, tiled=True)]
    all_to_all x3 -> x2, waiting for transfers between devices: 34.5 us -> 19.1 us  [exchange(): return lax.all_to_all(array, AXES, split_axis=0, concat_axis=0, tiled=True)]
    all_to_all x3 -> x2, starting transfers between devices: 20.4 us -> 15.8 us  [exchange(): return lax.all_to_all(array, AXES, split_axis=0, concat_axis=0, tiled=True)]
    pallas_call x9, Pallas kernels: 25.7 us -> 24.2 us  [call(): pl.pallas_call(kernel, out_shape=out_shapes, grid_spec=pltpu.PrefetchScal...]
  transfers between devices with their start and end apart: 3 -> 2, of which waited for: 3 -> 2; matrix products, arithmetic and copies ran while one was open for 1% -> 0% of each run, Pallas kernels for 5% -> 5%
where the time goes in v3:
time: 130 us; the launch traced here: 129 us
  blocking collectives  68 us (52%)
  Pallas kernels  24.2 us (19%)
  waiting for transfers between devices  19.1 us (15%)
  starting transfers between devices  15.8 us (12%)
  local copies, waits for them, and re-layouts  1.39 us (1%)
    all_to_all x3, blocking collectives, exchange(): return lax.all_to_all(array, AXES, split_axis=0, concat_axis=0, tiled=True)  68 us
    pallas_call x9, Pallas kernels, call(): pl.pallas_call(kernel, out_shape=out_shapes, grid_spec=pltpu.PrefetchScal...  24.2 us
    all_to_all x2, waiting for transfers between devices, exchange(): return lax.all_to_all(array, AXES, split_axis=0, concat_axis=0, tiled=True)  19.1 us
    all_to_all x2, starting transfers between devices, exchange(): return lax.all_to_all(array, AXES, split_axis=0, concat_axis=0, tiled=True)  15.8 us
  transfers between devices with their start and end apart: 2, of which 2 were waited for; matrix products, arithmetic and copies ran while one was open for 0% of the time, Pallas kernels for 5%

profile of v3, /device:TPU:1, one launch (start us, length us, event | category | flops | bytes accessed | tf_op | source)
XLA Modules:
  0.0 129.3 jit_solution(10348607688522469544)
XLA Ops:
  0.6 0.0 copy-start.4
  0.6 0.7 copy-done.4
  1.3 0.0 copy-start.5
  1.3 0.7 copy-done.5
  2.0 0.0 copy-start.2
  2.0 0.0 copy-start.3
  2.0 1.2 shard_map.94
  3.2 0.0 copy-start.6
  3.2 0.0 copy-start
  3.2 11.5 %all-to-all-start = ((s32[128,1,128]{2,1,0:T(1,128)}), s32[128,1,128]{2,1,0:T(1,128)S(1)}, u32[]{:S(2)}, u32[]{:S(2)}) async-start(s32[128,1,128]{2,1,0:T(1,128)} %bitcast.3), calls=%async_computation | async-start | bytes 131072 | tf_op jit(solution)/shard_map/all_to_all | solution.py:279
  14.8 0.0 copy-done.6
  14.8 0.0 copy-done.2
  14.8 0.0 copy-done.3
  14.8 0.0 copy-done
  14.8 0.2 shard_map.95
  15.0 3.4 %shard_map.96._.local = f32[512,128]{1,0:T(8,128)S(1)} custom-call(s32[2,64]{1,0:T(2,128)S(1)} %get-tuple-element.28.pairs, f32[520,128]{1,0:T(8,128)S(1)} %get-tuple-element.16.state), custom_call_target="tpu_custom_call" | custom-call | flops 26214400 | bytes 1048576 | tf_op jit(solution)/shard_map/pallas_call | solution.py:259
  18.4 5.8 %all-to-all-done = s32[128,1,128]{2,1,0:T(1,128)S(1)} async-done(((s32[128,1,128]{2,1,0:T(1,128)}), s32[128,1,128]{2,1,0:T(1,128)S(1)}, u32[]{:S(2)}, u32[]{:S(2)}) %all-to-all-start) | async-done | bytes 65568 | tf_op jit(solution)/shard_map/all_to_all | solution.py:279
  24.2 1.5 %shard_map.97 = (f32[2048,128]{1,0:T(8,128)S(1)}, s32[8,128]{1,0:T(8,128)S(1)}) custom-call(s32[128,128]{1,0:T(8,128)S(1)} %bitcast.28, f32[520,128]{1,0:T(8,128)S(1)} %get-tuple-element.16.state, f32[512,128]{1,0:T(8,128)S(1)} %shard_map.96._.local), custom_call_target="tpu_custom_call" | custom-call | flops 65536 | bytes 2097152 | tf_op jit(solution)/shard_map/pallas_call | solution.py:259
  25.7 23.8 %all_to_all.25 = f32[128,16,128]{2,1,0:T(8,128)S(1)} all-to-all(f32[128,16,128]{2,1,0:T(8,128)S(1)} %bitcast.27), channel_id=1, replica_groups=mesh['gx'=4,'gy'=4,'gz'=8] {'gx','gy','gz'}, dimensions={0} | all-to-all | bytes 2097152 | tf_op jit(solution)/shard_map/all_to_all | solution.py:279
  49.4 5.4 %shard_map.98 = f32[1536,128]{1,0:T(8,128)S(1)} custom-call(s32[2,128]{1,0:T(2,128)S(1)} %get-tuple-element.19.places, f32[2048,128]{1,0:T(8,128)S(1)} %bitcast.22), custom_call_target="tpu_custom_call" | custom-call | flops 52428800 | bytes 2097152 | tf_op jit(solution)/shard_map/pallas_call | solution.py:259
  54.9 0.0 copy-start.1
  54.9 20.7 %all_to_all.26 = f32[128,3,4,128]{3,2,1,0:T(4,128)S(1)} all-to-all(f32[128,3,4,128]{3,2,1,0:T(4,128)S(1)} %bitcast.25), channel_id=1, replica_groups=mesh['gx'=4,'gy'=4,'gz'=8] {'gx','gy','gz'}, dimensions={0} | all-to-all | bytes 1572864 | tf_op jit(solution)/shard_map/all_to_all | solution.py:279
  75.5 0.0 copy-done.1
  75.5 1.5 %shard_map.99 = (f32[2048,128]{1,0:T(8,128)S(1)}, f32[520,128]{1,0:T(8,128)S(1)}, f32[192,128]{1,0:T(8,128)S(1)}, f32[192,128]{1,0:T(8,128)S(1)}) custom-call(s32[8,128]{1,0:T(8,128)S(1)} %get-tuple-element.17.asked, f32[1536,128]{1,0:T(8,128)S(1)} %bitcast.24, f32[512,128]{1,0:T(8,128)S(1)} %shard_map.96._.local, f32[64,128]{1,0:T(8,128)S(1)} %bitcast.30, ...), custom_call_target="tpu_custom_call" | custom-call | flops 65536 | bytes 4194304 | tf_op jit(solution)/shard_map/pallas_call | solution.py:259
  77.0 23.6 %all_to_all.27 = f32[128,16,128]{2,1,0:T(8,128)S(1)} all-to-all(f32[128,16,128]{2,1,0:T(8,128)S(1)} %bitcast.26), channel_id=1, replica_groups=mesh['gx'=4,'gy'=4,'gz'=8] {'gx','gy','gz'}, dimensions={0} | all-to-all | bytes 2097152 | tf_op jit(solution)/shard_map/all_to_all | solution.py:279
  100.6 6.3 %shard_map.100 = f32[1536,128]{1,0:T(8,128)} custom-call(s32[2,128]{1,0:T(2,128)S(1)} %get-tuple-element.18.places, f32[2048,128]{1,0:T(8,128)S(1)} %bitcast.21), custom_call_target="tpu_custom_call" | custom-call | flops 52428800 | bytes 2097152 | tf_op jit(solution)/shard_map/pallas_call | solution.py:259
  106.9 4.3 %all-to-all-start.4 = ((f32[128,3,4,128]{3,2,1,0:T(4,128)}), f32[128,3,4,128]{3,2,1,0:T(4,128)S(1)}, u32[]{:S(2)}, u32[]{:S(2)}) async-start(f32[128,3,4,128]{3,2,1,0:T(4,128)} %bitcast.15), calls=%async_computation.4 | async-start | bytes 1572864 | tf_op jit(solution)/shard_map/all_to_all | solution.py:279
  111.3 3.4 %shard_map.101.local = f32[512,128]{1,0:T(8,128)S(1)} custom-call(s32[2,64]{1,0:T(2,128)S(1)} %get-tuple-element.27.pairs, f32[520,128]{1,0:T(8,128)S(1)} %get-tuple-element.24.state), custom_call_target="tpu_custom_call" | custom-call | flops 26214400 | bytes 1048576 | tf_op jit(solution)/shard_map/pallas_call | solution.py:259
  114.7 13.3 %all-to-all-done.4 = f32[128,3,4,128]{3,2,1,0:T(4,128)S(1)} async-done(((f32[128,3,4,128]{3,2,1,0:T(4,128)}), f32[128,3,4,128]{3,2,1,0:T(4,128)S(1)}, u32[]{:S(2)}, u32[]{:S(2)}) %all-to-all-start.4) | async-done | bytes 786464 | tf_op jit(solution)/shard_map/all_to_all | solution.py:279
  127.9 1.4 %shard_map.102 = (f32[3,8192]{1,0:T(4,128)}, f32[3,8192]{1,0:T(4,128)}, f32[3,8192]{1,0:T(4,128)}) custom-call(s32[8,128]{1,0:T(8,128)S(1)} %get-tuple-element.17.asked, f32[1536,128]{1,0:T(8,128)S(1)} %bitcast.23, f32[512,128]{1,0:T(8,128)S(1)} %shard_map.101.local, f32[192,128]{1,0:T(8,128)S(1)} %get-tuple-element.25.where, ...), custom_call_target="tpu_custom_call" | custom-call | flops 65536 | bytes 4194304 | tf_op jit(solution)/shard_map/pallas_call | solution.py:259
  (1 shorter events, 0.0 us)
Async XLA Ops:
  0.6 0.7 copy-start.4
  1.3 0.7 copy-start.5
  2.0 12.8 %copy-start.2 = (f32[3,8192]{1,0:T(4,128)S(1)}, f32[3,8192]{1,0:T(4,128)}, u32[]{:S(2)}) copy-start(f32[3,8192]{1,0:T(4,128)} %positions.1) | copy-start | bytes 294916
  2.0 12.8 %copy-start.3 = (f32[3,8192]{1,0:T(4,128)S(1)}, f32[3,8192]{1,0:T(4,128)}, u32[]{:S(2)}) copy-start(f32[3,8192]{1,0:T(4,128)} %velocities.1) | copy-start | bytes 294916
  3.2 11.5 %copy-start.6 = (s32[2,64,2]{1,2,0:T(2,128)S(1)}, s32[2,64,2]{1,2,0:T(2,128)}, u32[]{:S(2)}) copy-start(s32[2,64,2]{1,2,0:T(2,128)} %param.13) | copy-start | bytes 3076
  3.2 11.6 %copy-start = (f32[8192]{0:T(1024)S(1)}, f32[8192]{0:T(1024)}, u32[]{:S(2)}) copy-start(f32[8192]{0:T(1024)} %param.9) | copy-start | bytes 98308
  3.2 20.9 %all-to-all-start = ((s32[128,1,128]{2,1,0:T(1,128)}), s32[128,1,128]{2,1,0:T(1,128)S(1)}, u32[]{:S(2)}, u32[]{:S(2)}) async-start(s32[128,1,128]{2,1,0:T(1,128)} %bitcast.3), calls=%async_computation | async-start | bytes 131072 | tf_op jit(solution)/shard_map/all_to_all | solution.py:279
  54.9 20.7 %copy-start.1 = (s32[8192]{0:T(1024)S(1)}, s32[8192]{0:T(1024)}, u32[]{:S(2)}) copy-start(s32[8192]{0:T(1024)} %param.10) | copy-start | bytes 98308
  106.9 21.0 %all-to-all-start.4 = ((f32[128,3,4,128]{3,2,1,0:T(4,128)}), f32[128,3,4,128]{3,2,1,0:T(4,128)S(1)}, u32[]{:S(2)}, u32[]{:S(2)}) async-start(f32[128,3,4,128]{3,2,1,0:T(4,128)} %bitcast.15), calls=%async_computation.4 | async-start | bytes 1572864 | tf_op jit(solution)/shard_map/all_to_all | solution.py:279

commit v4 on v3

--- a/solution.py
+++ b/solution.py
@@ -1,3 +1,5 @@
+import functools
+
 import jax
 import jax.numpy as jnp
 from jax import lax
@@ -89,16 +91,16 @@
 
 
 def pair_forces(tiles, row):
-    count, lag = len(tiles), 4
+    count = len(tiles)
     parts, dists, sums, out = {}, {}, {}, []
-    for step in range(count + 2 * lag):
+    for step in range(count + 10):
         if step < count:
             parts[step] = pair_parts(tiles[step], row)
             dists[step] = softened_distances(parts[step][1], parts[step][2], row)
-        k = step - lag
+        k = step - 6
         if 0 <= k < count:
             sums[k] = moments(parts[k][3], pair_kernel(dists[k]))
-        k = step - 2 * lag
+        k = step - 10
         if k >= 0:
             out.append(force_tile(sums[k], parts[k][0], row))
     return out
@@ -112,21 +114,16 @@
     return state[pl.ds(pl.multiple_of(leaf * 8, 8), 8), :]
 
 
-def fill_slots(first, asked, state, looked):
-    row = row_iota()
-
-    def body(step, carry):
-        for u in range(8):
-            worker = step * 8 + u
-            for half in range(2):
-                left = leaf_tile(state, asked[first + 2 * half, worker])
-                right = leaf_tile(state, asked[first + 2 * half + 1, worker])
-                looked[pl.ds(pl.multiple_of(worker * 16 + half * 8, 8), 8), :] = jnp.where(
-                    row < 4, left, right
-                )
-        return carry
-
-    lax.fori_loop(0, DEVICES // 8, body, 0)
+def fill_slots(first, wanted, leaves, looked):
+    parts = jnp.concatenate([part.astype(BF16) for part in split3(leaves)], axis=0)
+    leaf = lax.broadcasted_iota(jnp.int32, (DEVICES, 3 * NLEAF), 1) & (NLEAF - 1)
+    for turn in range(CAP):
+        chosen = jnp.where(leaf == wanted[:, first + turn : first + turn + 1], 1.0, 0.0)
+        found = lax.dot_general(chosen.astype(BF16), parts, NN, preferred_element_type=F32)
+        for index in range(4):
+            looked[pl.ds(4 * turn + index, DEVICES, stride=4 * CAP), :] = found[
+                :, index * LEAF : (index + 1) * LEAF
+            ]
 
 
 def component(index):
@@ -138,7 +135,9 @@
     state[pl.ds(index + 4, NLEAF, stride=8), :] = value
 
 
-def pack_kernel(positions, velocities, masses, state, where, moving):
+def pack_kernel(positions, velocities, masses, places0, places1, state, where, moving, placed0, placed1):
+    placed0[...] = places0[...]
+    placed1[...] = places1[...]
     for leaf in range(NLEAF):
         lanes = slice(leaf * LEAF, (leaf + 1) * LEAF)
         where[pl.ds(leaf, 3, stride=NLEAF), :] = positions[:, lanes]
@@ -146,15 +145,12 @@
     for index in range(3):
         store_state(state, index, where[component(index), :])
     store_state(state, 3, masses[...])
-    state[8 * NLEAF :, :] = jnp.zeros((8, LEAF), F32)
-
-
-def gather_kernel(wanted, state, _, looked, asked, scalars, sem):
+
+
+def gather_kernel(wanted, where, masses, _, looked, asked):
     asked[...] = wanted[...].T[: 2 * CAP]
-    copy = pltpu.make_async_copy(asked, scalars, sem)
-    copy.start()
-    copy.wait()
-    fill_slots(0, scalars, state, looked)
+    leaves = [where[component(index), :] for index in range(3)] + [masses[...]]
+    fill_slots(0, wanted, jnp.concatenate(leaves, axis=1), looked)
 
 
 def local_kernel(pairs, state, forces):
@@ -178,7 +174,8 @@
     lax.fori_loop(0, LOCAL // unroll, body, 0)
 
 
-def remote_kernel(places, arrived, pushed, placed, sem):
+def remote_kernel(unused, places, arrived, *refs):
+    pushed, placed, sem = refs[unused:]
     row = row_iota()
     copy = pltpu.make_async_copy(places, placed, sem)
     copy.start()
@@ -231,18 +228,17 @@
 
 
 def advance_kernel(
-    asked, returned, local, masses, where, moving, bins, looked, state, new_where, new_moving, scalars, sem
+    wanted, asked, returned, local, masses, where, moving, bins, looked, state, new_where, new_moving
 ):
-    copy = pltpu.make_async_copy(asked, scalars, sem)
-    copy.start()
-    store_state(state, 3, masses[...])
-    state[8 * NLEAF :, :] = jnp.zeros((8, LEAF), F32)
+    leaves = []
     for index, _, velocity, position in kick_drift(0, asked, returned, local, where, moving, bins):
         new_moving[component(index), :] = velocity
         new_where[component(index), :] = position
         store_state(state, index, position)
-    copy.wait()
-    fill_slots(CAP, scalars, state, looked)
+        leaves.append(position)
+    leaves.append(masses[...])
+    fill_slots(CAP, wanted, jnp.concatenate(leaves, axis=1), looked)
+    store_state(state, 3, masses[...])
 
 
 def finish_kernel(asked, returned, local, where, moving, bins, positions, velocities, accels, rows):
@@ -255,7 +251,9 @@
             out[:, lanes] = rows[number, pl.ds(leaf, 3, stride=NLEAF), :]
 
 
-def call(kernel, out_shapes, arrays, flops, size, scratch=(), in_specs=None, scalars=()):
+def call(
+    kernel, out_shapes, arrays, flops, size, scratch=(), in_specs=None, scalars=(), vmem=40 * 2**20
+):
     return pl.pallas_call(
         kernel,
         out_shape=out_shapes,
@@ -266,7 +264,7 @@
             out_specs=jax.tree.map(lambda _: VMEM, out_shapes),
             scratch_shapes=scratch,
         ),
-        compiler_params=pltpu.CompilerParams(vmem_limit_bytes=40 * 2**20),
+        compiler_params=pltpu.CompilerParams(vmem_limit_bytes=vmem),
         cost_estimate=pl.CostEstimate(flops=flops, bytes_accessed=size, transcendentals=0),
     )(*scalars, *arrays)
 
@@ -325,8 +323,7 @@
     masses = masses.reshape(NLEAF, LEAF)
     bins = time_bins.reshape(NLEAF, LEAF)
     local_ids = local_pairs.transpose(0, 2, 1)
-    state_shape = shape(8 * (NLEAF + 1), LEAF)
-    local_shape = shape(8 * NLEAF, LEAF)
+    tiles_shape = shape(8 * NLEAF, LEAF)
     rows_shape = shape(3 * NLEAF, LEAF)
     looked_shape = shape(4 * SLOTS, LEAF)
     pushed_shape = shape(3 * SLOTS, LEAF)
@@ -334,15 +331,21 @@
     ends_shape = shape(2, PAIRS, dtype=jnp.int32)
     anywhere = pl.BlockSpec(memory_space=pl.ANY)
     dma = pltpu.SemaphoreType.DMA
-    asked_scratch = [pltpu.SMEM((2 * CAP, DEVICES), jnp.int32), dma(())]
 
     def local_forces(ids, state):
-        return call(local_kernel, local_shape, [state], 64 * 2**14 * 25, 2**20, scalars=[ids])
-
-    def remote_forces(places, arrived):
+        return call(local_kernel, tiles_shape, [state], 64 * 2**14 * 25, 2**20, scalars=[ids])
+
+    def remote_forces(places, arrived, *earlier):
         scratch = [pltpu.SMEM((2, PAIRS), jnp.int32), dma(())]
+        specs = [VMEM] * 2 + [anywhere] * len(earlier)
         return call(
-            remote_kernel, pushed_shape, [places, arrived], 128 * 2**14 * 25, 2**21, scratch
+            functools.partial(remote_kernel, len(earlier)),
+            pushed_shape,
+            [places, arrived, *earlier],
+            128 * 2**14 * 25,
+            2**21,
+            scratch,
+            specs,
         )
 
     *placed, wanted = call(
@@ -353,12 +356,13 @@
         2**18,
         [pltpu.VMEM((2, 2, PAIRS), jnp.int32), pltpu.VMEM((2, 2, PAIRS), jnp.int32), dma((2,))],
         [pl.BlockSpec(memory_space=pltpu.HBM)] * 2,
+        vmem=60 * 2**20,
     )
     wanted = exchange(wanted.reshape(DEVICES, 1, LEAF)).reshape(DEVICES, LEAF)
-    state, where, moving = call(
+    state, where, moving, *placed = call(
         pack_kernel,
-        (state_shape, rows_shape, rows_shape),
-        [positions, velocities, masses],
+        (tiles_shape, rows_shape, rows_shape, ends_shape, ends_shape),
+        [positions, velocities, masses, *placed],
         2**16,
         2**20,
     )
@@ -366,24 +370,22 @@
     looked, asked = call(
         gather_kernel,
         (looked_shape, asked_shape),
-        [wanted, state, local],
+        [wanted, where, masses, local],
         2**16,
         2**21,
-        asked_scratch,
-        [VMEM, VMEM, anywhere],
+        in_specs=[VMEM, VMEM, VMEM, anywhere],
     )
     pushed = remote_forces(placed[0], send_leaves(looked))
     returned = send_forces(pushed)
     looked, state, where, moving = call(
         advance_kernel,
-        (looked_shape, state_shape, rows_shape, rows_shape),
-        [asked, returned, local, masses, where, moving, bins],
+        (looked_shape, tiles_shape, rows_shape, rows_shape),
+        [wanted, asked, returned, local, masses, where, moving, bins],
         2**16,
         2**22,
-        asked_scratch,
     )
     local = local_forces(local_ids[1], state)
-    pushed = remote_forces(placed[1], send_leaves(looked))
+    pushed = remote_forces(placed[1], send_leaves(looked), local)
     returned = send_forces(pushed)
     out = shape(3, NLEAF * LEAF)
     return call(

time: 130 us -> 127 us (0.977)
  blocking collectives: 68 us -> 65.1 us
  waiting for transfers between devices: 19.1 us -> 21.3 us
  Pallas kernels: 24.2 us -> 22.9 us
    all_to_all x3, blocking collectives: 68 us -> 65.1 us  [exchange(): return lax.all_to_all(array, AXES, split_axis=0, concat_axis=0, tiled=True)]
    all_to_all x2, waiting for transfers between devices: 19.1 us -> 21.3 us  [exchange(): return lax.all_to_all(array, AXES, split_axis=0, concat_axis=0, tiled=True)]
where the time goes in v4:
time: 127 us
  blocking collectives  65.1 us (51%)
  Pallas kernels  22.9 us (18%)
  waiting for transfers between devices  21.3 us (17%)
  starting transfers between devices  15.9 us (13%)
    all_to_all x3, blocking collectives, exchange(): return lax.all_to_all(array, AXES, split_axis=0, concat_axis=0, tiled=True)  65.1 us
    pallas_call x9, Pallas kernels, call(): pl.pallas_call(kernel, out_shape=out_shapes, grid_spec=pltpu.PrefetchScal...  22.9 us
    all_to_all x2, waiting for transfers between devices, exchange(): return lax.all_to_all(array, AXES, split_axis=0, concat_axis=0, tiled=True)  21.3 us
    all_to_all x2, starting transfers between devices, exchange(): return lax.all_to_all(array, AXES, split_axis=0, concat_axis=0, tiled=True)  15.9 us
  transfers between devices with their start and end apart: 2, of which 2 were waited for; matrix products, arithmetic and copies ran while one was open for 0% of the time, Pallas kernels for 5%

profile of v4, /device:TPU:1, one launch (start us, length us, event | category | flops | bytes accessed | tf_op | source)
XLA Modules:
  0.0 126.7 jit_solution(3990500086044156358)
XLA Ops:
  0.6 0.0 copy-start.2
  0.6 0.0 copy-start.3
  0.7 1.9 %shard_map.94 = (s32[2,128]{1,0:T(2,128)}, s32[2,128]{1,0:T(2,128)}, s32[128,128]{1,0:T(8,128)}) custom-call(s32[2,2,128]{2,1,0:T(2,128)} %bitcast.37, s32[2,2,128]{2,1,0:T(2,128)} %bitcast.38), custom_call_target="tpu_custom_call" | custom-call | flops 67108864 | bytes 262144 | tf_op jit(solution)/shard_map/pallas_call | solution.py:257
  2.6 0.0 copy-start.6
  2.6 0.0 copy-start
  2.6 11.5 %all-to-all-start = ((s32[128,1,128]{2,1,0:T(1,128)}), s32[128,1,128]{2,1,0:T(1,128)S(1)}, u32[]{:S(2)}, u32[]{:S(2)}) async-start(s32[128,1,128]{2,1,0:T(1,128)} %bitcast.35), calls=%async_computation | async-start | bytes 131072 | tf_op jit(solution)/shard_map/all_to_all | solution.py:277
  14.1 0.0 copy-done.6
  14.2 0.0 copy-start.5
  14.2 0.0 copy-start.4
  14.2 0.0 copy-done.2
  14.2 0.0 copy-done.3
  14.2 0.0 copy-done
  14.2 0.6 copy-done.5
  14.8 0.0 copy-done.4
  14.9 0.2 shard_map.95
  15.0 3.3 %shard_map.96._.local = f32[512,128]{1,0:T(8,128)S(1)} custom-call(s32[2,64]{1,0:T(2,128)S(1)} %get-tuple-element.32.pairs, f32[512,128]{1,0:T(8,128)S(1)} %get-tuple-element.21.state), custom_call_target="tpu_custom_call" | custom-call | flops 26214400 | bytes 1048576 | tf_op jit(solution)/shard_map/pallas_call | solution.py:257
  18.3 5.3 %all-to-all-done = s32[128,1,128]{2,1,0:T(1,128)S(1)} async-done(((s32[128,1,128]{2,1,0:T(1,128)}), s32[128,1,128]{2,1,0:T(1,128)S(1)}, u32[]{:S(2)}, u32[]{:S(2)}) %all-to-all-start) | async-done | bytes 65568 | tf_op jit(solution)/shard_map/all_to_all | solution.py:277
  23.6 0.5 shard_map.97
  24.1 23.8 %all_to_all.25 = f32[128,16,128]{2,1,0:T(8,128)S(1)} all-to-all(f32[128,16,128]{2,1,0:T(8,128)S(1)} %bitcast.27), channel_id=1, replica_groups=mesh['gx'=4,'gy'=4,'gz'=8] {'gx','gy','gz'}, dimensions={0} | all-to-all | bytes 2097152 | tf_op jit(solution)/shard_map/all_to_all | solution.py:277
  47.8 5.2 %shard_map.98 = f32[1536,128]{1,0:T(8,128)S(1)} custom-call(s32[2,128]{1,0:T(2,128)S(1)} %get-tuple-element.24.places, f32[2048,128]{1,0:T(8,128)S(1)} %bitcast.21), custom_call_target="tpu_custom_call" | custom-call | flops 52428800 | bytes 2097152 | tf_op jit(solution)/shard_map/pallas_call | solution.py:257
  53.1 0.0 copy-start.1
  53.1 20.7 %all_to_all.26 = f32[128,3,4,128]{3,2,1,0:T(4,128)S(1)} all-to-all(f32[128,3,4,128]{3,2,1,0:T(4,128)S(1)} %bitcast.24), channel_id=1, replica_groups=mesh['gx'=4,'gy'=4,'gz'=8] {'gx','gy','gz'}, dimensions={0} | all-to-all | bytes 1572864 | tf_op jit(solution)/shard_map/all_to_all | solution.py:277
  73.8 0.0 copy-done.1
  73.8 1.9 %shard_map.99 = (f32[2048,128]{1,0:T(8,128)}, f32[512,128]{1,0:T(8,128)S(1)}, f32[192,128]{1,0:T(8,128)S(1)}, f32[192,128]{1,0:T(8,128)S(1)}) custom-call(s32[128,128]{1,0:T(8,128)S(1)} %bitcast.29, s32[8,128]{1,0:T(8,128)S(1)} %get-tuple-element.22.asked, f32[1536,128]{1,0:T(8,128)S(1)} %bitcast.25, f32[512,128]{1,0:T(8,128)S(1)} %shard_map.96._.local, ...), custom_call_target="tpu_custom_call" | custom-call | flops 65536 | bytes 4194304 | tf_op jit(solution)/shard_map/pallas_call | solution.py:257
  75.7 4.4 %all-to-all-start.3 = ((f32[128,16,128]{2,1,0:T(8,128)}), f32[128,16,128]{2,1,0:T(8,128)S(1)}, u32[]{:S(2)}, u32[]{:S(2)}) async-start(f32[128,16,128]{2,1,0:T(8,128)} %bitcast.13), calls=%async_computation.3 | async-start | bytes 2097152 | tf_op jit(solution)/shard_map/all_to_all | solution.py:277
  80.1 3.3 %shard_map.100.refs_0_.local = f32[512,128]{1,0:T(8,128)S(1)} custom-call(s32[2,64]{1,0:T(2,128)S(1)} %get-tuple-element.31.pairs, f32[512,128]{1,0:T(8,128)S(1)} %get-tuple-element.28.state), custom_call_target="tpu_custom_call" | custom-call | flops 26214400 | bytes 1048576 | tf_op jit(solution)/shard_map/pallas_call | solution.py:257
  83.4 16.0 %all-to-all-done.3 = f32[128,16,128]{2,1,0:T(8,128)S(1)} async-done(((f32[128,16,128]{2,1,0:T(8,128)}), f32[128,16,128]{2,1,0:T(8,128)S(1)}, u32[]{:S(2)}, u32[]{:S(2)}) %all-to-all-start.3) | async-done | bytes 1048608 | tf_op jit(solution)/shard_map/all_to_all | solution.py:277
  99.5 5.2 %shard_map.101 = f32[1536,128]{1,0:T(8,128)S(1)} custom-call(s32[2,128]{1,0:T(2,128)S(1)} %get-tuple-element.23.places, f32[2048,128]{1,0:T(8,128)S(1)} %bitcast.22, f32[512,128]{1,0:T(8,128)S(1)} %shard_map.100.refs_0_.local), custom_call_target="tpu_custom_call" | custom-call | flops 52428800 | bytes 2097152 | tf_op jit(solution)/shard_map/pallas_call | solution.py:257
  104.7 20.7 %all_to_all.27 = f32[128,3,4,128]{3,2,1,0:T(4,128)S(1)} all-to-all(f32[128,3,4,128]{3,2,1,0:T(4,128)S(1)} %bitcast.26), channel_id=1, replica_groups=mesh['gx'=4,'gy'=4,'gz'=8] {'gx','gy','gz'}, dimensions={0} | all-to-all | bytes 1572864 | tf_op jit(solution)/shard_map/all_to_all | solution.py:277
  125.4 1.4 %shard_map.102 = (f32[3,8192]{1,0:T(4,128)}, f32[3,8192]{1,0:T(4,128)}, f32[3,8192]{1,0:T(4,128)}) custom-call(s32[8,128]{1,0:T(8,128)S(1)} %get-tuple-element.22.asked, f32[1536,128]{1,0:T(8,128)S(1)} %bitcast.23, f32[512,128]{1,0:T(8,128)S(1)} %shard_map.100.refs_0_.local, f32[192,128]{1,0:T(8,128)S(1)} %get-tuple-element.29.where, ...), custom_call_target="tpu_custom_call" | custom-call | flops 65536 | bytes 4194304 | tf_op jit(solution)/shard_map/pallas_call | solution.py:257
  (1 shorter events, 0.0 us)
Async XLA Ops:
  0.6 13.6 %copy-start.2 = (f32[3,8192]{1,0:T(4,128)S(1)}, f32[3,8192]{1,0:T(4,128)}, u32[]{:S(2)}) copy-start(f32[3,8192]{1,0:T(4,128)} %positions.1) | copy-start | bytes 294916
  0.6 13.6 %copy-start.3 = (f32[3,8192]{1,0:T(4,128)S(1)}, f32[3,8192]{1,0:T(4,128)}, u32[]{:S(2)}) copy-start(f32[3,8192]{1,0:T(4,128)} %velocities.1) | copy-start | bytes 294916
  2.6 11.5 %copy-start.6 = (s32[2,64,2]{1,2,0:T(2,128)S(1)}, s32[2,64,2]{1,2,0:T(2,128)}, u32[]{:S(2)}) copy-start(s32[2,64,2]{1,2,0:T(2,128)} %param.13) | copy-start | bytes 3076
  2.6 11.6 %copy-start = (f32[8192]{0:T(1024)S(1)}, f32[8192]{0:T(1024)}, u32[]{:S(2)}) copy-start(f32[8192]{0:T(1024)} %param.9) | copy-start | bytes 98308
  2.6 20.9 %all-to-all-start = ((s32[128,1,128]{2,1,0:T(1,128)}), s32[128,1,128]{2,1,0:T(1,128)S(1)}, u32[]{:S(2)}, u32[]{:S(2)}) async-start(s32[128,1,128]{2,1,0:T(1,128)} %bitcast.35), calls=%async_computation | async-start | bytes 131072 | tf_op jit(solution)/shard_map/all_to_all | solution.py:277
  14.2 0.7 copy-start.5
  14.2 0.7 copy-start.4
  53.1 20.7 %copy-start.1 = (s32[8192]{0:T(1024)S(1)}, s32[8192]{0:T(1024)}, u32[]{:S(2)}) copy-start(s32[8192]{0:T(1024)} %param.10) | copy-start | bytes 98308
  75.7 23.8 %all-to-all-start.3 = ((f32[128,16,128]{2,1,0:T(8,128)}), f32[128,16,128]{2,1,0:T(8,128)S(1)}, u32[]{:S(2)}, u32[]{:S(2)}) async-start(f32[128,16,128]{2,1,0:T(8,128)} %bitcast.13), calls=%async_computation.3 | async-start | bytes 2097152 | tf_op jit(solution)/shard_map/all_to_all | solution.py:277

commit v5 on v4

--- a/solution.py
+++ b/solution.py
@@ -135,7 +135,10 @@
     state[pl.ds(index + 4, NLEAF, stride=8), :] = value
 
 
-def pack_kernel(positions, velocities, masses, places0, places1, state, where, moving, placed0, placed1):
+def pack_kernel(
+    positions, velocities, masses, bins, places0, places1,
+    state, where, moving, placed0, placed1, order, ordered,
+):
     placed0[...] = places0[...]
     placed1[...] = places1[...]
     for leaf in range(NLEAF):
@@ -145,11 +148,43 @@
     for index in range(3):
         store_state(state, index, where[component(index), :])
     store_state(state, 3, masses[...])
-
-
-def gather_kernel(wanted, where, masses, _, looked, asked):
+    kicked = jnp.where(bins[...] >= 3, 1.0, 0.0)
+    earlier = lax.broadcasted_iota(jnp.int32, (LEAF, LEAF), 0) < lax.broadcasted_iota(
+        jnp.int32, (LEAF, LEAF), 1
+    )
+    before = lax.dot_general(
+        kicked.astype(BF16), jnp.where(earlier, 1.0, 0.0).astype(BF16), NN, preferred_element_type=F32
+    )
+    lane = lax.broadcasted_iota(jnp.int32, (NLEAF, LEAF), 1).astype(F32)
+    last = jnp.sum(kicked, axis=1, keepdims=True) + lane - before
+    order[...] = jnp.where(kicked > 0.0, before, last).astype(jnp.int32)
+
+    def body(step, carry):
+        for u in range(8):
+            leaf = step * 8 + u
+            moved = lax.dot_general(
+                stacked(split3(leaf_tile(state, leaf))), lanes_of(order, leaf, LEAF), NT,
+                preferred_element_type=F32,
+            )
+            ordered[pl.ds(pl.multiple_of(leaf * 8, 8), 8), :] = moved[0:8] + moved[8:16] + moved[16:24]
+        return carry
+
+    lax.fori_loop(0, NLEAF // 8, body, 0)
+
+
+def stacked(parts):
+    return jnp.concatenate([*parts, jnp.zeros_like(parts[0])], axis=0).astype(BF16)
+
+
+def lanes_of(order, leaf, count):
+    lane = lax.broadcasted_iota(jnp.int32, (count, LEAF), 0)
+    return jnp.where(lane == order[pl.ds(leaf, 1), :], 1.0, 0.0).astype(BF16)
+
+
+def gather_kernel(wanted, ordered, looked, asked, most):
     asked[...] = wanted[...].T[: 2 * CAP]
-    leaves = [where[component(index), :] for index in range(3)] + [masses[...]]
+    most[...] = jnp.max(wanted[:, 2 * CAP : 2 * CAP + 1], axis=0, keepdims=True)
+    leaves = [ordered[pl.ds(index, NLEAF, stride=8), :] for index in range(4)]
     fill_slots(0, wanted, jnp.concatenate(leaves, axis=1), looked)
 
 
@@ -174,12 +209,13 @@
     lax.fori_loop(0, LOCAL // unroll, body, 0)
 
 
-def remote_kernel(unused, places, arrived, *refs):
-    pushed, placed, sem = refs[unused:]
+def remote_kernel(unused, half, places, arrived, *refs):
+    pushed, placed, sem, *apart = refs[unused:]
+    forces = apart[0] if half else pushed
     row = row_iota()
     copy = pltpu.make_async_copy(places, placed, sem)
     copy.start()
-    pushed[...] = jnp.zeros_like(pushed)
+    forces[...] = jnp.zeros_like(forces)
     copy.wait()
     unroll = 64
 
@@ -194,44 +230,86 @@
         ]
         found = pair_forces([jnp.where(row < 4, leaf(a, 0), leaf(b, 1)) for a, b in ids], row)
         for (a, b), force in zip(ids, found):
-            pushed[pl.ds(3 * a, 3), :] = force[4:7]
-            pushed[pl.ds(3 * b, 3), :] = force[0:3]
+            for slot, first in ((a, 4), (b, 0)):
+                at = 3 * ((slot >> 1) + (slot & 1) * (SLOTS // 2)) if half else 3 * slot
+                forces[pl.ds(at, 3), :] = force[first : first + 3]
         return carry
 
     lax.fori_loop(0, PAIRS // unroll, body, 0)
-
-
-def summed(first, asked, returned):
+    if half:
+        rows = pushed.shape[0]
+        lower = lax.broadcasted_iota(jnp.int32, (rows, LEAF), 1) < LEAF // 2
+        odd = pltpu.roll(forces[rows:, :], LEAF // 2, 1)
+        pushed[...] = jnp.where(lower, forces[:rows, :], odd)
+
+
+def summed(first, half, asked, returned):
     target = lax.broadcasted_iota(jnp.int32, (NLEAF, DEVICES), 0)
-    chosen, blocks = [], []
-    for turn in range(CAP):
-        chosen.append(jnp.where(target == asked[first + turn : first + turn + 1, :], 1.0, 0.0))
-        rows = [
-            returned[pl.ds(3 * turn + index, DEVICES, stride=3 * CAP), :] for index in range(3)
-        ]
-        blocks.append(jnp.concatenate(rows, axis=1))
-    chosen = jnp.concatenate(chosen, axis=1).astype(BF16)
-    total = jnp.zeros((NLEAF, 3 * LEAF), F32)
+    chosen = [
+        jnp.where(target == asked[first + turn : first + turn + 1, :], 1.0, 0.0) for turn in range(CAP)
+    ]
+    groups = CAP // 2 if half else CAP
+    blocks = [
+        jnp.concatenate(
+            [returned[pl.ds(3 * group + index, DEVICES, stride=3 * groups), :] for index in range(3)],
+            axis=1,
+        )
+        for group in range(groups)
+    ]
+    if half:
+        even, odd = (jnp.concatenate(chosen[part::2], axis=1) for part in range(2))
+        chosen = jnp.concatenate([even, odd], axis=0).astype(BF16)
+    else:
+        chosen = jnp.concatenate(chosen, axis=1).astype(BF16)
+    total = jnp.zeros((chosen.shape[0], 3 * LEAF), F32)
     for part in split3(jnp.concatenate(blocks, axis=0)):
         total += lax.dot_general(chosen, part.astype(BF16), NN, preferred_element_type=F32)
-    return total
-
-
-def kick_drift(subcycle, asked, returned, local, where, moving, bins):
-    total = summed(CAP * subcycle, asked, returned)
-    active = bins[...] >= 3 - subcycle
-    for index in range(3):
-        accel = total[:, index * LEAF : (index + 1) * LEAF]
+    totals = [total[:, index * LEAF : (index + 1) * LEAF] for index in range(3)]
+    if half:
+        lower = lax.broadcasted_iota(jnp.int32, (NLEAF, LEAF), 1) < LEAF // 2
+        totals = [
+            jnp.where(lower, one[:NLEAF] + pltpu.roll(one[NLEAF:], LEAF // 2, 1), 0.0) for one in totals
+        ]
+    return totals
+
+
+def disordered(totals, half, order, rows, spread):
+    rows[...] = jnp.zeros_like(rows)
+    for index, total in enumerate(totals):
+        for number, part in enumerate(split3(total)):
+            rows[number, component(index), :] = part
+    count = LEAF // 2 if half else LEAF
+
+    def body(step, carry):
+        for u in range(32):
+            leaf = step * 32 + u
+            parts = [rows[number, pl.ds(leaf, 8, stride=NLEAF), :] for number in range(3)]
+            moved = lax.dot_general(
+                stacked(parts)[:, :count], lanes_of(order, leaf, count), NN, preferred_element_type=F32
+            )
+            moved = moved[0:8] + moved[8:16] + moved[16:24]
+            spread[pl.ds(leaf, 3, stride=NLEAF), :] = moved[0:3]
+        return carry
+
+    lax.fori_loop(0, NLEAF // 32, body, 0)
+    return [spread[component(index), :] for index in range(3)]
+
+
+def kick_drift(threshold, totals, local, where, moving, bins):
+    active = bins[...] >= threshold
+    for index, accel in enumerate(totals):
         accel += local[pl.ds(index, NLEAF, stride=8), :] + local[pl.ds(index + 4, NLEAF, stride=8), :]
         velocity = moving[component(index), :] + jnp.where(active, TIME_STEP * accel, 0.0)
         yield index, accel, velocity, where[component(index), :] + TIME_STEP * velocity
 
 
 def advance_kernel(
-    wanted, asked, returned, local, masses, where, moving, bins, looked, state, new_where, new_moving
+    half, wanted, asked, returned, local, masses, where, moving, bins, order,
+    looked, state, new_where, new_moving, rows, spread,
 ):
+    totals = disordered(summed(0, half, asked, returned), half, order, rows, spread)
     leaves = []
-    for index, _, velocity, position in kick_drift(0, asked, returned, local, where, moving, bins):
+    for index, _, velocity, position in kick_drift(3, totals, local, where, moving, bins):
         new_moving[component(index), :] = velocity
         new_where[component(index), :] = position
         store_state(state, index, position)
@@ -242,7 +320,8 @@
 
 
 def finish_kernel(asked, returned, local, where, moving, bins, positions, velocities, accels, rows):
-    for index, *results in kick_drift(1, asked, returned, local, where, moving, bins):
+    totals = summed(CAP, False, asked, returned)
+    for index, *results in kick_drift(2, totals, local, where, moving, bins):
         for number, result in enumerate(results):
             rows[number, component(index), :] = result
     for leaf in range(NLEAF):
@@ -282,11 +361,12 @@
 
 
 def send_forces(pushed):
-    return exchange(pushed.reshape(DEVICES, 3, CAP, LEAF)).reshape(3 * SLOTS, LEAF)
-
-
-def request_kernel(pair_owner, pair_slot, placed0, placed1, wanted, owners, slots, sems):
+    return exchange(pushed.reshape(DEVICES, 3, -1, LEAF)).reshape(pushed.shape)
+
+
+def request_kernel(pair_owner, pair_slot, time_bins, placed0, placed1, wanted, owners, slots, bins, sems):
     copies = [
+        pltpu.make_async_copy(time_bins, bins, sems.at[2]),
         pltpu.make_async_copy(pair_owner, owners, sems.at[0]),
         pltpu.make_async_copy(pair_slot, slots, sems.at[1]),
     ]
@@ -316,7 +396,10 @@
             mine = jnp.where(before == float(turn), asked, 0.0).astype(BF16)
             here = jnp.where(column == CAP * sub + turn, 1.0, 0.0).astype(BF16)
             total += lax.dot_general(mine, here, NN, preferred_element_type=F32)
-    wanted[...] = total.astype(jnp.int32) + NLEAF
+    kicked = jnp.sum(jnp.where(bins[...] >= 3, 1.0, 0.0), axis=1, keepdims=True)
+    most = jnp.max(kicked, axis=0, keepdims=True)
+    lane = lax.broadcasted_iota(jnp.int32, (DEVICES, LEAF), 1)
+    wanted[...] = jnp.where(lane == 2 * CAP, most, total + float(NLEAF)).astype(jnp.int32)
 
 
 def shards(positions, velocities, masses, time_bins, pair_owner, pair_slot, local_pairs):
@@ -326,7 +409,6 @@
     tiles_shape = shape(8 * NLEAF, LEAF)
     rows_shape = shape(3 * NLEAF, LEAF)
     looked_shape = shape(4 * SLOTS, LEAF)
-    pushed_shape = shape(3 * SLOTS, LEAF)
     asked_shape = shape(2 * CAP, DEVICES, dtype=jnp.int32)
     ends_shape = shape(2, PAIRS, dtype=jnp.int32)
     anywhere = pl.BlockSpec(memory_space=pl.ANY)
@@ -335,12 +417,14 @@
     def local_forces(ids, state):
         return call(local_kernel, tiles_shape, [state], 64 * 2**14 * 25, 2**20, scalars=[ids])
 
-    def remote_forces(places, arrived, *earlier):
+    def remote_forces(places, arrived, *earlier, half=False):
         scratch = [pltpu.SMEM((2, PAIRS), jnp.int32), dma(())]
+        if half:
+            scratch.append(pltpu.VMEM((3 * SLOTS, LEAF), F32))
         specs = [VMEM] * 2 + [anywhere] * len(earlier)
         return call(
-            functools.partial(remote_kernel, len(earlier)),
-            pushed_shape,
+            functools.partial(remote_kernel, len(earlier), half),
+            shape((3 * SLOTS) // (2 if half else 1), LEAF),
             [places, arrived, *earlier],
             128 * 2**14 * 25,
             2**21,
@@ -348,41 +432,59 @@
             specs,
         )
 
+    def subcycle0(half):
+        def run(places, arrived, *arrays):
+            returned = send_forces(remote_forces(places, arrived, half=half))
+            wanted, asked, *others = arrays
+            return call(
+                functools.partial(advance_kernel, half),
+                (looked_shape, tiles_shape, rows_shape, rows_shape),
+                [wanted, asked, returned, *others],
+                2**16,
+                2**22,
+                [pltpu.VMEM((3, 8 * NLEAF, LEAF), F32), pltpu.VMEM((3 * NLEAF, LEAF), F32)],
+            )
+
+        return run
+
     *placed, wanted = call(
         request_kernel,
         (ends_shape, ends_shape, shape(DEVICES, LEAF, dtype=jnp.int32)),
-        [pair_owner.transpose(0, 2, 1), pair_slot.transpose(0, 2, 1)],
+        [pair_owner.transpose(0, 2, 1), pair_slot.transpose(0, 2, 1), bins],
         2**26,
         2**18,
-        [pltpu.VMEM((2, 2, PAIRS), jnp.int32), pltpu.VMEM((2, 2, PAIRS), jnp.int32), dma((2,))],
-        [pl.BlockSpec(memory_space=pltpu.HBM)] * 2,
+        [
+            pltpu.VMEM((2, 2, PAIRS), jnp.int32),
+            pltpu.VMEM((2, 2, PAIRS), jnp.int32),
+            pltpu.VMEM((NLEAF, LEAF), jnp.int32),
+            dma((3,)),
+        ],
+        [pl.BlockSpec(memory_space=pltpu.HBM)] * 3,
         vmem=60 * 2**20,
     )
     wanted = exchange(wanted.reshape(DEVICES, 1, LEAF)).reshape(DEVICES, LEAF)
-    state, where, moving, *placed = call(
+    state, where, moving, *placed, order, ordered = call(
         pack_kernel,
-        (tiles_shape, rows_shape, rows_shape, ends_shape, ends_shape),
-        [positions, velocities, masses, *placed],
+        (
+            tiles_shape, rows_shape, rows_shape, ends_shape, ends_shape,
+            shape(NLEAF, LEAF, dtype=jnp.int32), tiles_shape,
+        ),
+        [positions, velocities, masses, bins, *placed],
         2**16,
         2**20,
     )
-    local = local_forces(local_ids[0], state)
-    looked, asked = call(
+    looked, asked, most = call(
         gather_kernel,
-        (looked_shape, asked_shape),
-        [wanted, where, masses, local],
+        (looked_shape, shape(2 * CAP, DEVICES, dtype=jnp.int32), shape(1, 1, dtype=jnp.int32)),
+        [wanted, ordered],
         2**16,
         2**21,
-        in_specs=[VMEM, VMEM, VMEM, anywhere],
-    )
-    pushed = remote_forces(placed[0], send_leaves(looked))
-    returned = send_forces(pushed)
-    looked, state, where, moving = call(
-        advance_kernel,
-        (looked_shape, tiles_shape, rows_shape, rows_shape),
-        [wanted, asked, returned, local, masses, where, moving, bins],
-        2**16,
-        2**22,
+    )
+    local = local_forces(local_ids[0], state)
+    few = most[0, 0] <= LEAF // 2
+    looked, state, where, moving = lax.cond(
+        few, subcycle0(True), subcycle0(False),
+        placed[0], send_leaves(looked), wanted, asked, local, masses, where, moving, bins, order,
     )
     local = local_forces(local_ids[1], state)
     pushed = remote_forces(placed[1], send_leaves(looked), local)

time: 127 us -> 125 us (0.984)
  blocking collectives: 65.1 us -> 37.1 us
  waiting for transfers between devices: 21.3 us -> 37.8 us
  starting transfers between devices: 15.9 us -> 20.7 us
  Pallas kernels: 22.9 us -> 27 us
    all_to_all x3 -> x2, blocking collectives: 65.1 us -> 37.1 us  [exchange(): return lax.all_to_all(array, AXES, split_axis=0, concat_axis=0, tiled=True)]
    all_to_all x2 -> x3, waiting for transfers between devices: 21.3 us -> 37.8 us  [exchange(): return lax.all_to_all(array, AXES, split_axis=0, concat_axis=0, tiled=True)]
    all_to_all x2 -> x3, starting transfers between devices: 15.9 us -> 20.7 us  [exchange(): return lax.all_to_all(array, AXES, split_axis=0, concat_axis=0, tiled=True)]
    pallas_call x9, Pallas kernels: 22.9 us -> 27 us  [call(): pl.pallas_call(kernel, out_shape=out_shapes, grid_spec=pltpu.PrefetchScal...]
  transfers between devices with their start and end apart: 2 -> 3, of which waited for: 2 -> 3; matrix products, arithmetic and copies ran while one was open for 0% -> 0% of each run, Pallas kernels for 5% -> 7%
where the time goes in v5:
time: 125 us
  waiting for transfers between devices  37.8 us (30%)
  blocking collectives  37.1 us (30%)
  Pallas kernels  27 us (22%)
  starting transfers between devices  20.7 us (17%)
  between operations  1.44 us (1%)
    all_to_all x3, waiting for transfers between devices, exchange(): return lax.all_to_all(array, AXES, split_axis=0, concat_axis=0, tiled=True)  37.8 us
    all_to_all x2, blocking collectives, exchange(): return lax.all_to_all(array, AXES, split_axis=0, concat_axis=0, tiled=True)  37.1 us
    pallas_call x9, Pallas kernels, call(): pl.pallas_call(kernel, out_shape=out_shapes, grid_spec=pltpu.PrefetchScal...  27 us
    all_to_all x3, starting transfers between devices, exchange(): return lax.all_to_all(array, AXES, split_axis=0, concat_axis=0, tiled=True)  20.7 us
  transfers between devices with their start and end apart: 3, of which 3 were waited for; matrix products, arithmetic and copies ran while one was open for 0% of the time, Pallas kernels for 7%

profile of v5, /device:TPU:1, one launch (start us, length us, event | category | flops | bytes accessed | tf_op | source)
XLA Modules:
  0.0 124.8 jit_solution(15536944041116742128)
XLA Ops:
  0.6 0.0 copy-start.1
  0.6 0.0 copy-start.4
  0.7 0.0 copy-start.5
  0.7 2.0 %shard_map.94 = (s32[2,128]{1,0:T(2,128)}, s32[2,128]{1,0:T(2,128)}, s32[128,128]{1,0:T(8,128)}) custom-call(s32[2,2,128]{2,1,0:T(2,128)} %bitcast.46, s32[2,2,128]{2,1,0:T(2,128)} %bitcast.47, s32[64,128]{1,0:T(8,128)} %bitcast.36), custom_call_target="tpu_custom_call" | custom-call | flops 67108864 | bytes 262144 | tf_op jit(solution)/shard_map/pallas_call | solution.py:336
  2.7 0.0 copy-start
  2.7 11.5 %all-to-all-start.2 = ((s32[128,1,128]{2,1,0:T(1,128)}), s32[128,1,128]{2,1,0:T(1,128)S(1)}, u32[]{:S(2)}, u32[]{:S(2)}) async-start(s32[128,1,128]{2,1,0:T(1,128)} %bitcast.44), calls=%async_computation.2 | async-start | bytes 131072 | tf_op jit(solution)/shard_map/all_to_all | solution.py:356
  14.2 0.0 copy-start.3
  14.2 0.0 copy-start.2
  14.2 0.0 copy-done.1
  14.3 0.0 copy-done.4
  14.3 0.0 copy-done.5
  14.3 0.0 copy-done
  14.3 0.6 copy-done.3
  14.9 0.0 copy-done.2
  14.9 2.3 %shard_map.95 = (f32[512,128]{1,0:T(8,128)S(1)}, f32[192,128]{1,0:T(8,128)S(1)}, f32[192,128]{1,0:T(8,128)S(1)}, s32[2,128]{1,0:T(2,128)S(1)}, s32[2,128]{1,0:T(...) custom-call(f32[3,8192]{1,0:T(4,128)S(1)} %copy-done, f32[3,8192]{1,0:T(4,128)S(1)} %copy-done.1, ...), custom_call_target="tpu_custom_call" | custom-call | flops 65536 | bytes 1048576 | tf_op jit(solution)/shard_map/pallas_call | solution.py:336
  17.3 6.4 %all-to-all-done.2 = s32[128,1,128]{2,1,0:T(1,128)S(1)} async-done(((s32[128,1,128]{2,1,0:T(1,128)}), s32[128,1,128]{2,1,0:T(1,128)S(1)}, u32[]{:S(2)}, u32[]{:S(2)}) %all-to-all-start.2) | async-done | bytes 65568 | tf_op jit(solution)/shard_map/all_to_all | solution.py:356
  23.6 1.5 %shard_map.96 = (f32[2048,128]{1,0:T(8,128)}, s32[8,128]{1,0:T(8,128)S(1)}, s32[1,1]{1,0:T(1,128)}) custom-call(s32[128,128]{1,0:T(8,128)S(1)} %bitcast.33, f32[512,128]{1,0:T(8,128)S(1)} %get-tuple-element.83.ordered), custom_call_target="tpu_custom_call" | custom-call | flops 65536 | bytes 2097152 | tf_op jit(solution)/shard_map/pallas_call | solution.py:336
  25.2 0.0 copy-start.6
  25.2 4.6 %all-to-all-start.3 = ((f32[128,16,128]{2,1,0:T(8,128)}), f32[128,16,128]{2,1,0:T(8,128)S(1)}, u32[]{:S(2)}, u32[]{:S(2)}) async-start(f32[128,16,128]{2,1,0:T(8,128)} %bitcast.12), calls=%async_computation.3 | async-start | bytes 2097152 | tf_op jit(solution)/shard_map/all_to_all | solution.py:356
  29.8 0.0 copy-done.6
  29.8 3.3 %shard_map.97 = f32[512,128]{1,0:T(8,128)S(1)} custom-call(s32[2,64]{1,0:T(2,128)S(1)} %get-tuple-element.98.pairs, f32[512,128]{1,0:T(8,128)S(1)} %get-tuple-element.89.state), custom_call_target="tpu_custom_call" | custom-call | flops 26214400 | bytes 1048576 | tf_op jit(solution)/shard_map/pallas_call | solution.py:336
  33.8 15.4 %all-to-all-done.3 = f32[128,16,128]{2,1,0:T(8,128)S(1)} async-done(((f32[128,16,128]{2,1,0:T(8,128)}), f32[128,16,128]{2,1,0:T(8,128)S(1)}, u32[]{:S(2)}, u32[]{:S(2)}) %all-to-all-start.3) | async-done | bytes 1048608 | tf_op jit(solution)/shard_map/all_to_all | solution.py:356
  49.1 24.5 %conditional.1 = ((f32[2048,128]{1,0:T(8,128)}, f32[512,128]{1,0:T(8,128)S(1)}, f32[192,128]{1,0:T(8,128)S(1)}, f32[192,128]{1,0:T(8,128)S(1)})) conditional(s32[]{:T(128)} %bitcast.11, (s32[2,128]{1,0:T(2,128)S(1)}, f32[2048,128]{1,0:T(8,128)S(1)}, s32[128,128]{1,0:T(8,128)S(1)}, s32[8,128]{1,0:T(8,128)S(1)}, f32[512,128]{1,0:T(8,128)S(1)}, ...), branch_computations={%region_0.0_spmd, %region_1.0_spmd} | conditional | flops 52494336 | bytes 7864328 | solution.py:485
  49.1 5.4 %branch_1_fun.2 = f32[768,128]{1,0:T(8,128)S(1)} custom-call(s32[2,128]{1,0:T(2,128)S(1)} %get-tuple-element.52.places, f32[2048,128]{1,0:T(8,128)S(1)} %get-tuple-element.53.arrived), custom_call_target="tpu_custom_call" | custom-call | flops 52428800 | bytes 2097152 | tf_op jit(solution)/shard_map/cond/branch_1_fun/pallas_call | solution.py:336
  54.5 16.5 %all_to_all.29 = f32[128,3,2,128]{3,2,1,0:T(2,128)S(1)} all-to-all(f32[128,3,2,128]{3,2,1,0:T(2,128)S(1)} %bitcast.30), channel_id=1, replica_groups=mesh['gx'=4,'gy'=4,'gz'=8] {'gx','gy','gz'}, dimensions={0} | all-to-all | bytes 786432 | tf_op jit(solution)/shard_map/cond/branch_1_fun/all_to_all | solution.py:356
  71.0 2.6 %branch_1_fun.3 = (f32[2048,128]{1,0:T(8,128)}, f32[512,128]{1,0:T(8,128)S(1)}, f32[192,128]{1,0:T(8,128)S(1)}, f32[192,128]{1,0:T(8,128)S(1)}) custom-call(s32[128,128]{1,0:T(8,128)S(1)} %get-tuple-element.50.wanted, s32[8,128]{1,0:T(8,128)S(1)} %get-tuple-element.51.asked, f32[768,128]{1,0:T(8,128)S(1)} %bitcast.29, ...), custom_call_target="tpu_custom_call" | custom-call | flops 65536 | bytes 4194304 | tf_op jit(solution)/shard_map/cond/branch_1_fun/pallas_call | solution.py:336
  73.6 4.6 %all-to-all-start.4 = ((f32[128,16,128]{2,1,0:T(8,128)}), f32[128,16,128]{2,1,0:T(8,128)S(1)}, u32[]{:S(2)}, u32[]{:S(2)}) async-start(f32[128,16,128]{2,1,0:T(8,128)} %bitcast.16), calls=%async_computation.4 | async-start | bytes 2097152 | tf_op jit(solution)/shard_map/all_to_all | solution.py:356
  78.2 3.3 %shard_map.98.refs_0_.local = f32[512,128]{1,0:T(8,128)S(1)} custom-call(s32[2,64]{1,0:T(2,128)S(1)} %get-tuple-element.97.pairs, f32[512,128]{1,0:T(8,128)S(1)} %get-tuple-element.94.state), custom_call_target="tpu_custom_call" | custom-call | flops 26214400 | bytes 1048576 | tf_op jit(solution)/shard_map/pallas_call | solution.py:336
  81.5 16.1 %all-to-all-done.4 = f32[128,16,128]{2,1,0:T(8,128)S(1)} async-done(((f32[128,16,128]{2,1,0:T(8,128)}), f32[128,16,128]{2,1,0:T(8,128)S(1)}, u32[]{:S(2)}, u32[]{:S(2)}) %all-to-all-start.4) | async-done | bytes 1048608 | tf_op jit(solution)/shard_map/all_to_all | solution.py:356
  97.5 5.2 %shard_map.99 = f32[1536,128]{1,0:T(8,128)S(1)} custom-call(s32[2,128]{1,0:T(2,128)S(1)} %get-tuple-element.85.places, f32[2048,128]{1,0:T(8,128)S(1)} %bitcast.24, f32[512,128]{1,0:T(8,128)S(1)} %shard_map.98.refs_0_.local), custom_call_target="tpu_custom_call" | custom-call | flops 52428800 | bytes 2097152 | tf_op jit(solution)/shard_map/pallas_call | solution.py:336
  102.8 20.7 %all_to_all.30 = f32[128,3,4,128]{3,2,1,0:T(4,128)S(1)} all-to-all(f32[128,3,4,128]{3,2,1,0:T(4,128)S(1)} %bitcast.28), channel_id=1, replica_groups=mesh['gx'=4,'gy'=4,'gz'=8] {'gx','gy','gz'}, dimensions={0} | all-to-all | bytes 1572864 | tf_op jit(solution)/shard_map/all_to_all | solution.py:356
  123.4 1.4 %shard_map.100 = (f32[3,8192]{1,0:T(4,128)}, f32[3,8192]{1,0:T(4,128)}, f32[3,8192]{1,0:T(4,128)}) custom-call(s32[8,128]{1,0:T(8,128)S(1)} %get-tuple-element.84.asked, f32[1536,128]{1,0:T(8,128)S(1)} %bitcast.25, f32[512,128]{1,0:T(8,128)S(1)} %shard_map.98.refs_0_.local, f32[192,128]{1,0:T(8,128)S(1)} %get-tuple-element.95.where, ...), custom_call_target="tpu_custom_call" | custom-call | flops 65536 | bytes 4194304 | tf_op jit(solution)/shard_map/pallas_call | solution.py:336
  (1 shorter events, 0.0 us)
Async XLA Ops:
  0.6 13.6 %copy-start.1 = (f32[3,8192]{1,0:T(4,128)S(1)}, f32[3,8192]{1,0:T(4,128)}, u32[]{:S(2)}) copy-start(f32[3,8192]{1,0:T(4,128)} %velocities.1) | copy-start | bytes 294916
  0.6 13.6 %copy-start.4 = (s32[8192]{0:T(1024)S(1)}, s32[8192]{0:T(1024)}, u32[]{:S(2)}) copy-start(s32[8192]{0:T(1024)} %param.12) | copy-start | bytes 98308
  0.7 13.6 %copy-start.5 = (f32[8192]{0:T(1024)S(1)}, f32[8192]{0:T(1024)}, u32[]{:S(2)}) copy-start(f32[8192]{0:T(1024)} %param.11) | copy-start | bytes 98308
  2.7 11.6 %copy-start = (f32[3,8192]{1,0:T(4,128)S(1)}, f32[3,8192]{1,0:T(4,128)}, u32[]{:S(2)}) copy-start(f32[3,8192]{1,0:T(4,128)} %positions.1) | copy-start | bytes 294916
  2.7 20.9 %all-to-all-start.2 = ((s32[128,1,128]{2,1,0:T(1,128)}), s32[128,1,128]{2,1,0:T(1,128)S(1)}, u32[]{:S(2)}, u32[]{:S(2)}) async-start(s32[128,1,128]{2,1,0:T(1,128)} %bitcast.44), calls=%async_computation.2 | async-start | bytes 131072 | tf_op jit(solution)/shard_map/all_to_all | solution.py:356
  14.2 0.7 copy-start.3
  14.2 0.7 copy-start.2
  25.2 4.6 %copy-start.6 = (s32[2,64,2]{1,2,0:T(2,128)S(1)}, s32[2,64,2]{1,2,0:T(2,128)}, u32[]{:S(2)}) copy-start(s32[2,64,2]{1,2,0:T(2,128)} %param.15) | copy-start | bytes 3076
  25.2 24.0 %all-to-all-start.3 = ((f32[128,16,128]{2,1,0:T(8,128)}), f32[128,16,128]{2,1,0:T(8,128)S(1)}, u32[]{:S(2)}, u32[]{:S(2)}) async-start(f32[128,16,128]{2,1,0:T(8,128)} %bitcast.12), calls=%async_computation.3 | async-start | bytes 2097152 | tf_op jit(solution)/shard_map/all_to_all | solution.py:356
  73.6 23.9 %all-to-all-start.4 = ((f32[128,16,128]{2,1,0:T(8,128)}), f32[128,16,128]{2,1,0:T(8,128)S(1)}, u32[]{:S(2)}, u32[]{:S(2)}) async-start(f32[128,16,128]{2,1,0:T(8,128)} %bitcast.16), calls=%async_computation.4 | async-start | bytes 2097152 | tf_op jit(solution)/shard_map/all_to_all | solution.py:356

commit v6 on v5

--- a/solution.py
+++ b/solution.py
@@ -37,14 +37,12 @@
 
 
 def pair_parts(tile, row):
-    vector = (row & 3) < 3
-    xyz = jnp.where(vector, tile - CENTRE, 0.0)
+    xyz = jnp.where((row & 3) < 3, tile - CENTRE, 1.0)
     parts = split3(xyz)
     square = xyz * xyz
     norm = pltpu.roll(square, 1, 0) + pltpu.roll(square, 2, 0) + pltpu.roll(square, 3, 0)
     norms = split3(norm + jnp.where(row == 3, SOFTENING, 0.0))
-    mass = jnp.where(row < 4, tile[3:4], tile[7:8]) * (1.0 / CUTOFF_SQ**2)
-    weights = split3(jnp.where(vector, xyz, 1.0) * mass)
+    weights = split3(xyz * jnp.where(row < 4, tile[3:4], tile[7:8]))
     weights = jnp.concatenate([*weights, jnp.zeros_like(xyz)], axis=0).astype(BF16)
     return xyz, parts, norms, weights
 
@@ -52,13 +50,17 @@
 def softened_distances(parts, norms, row):
     high, middle, low = parts
     minus_two = jnp.where(row < 3, -2.0, 0.0)
+    one = jnp.where(row == 3, 1.0, 0.0)
     h2, m2, l2 = (pltpu.roll(part, 4, 0) * minus_two for part in parts)
-    lhs, rhs = [], []
-    for left, right, norm in zip(parts, (h2, h2, h2), norms):
-        lhs.append(left + jnp.where(row == 3, norm, jnp.where(row == 7, 1.0, 0.0)))
-        rhs.append(right + jnp.where(row == 7, norm, jnp.where(row == 3, 1.0, 0.0)))
-    lhs = jnp.concatenate(lhs + [high, high, middle], axis=0).astype(BF16)
-    rhs = jnp.concatenate(rhs + [m2, l2, m2], axis=0).astype(BF16)
+    n0, n1, n2 = norms
+    h3 = h2 + one
+    lhs = [high, high, high] + [
+        jnp.where(row == 3, norm, part) for norm, part in ((n0, middle), (n1, low), (n2, middle))
+    ]
+    rhs = [jnp.where(row == 7, norm, part) for norm, part in ((n0, h2), (n1, m2), (n2, l2))]
+    rhs += [h3, h3, m2 + one]
+    lhs = jnp.concatenate(lhs, axis=0).astype(BF16)
+    rhs = jnp.concatenate(rhs, axis=0).astype(BF16)
     return lax.dot_general(lhs, rhs, TN, preferred_element_type=F32)
 
 
@@ -71,12 +73,15 @@
     return high, (kernel - high.astype(F32)).astype(BF16)
 
 
-def moments(weights, kernel):
+def moments(weights, kernel, half):
     high, low = kernel
+    count = LEAF // 2 if half else LEAF
     twice = jnp.concatenate([weights, weights], axis=1)
     on_left = lax.dot_general(
-        jnp.concatenate([high, low], axis=1), twice, NT, preferred_element_type=F32
+        jnp.concatenate([high[:count], low[:count]], axis=1), twice, NT, preferred_element_type=F32
     ).T
+    if half:
+        on_left = jnp.concatenate([on_left, jnp.zeros_like(on_left)], axis=1)
     on_right = lax.dot_general(
         twice, jnp.concatenate([high, low], axis=0), NN, preferred_element_type=F32
     )
@@ -90,7 +95,7 @@
     return total - pltpu.roll(xyz, 4, 0) * mass
 
 
-def pair_forces(tiles, row):
+def pair_forces(tiles, row, half=False):
     count = len(tiles)
     parts, dists, sums, out = {}, {}, {}, []
     for step in range(count + 10):
@@ -99,7 +104,7 @@
             dists[step] = softened_distances(parts[step][1], parts[step][2], row)
         k = step - 6
         if 0 <= k < count:
-            sums[k] = moments(parts[k][3], pair_kernel(dists[k]))
+            sums[k] = moments(parts[k][3], pair_kernel(dists[k]), half)
         k = step - 10
         if k >= 0:
             out.append(force_tile(sums[k], parts[k][0], row))
@@ -219,16 +224,16 @@
     copy.wait()
     unroll = 64
 
-    def leaf(slot, half):
+    def leaf(slot, side):
         tile = arrived[pl.ds(pl.multiple_of((slot >> 1) * 8, 8), 8), :]
-        return jnp.where((slot & 1) == half, tile, pltpu.roll(tile, 4, 0))
+        return jnp.where((slot & 1) == side, tile, pltpu.roll(tile, 4, 0))
 
     def body(step, carry):
         ids = [
             (placed[0, step * unroll + u], placed[1, step * unroll + u])
             for u in range(unroll)
         ]
-        found = pair_forces([jnp.where(row < 4, leaf(a, 0), leaf(b, 1)) for a, b in ids], row)
+        found = pair_forces([jnp.where(row < 4, leaf(a, 0), leaf(b, 1)) for a, b in ids], row, half)
         for (a, b), force in zip(ids, found):
             for slot, first in ((a, 4), (b, 0)):
                 at = 3 * ((slot >> 1) + (slot & 1) * (SLOTS // 2)) if half else 3 * slot
@@ -274,15 +279,15 @@
 
 
 def disordered(totals, half, order, rows, spread):
-    rows[...] = jnp.zeros_like(rows)
+    rows[:, 3 * NLEAF :, :] = jnp.zeros((3, 5 * NLEAF, LEAF), F32)
     for index, total in enumerate(totals):
         for number, part in enumerate(split3(total)):
             rows[number, component(index), :] = part
     count = LEAF // 2 if half else LEAF
 
     def body(step, carry):
-        for u in range(32):
-            leaf = step * 32 + u
+        for u in range(64):
+            leaf = step * 64 + u
             parts = [rows[number, pl.ds(leaf, 8, stride=NLEAF), :] for number in range(3)]
             moved = lax.dot_general(
                 stacked(parts)[:, :count], lanes_of(order, leaf, count), NN, preferred_element_type=F32
@@ -291,7 +296,7 @@
             spread[pl.ds(leaf, 3, stride=NLEAF), :] = moved[0:3]
         return carry
 
-    lax.fori_loop(0, NLEAF // 32, body, 0)
+    lax.fori_loop(0, NLEAF // 64, body, 0)
     return [spread[component(index), :] for index in range(3)]
 
 
@@ -299,6 +304,7 @@
     active = bins[...] >= threshold
     for index, accel in enumerate(totals):
         accel += local[pl.ds(index, NLEAF, stride=8), :] + local[pl.ds(index + 4, NLEAF, stride=8), :]
+        accel *= 1.0 / CUTOFF_SQ**2
         velocity = moving[component(index), :] + jnp.where(active, TIME_STEP * accel, 0.0)
         yield index, accel, velocity, where[component(index), :] + TIME_STEP * velocity
 

time: 125 us -> 125 us (level)
  no operation moved by 1% of the time
where the time goes in v6:
time: 125 us; the launch traced here: 124 us
  waiting for transfers between devices  37.8 us (30%)
  blocking collectives  37.1 us (30%)
  Pallas kernels  26.6 us (21%)
  starting transfers between devices  20.7 us (17%)
  between operations  1.44 us (1%)
    all_to_all x3, waiting for transfers between devices, exchange(): return lax.all_to_all(array, AXES, split_axis=0, concat_axis=0, tiled=True)  37.8 us
    all_to_all x2, blocking collectives, exchange(): return lax.all_to_all(array, AXES, split_axis=0, concat_axis=0, tiled=True)  37.1 us
    pallas_call x9, Pallas kernels, call(): pl.pallas_call(kernel, out_shape=out_shapes, grid_spec=pltpu.PrefetchScal...  26.6 us
    all_to_all x3, starting transfers between devices, exchange(): return lax.all_to_all(array, AXES, split_axis=0, concat_axis=0, tiled=True)  20.7 us
  transfers between devices with their start and end apart: 3, of which 3 were waited for; matrix products, arithmetic and copies ran while one was open for 0% of the time, Pallas kernels for 7%

profile of v6, /device:TPU:1, one launch (start us, length us, event | category | flops | bytes accessed | tf_op | source)
XLA Modules:
  0.0 124.4 jit_solution(12161681860146617023)
XLA Ops:
  0.6 0.0 copy-start.1
  0.6 0.0 copy-start.4
  0.7 0.0 copy-start.5
  0.7 2.0 %shard_map.94 = (s32[2,128]{1,0:T(2,128)}, s32[2,128]{1,0:T(2,128)}, s32[128,128]{1,0:T(8,128)}) custom-call(s32[2,2,128]{2,1,0:T(2,128)} %bitcast.46, s32[2,2,128]{2,1,0:T(2,128)} %bitcast.47, s32[64,128]{1,0:T(8,128)} %bitcast.36), custom_call_target="tpu_custom_call" | custom-call | flops 67108864 | bytes 262144 | tf_op jit(solution)/shard_map/pallas_call | solution.py:342
  2.7 0.0 copy-start
  2.7 11.5 %all-to-all-start.2 = ((s32[128,1,128]{2,1,0:T(1,128)}), s32[128,1,128]{2,1,0:T(1,128)S(1)}, u32[]{:S(2)}, u32[]{:S(2)}) async-start(s32[128,1,128]{2,1,0:T(1,128)} %bitcast.44), calls=%async_computation.2 | async-start | bytes 131072 | tf_op jit(solution)/shard_map/all_to_all | solution.py:362
  14.2 0.0 copy-start.3
  14.2 0.0 copy-start.2
  14.2 0.0 copy-done.1
  14.3 0.0 copy-done.4
  14.3 0.0 copy-done.5
  14.3 0.0 copy-done
  14.3 0.6 copy-done.3
  14.9 0.0 copy-done.2
  14.9 2.3 %shard_map.95 = (f32[512,128]{1,0:T(8,128)S(1)}, f32[192,128]{1,0:T(8,128)S(1)}, f32[192,128]{1,0:T(8,128)S(1)}, s32[2,128]{1,0:T(2,128)S(1)}, s32[2,128]{1,0:T(...) custom-call(f32[3,8192]{1,0:T(4,128)S(1)} %copy-done, f32[3,8192]{1,0:T(4,128)S(1)} %copy-done.1, ...), custom_call_target="tpu_custom_call" | custom-call | flops 65536 | bytes 1048576 | tf_op jit(solution)/shard_map/pallas_call | solution.py:342
  17.3 6.4 %all-to-all-done.2 = s32[128,1,128]{2,1,0:T(1,128)S(1)} async-done(((s32[128,1,128]{2,1,0:T(1,128)}), s32[128,1,128]{2,1,0:T(1,128)S(1)}, u32[]{:S(2)}, u32[]{:S(2)}) %all-to-all-start.2) | async-done | bytes 65568 | tf_op jit(solution)/shard_map/all_to_all | solution.py:362
  23.6 1.5 %shard_map.96 = (f32[2048,128]{1,0:T(8,128)}, s32[8,128]{1,0:T(8,128)S(1)}, s32[1,1]{1,0:T(1,128)}) custom-call(s32[128,128]{1,0:T(8,128)S(1)} %bitcast.33, f32[512,128]{1,0:T(8,128)S(1)} %get-tuple-element.83.ordered), custom_call_target="tpu_custom_call" | custom-call | flops 65536 | bytes 2097152 | tf_op jit(solution)/shard_map/pallas_call | solution.py:342
  25.2 0.0 copy-start.6
  25.2 4.6 %all-to-all-start.3 = ((f32[128,16,128]{2,1,0:T(8,128)}), f32[128,16,128]{2,1,0:T(8,128)S(1)}, u32[]{:S(2)}, u32[]{:S(2)}) async-start(f32[128,16,128]{2,1,0:T(8,128)} %bitcast.12), calls=%async_computation.3 | async-start | bytes 2097152 | tf_op jit(solution)/shard_map/all_to_all | solution.py:362
  29.8 0.0 copy-done.6
  29.8 3.3 %shard_map.97 = f32[512,128]{1,0:T(8,128)S(1)} custom-call(s32[2,64]{1,0:T(2,128)S(1)} %get-tuple-element.98.pairs, f32[512,128]{1,0:T(8,128)S(1)} %get-tuple-element.89.state), custom_call_target="tpu_custom_call" | custom-call | flops 26214400 | bytes 1048576 | tf_op jit(solution)/shard_map/pallas_call | solution.py:342
  33.7 15.4 %all-to-all-done.3 = f32[128,16,128]{2,1,0:T(8,128)S(1)} async-done(((f32[128,16,128]{2,1,0:T(8,128)}), f32[128,16,128]{2,1,0:T(8,128)S(1)}, u32[]{:S(2)}, u32[]{:S(2)}) %all-to-all-start.3) | async-done | bytes 1048608 | tf_op jit(solution)/shard_map/all_to_all | solution.py:362
  49.1 24.1 %conditional.1 = ((f32[2048,128]{1,0:T(8,128)}, f32[512,128]{1,0:T(8,128)S(1)}, f32[192,128]{1,0:T(8,128)S(1)}, f32[192,128]{1,0:T(8,128)S(1)})) conditional(s32[]{:T(128)} %bitcast.11, (s32[2,128]{1,0:T(2,128)S(1)}, f32[2048,128]{1,0:T(8,128)S(1)}, s32[128,128]{1,0:T(8,128)S(1)}, s32[8,128]{1,0:T(8,128)S(1)}, f32[512,128]{1,0:T(8,128)S(1)}, ...), branch_computations={%region_0.0_spmd, %region_1.0_spmd} | conditional | flops 52494336 | bytes 7864328 | solution.py:491
  49.1 5.2 %branch_1_fun.2 = f32[768,128]{1,0:T(8,128)S(1)} custom-call(s32[2,128]{1,0:T(2,128)S(1)} %get-tuple-element.52.places, f32[2048,128]{1,0:T(8,128)S(1)} %get-tuple-element.53.arrived), custom_call_target="tpu_custom_call" | custom-call | flops 52428800 | bytes 2097152 | tf_op jit(solution)/shard_map/cond/branch_1_fun/pallas_call | solution.py:342
  54.3 16.5 %all_to_all.29 = f32[128,3,2,128]{3,2,1,0:T(2,128)S(1)} all-to-all(f32[128,3,2,128]{3,2,1,0:T(2,128)S(1)} %bitcast.30), channel_id=1, replica_groups=mesh['gx'=4,'gy'=4,'gz'=8] {'gx','gy','gz'}, dimensions={0} | all-to-all | bytes 786432 | tf_op jit(solution)/shard_map/cond/branch_1_fun/all_to_all | solution.py:362
  70.8 2.5 %branch_1_fun.3 = (f32[2048,128]{1,0:T(8,128)}, f32[512,128]{1,0:T(8,128)S(1)}, f32[192,128]{1,0:T(8,128)S(1)}, f32[192,128]{1,0:T(8,128)S(1)}) custom-call(s32[128,128]{1,0:T(8,128)S(1)} %get-tuple-element.50.wanted, s32[8,128]{1,0:T(8,128)S(1)} %get-tuple-element.51.asked, f32[768,128]{1,0:T(8,128)S(1)} %bitcast.29, ...), custom_call_target="tpu_custom_call" | custom-call | flops 65536 | bytes 4194304 | tf_op jit(solution)/shard_map/cond/branch_1_fun/pallas_call | solution.py:342
  73.3 4.6 %all-to-all-start.4 = ((f32[128,16,128]{2,1,0:T(8,128)}), f32[128,16,128]{2,1,0:T(8,128)S(1)}, u32[]{:S(2)}, u32[]{:S(2)}) async-start(f32[128,16,128]{2,1,0:T(8,128)} %bitcast.16), calls=%async_computation.4 | async-start | bytes 2097152 | tf_op jit(solution)/shard_map/all_to_all | solution.py:362
  77.8 3.3 %shard_map.98.refs_0_.local = f32[512,128]{1,0:T(8,128)S(1)} custom-call(s32[2,64]{1,0:T(2,128)S(1)} %get-tuple-element.97.pairs, f32[512,128]{1,0:T(8,128)S(1)} %get-tuple-element.94.state), custom_call_target="tpu_custom_call" | custom-call | flops 26214400 | bytes 1048576 | tf_op jit(solution)/shard_map/pallas_call | solution.py:342
  81.1 16.1 %all-to-all-done.4 = f32[128,16,128]{2,1,0:T(8,128)S(1)} async-done(((f32[128,16,128]{2,1,0:T(8,128)}), f32[128,16,128]{2,1,0:T(8,128)S(1)}, u32[]{:S(2)}, u32[]{:S(2)}) %all-to-all-start.4) | async-done | bytes 1048608 | tf_op jit(solution)/shard_map/all_to_all | solution.py:362
  97.2 5.2 %shard_map.99 = f32[1536,128]{1,0:T(8,128)S(1)} custom-call(s32[2,128]{1,0:T(2,128)S(1)} %get-tuple-element.85.places, f32[2048,128]{1,0:T(8,128)S(1)} %bitcast.24, f32[512,128]{1,0:T(8,128)S(1)} %shard_map.98.refs_0_.local), custom_call_target="tpu_custom_call" | custom-call | flops 52428800 | bytes 2097152 | tf_op jit(solution)/shard_map/pallas_call | solution.py:342
  102.4 20.7 %all_to_all.30 = f32[128,3,4,128]{3,2,1,0:T(4,128)S(1)} all-to-all(f32[128,3,4,128]{3,2,1,0:T(4,128)S(1)} %bitcast.28), channel_id=1, replica_groups=mesh['gx'=4,'gy'=4,'gz'=8] {'gx','gy','gz'}, dimensions={0} | all-to-all | bytes 1572864 | tf_op jit(solution)/shard_map/all_to_all | solution.py:362
  123.1 1.4 %shard_map.100 = (f32[3,8192]{1,0:T(4,128)}, f32[3,8192]{1,0:T(4,128)}, f32[3,8192]{1,0:T(4,128)}) custom-call(s32[8,128]{1,0:T(8,128)S(1)} %get-tuple-element.84.asked, f32[1536,128]{1,0:T(8,128)S(1)} %bitcast.25, f32[512,128]{1,0:T(8,128)S(1)} %shard_map.98.refs_0_.local, f32[192,128]{1,0:T(8,128)S(1)} %get-tuple-element.95.where, ...), custom_call_target="tpu_custom_call" | custom-call | flops 65536 | bytes 4194304 | tf_op jit(solution)/shard_map/pallas_call | solution.py:342
  (1 shorter events, 0.0 us)
Async XLA Ops:
  0.6 13.6 %copy-start.1 = (f32[3,8192]{1,0:T(4,128)S(1)}, f32[3,8192]{1,0:T(4,128)}, u32[]{:S(2)}) copy-start(f32[3,8192]{1,0:T(4,128)} %velocities.1) | copy-start | bytes 294916
  0.6 13.6 %copy-start.4 = (s32[8192]{0:T(1024)S(1)}, s32[8192]{0:T(1024)}, u32[]{:S(2)}) copy-start(s32[8192]{0:T(1024)} %param.12) | copy-start | bytes 98308
  0.7 13.6 %copy-start.5 = (f32[8192]{0:T(1024)S(1)}, f32[8192]{0:T(1024)}, u32[]{:S(2)}) copy-start(f32[8192]{0:T(1024)} %param.11) | copy-start | bytes 98308
  2.7 11.6 %copy-start = (f32[3,8192]{1,0:T(4,128)S(1)}, f32[3,8192]{1,0:T(4,128)}, u32[]{:S(2)}) copy-start(f32[3,8192]{1,0:T(4,128)} %positions.1) | copy-start | bytes 294916
  2.7 20.9 %all-to-all-start.2 = ((s32[128,1,128]{2,1,0:T(1,128)}), s32[128,1,128]{2,1,0:T(1,128)S(1)}, u32[]{:S(2)}, u32[]{:S(2)}) async-start(s32[128,1,128]{2,1,0:T(1,128)} %bitcast.44), calls=%async_computation.2 | async-start | bytes 131072 | tf_op jit(solution)/shard_map/all_to_all | solution.py:362
  14.2 0.7 copy-start.3
  14.2 0.7 copy-start.2
  25.2 4.6 %copy-start.6 = (s32[2,64,2]{1,2,0:T(2,128)S(1)}, s32[2,64,2]{1,2,0:T(2,128)}, u32[]{:S(2)}) copy-start(s32[2,64,2]{1,2,0:T(2,128)} %param.15) | copy-start | bytes 3076
  25.2 24.0 %all-to-all-start.3 = ((f32[128,16,128]{2,1,0:T(8,128)}), f32[128,16,128]{2,1,0:T(8,128)S(1)}, u32[]{:S(2)}, u32[]{:S(2)}) async-start(f32[128,16,128]{2,1,0:T(8,128)} %bitcast.12), calls=%async_computation.3 | async-start | bytes 2097152 | tf_op jit(solution)/shard_map/all_to_all | solution.py:362
  73.3 23.9 %all-to-all-start.4 = ((f32[128,16,128]{2,1,0:T(8,128)}), f32[128,16,128]{2,1,0:T(8,128)S(1)}, u32[]{:S(2)}, u32[]{:S(2)}) async-start(f32[128,16,128]{2,1,0:T(8,128)} %bitcast.16), calls=%async_computation.4 | async-start | bytes 2097152 | tf_op jit(solution)/shard_map/all_to_all | solution.py:362

commit v7 on v6

--- a/solution.py
+++ b/solution.py
@@ -142,14 +142,16 @@
 
 def pack_kernel(
     positions, velocities, masses, bins, places0, places1,
-    state, where, moving, placed0, placed1, order, ordered,
+    state, where, moving, placed0, placed1, order, ordered, spread,
 ):
     placed0[...] = places0[...]
     placed1[...] = places1[...]
     for leaf in range(NLEAF):
         lanes = slice(leaf * LEAF, (leaf + 1) * LEAF)
-        where[pl.ds(leaf, 3, stride=NLEAF), :] = positions[:, lanes]
-        moving[pl.ds(leaf, 3, stride=NLEAF), :] = velocities[:, lanes]
+        spread[0, pl.ds(leaf, 3, stride=NLEAF), :] = positions[:, lanes]
+        spread[1, pl.ds(leaf, 3, stride=NLEAF), :] = velocities[:, lanes]
+    where[...] = spread[0, : 3 * NLEAF, :]
+    moving[...] = spread[1, : 3 * NLEAF, :]
     for index in range(3):
         store_state(state, index, where[component(index), :])
     store_state(state, 3, masses[...])
@@ -164,17 +166,12 @@
     last = jnp.sum(kicked, axis=1, keepdims=True) + lane - before
     order[...] = jnp.where(kicked > 0.0, before, last).astype(jnp.int32)
 
-    def body(step, carry):
-        for u in range(8):
-            leaf = step * 8 + u
-            moved = lax.dot_general(
-                stacked(split3(leaf_tile(state, leaf))), lanes_of(order, leaf, LEAF), NT,
-                preferred_element_type=F32,
-            )
-            ordered[pl.ds(pl.multiple_of(leaf * 8, 8), 8), :] = moved[0:8] + moved[8:16] + moved[16:24]
-        return carry
-
-    lax.fori_loop(0, NLEAF // 8, body, 0)
+    for leaf in range(NLEAF):
+        tile = slice(leaf * 8, leaf * 8 + 8)
+        moved = lax.dot_general(
+            stacked(split3(state[tile, :])), lanes_of(order, leaf, LEAF), NT, preferred_element_type=F32
+        )
+        ordered[tile, :] = moved[0:8] + moved[8:16] + moved[16:24]
 
 
 def stacked(parts):
@@ -183,7 +180,7 @@
 
 def lanes_of(order, leaf, count):
     lane = lax.broadcasted_iota(jnp.int32, (count, LEAF), 0)
-    return jnp.where(lane == order[pl.ds(leaf, 1), :], 1.0, 0.0).astype(BF16)
+    return jnp.where(lane == order[leaf : leaf + 1, :], 1.0, 0.0).astype(BF16)
 
 
 def gather_kernel(wanted, ordered, looked, asked, most):
@@ -215,8 +212,7 @@
 
 
 def remote_kernel(unused, half, places, arrived, *refs):
-    pushed, placed, sem, *apart = refs[unused:]
-    forces = apart[0] if half else pushed
+    pushed, placed, sem, forces = refs[unused:]
     row = row_iota()
     copy = pltpu.make_async_copy(places, placed, sem)
     copy.start()
@@ -244,8 +240,10 @@
     if half:
         rows = pushed.shape[0]
         lower = lax.broadcasted_iota(jnp.int32, (rows, LEAF), 1) < LEAF // 2
-        odd = pltpu.roll(forces[rows:, :], LEAF // 2, 1)
+        odd = pltpu.roll(forces[rows : 2 * rows, :], LEAF // 2, 1)
         pushed[...] = jnp.where(lower, forces[:rows, :], odd)
+    else:
+        pushed[...] = forces[: 3 * SLOTS, :]
 
 
 def summed(first, half, asked, returned):
@@ -285,18 +283,12 @@
             rows[number, component(index), :] = part
     count = LEAF // 2 if half else LEAF
 
-    def body(step, carry):
-        for u in range(64):
-            leaf = step * 64 + u
-            parts = [rows[number, pl.ds(leaf, 8, stride=NLEAF), :] for number in range(3)]
-            moved = lax.dot_general(
-                stacked(parts)[:, :count], lanes_of(order, leaf, count), NN, preferred_element_type=F32
-            )
-            moved = moved[0:8] + moved[8:16] + moved[16:24]
-            spread[pl.ds(leaf, 3, stride=NLEAF), :] = moved[0:3]
-        return carry
-
-    lax.fori_loop(0, NLEAF // 64, body, 0)
+    for leaf in range(NLEAF):
+        parts = [rows[number, pl.ds(leaf, 8, stride=NLEAF), :] for number in range(3)]
+        moved = lax.dot_general(
+            stacked(parts)[:, :count], lanes_of(order, leaf, count), NN, preferred_element_type=F32
+        )
+        spread[pl.ds(leaf, 8, stride=NLEAF), :] = moved[0:8] + moved[8:16] + moved[16:24]
     return [spread[component(index), :] for index in range(3)]
 
 
@@ -425,8 +417,7 @@
 
     def remote_forces(places, arrived, *earlier, half=False):
         scratch = [pltpu.SMEM((2, PAIRS), jnp.int32), dma(())]
-        if half:
-            scratch.append(pltpu.VMEM((3 * SLOTS, LEAF), F32))
+        scratch.append(pltpu.VMEM((3 * SLOTS + 8, LEAF), F32))
         specs = [VMEM] * 2 + [anywhere] * len(earlier)
         return call(
             functools.partial(remote_kernel, len(earlier), half),
@@ -448,7 +439,7 @@
                 [wanted, asked, returned, *others],
                 2**16,
                 2**22,
-                [pltpu.VMEM((3, 8 * NLEAF, LEAF), F32), pltpu.VMEM((3 * NLEAF, LEAF), F32)],
+                [pltpu.VMEM((3, 8 * NLEAF, LEAF), F32), pltpu.VMEM((8 * NLEAF, LEAF), F32)],
             )
 
         return run
@@ -478,6 +469,7 @@
         [positions, velocities, masses, bins, *placed],
         2**16,
         2**20,
+        [pltpu.VMEM((2, 8 * NLEAF, LEAF), F32)],
     )
     looked, asked, most = call(
         gather_kernel,
@@ -502,7 +494,7 @@
         [asked, returned, local, where, moving, bins],
         2**16,
         2**22,
-        [pltpu.VMEM((3, 3 * NLEAF, LEAF), F32)],
+        [pltpu.VMEM((3, 8 * NLEAF, LEAF), F32)],
     )
 
 

time: 125 us -> 125 us (level)
  transfers between devices with their start and end apart: 3 -> 3, of which waited for: 3 -> 3; matrix products, arithmetic and copies ran while one was open for 0% -> 0% of each run, Pallas kernels for 7% -> 6%
where the time goes in v7:
time: 125 us; the launch traced here: 124 us
  waiting for transfers between devices  38.8 us (31%)
  blocking collectives  37.1 us (30%)
  Pallas kernels  25.8 us (21%)
  starting transfers between devices  20.7 us (17%)
  between operations  1.44 us (1%)
    all_to_all x3, waiting for transfers between devices, exchange(): return lax.all_to_all(array, AXES, split_axis=0, concat_axis=0, tiled=True)  38.8 us
    all_to_all x2, blocking collectives, exchange(): return lax.all_to_all(array, AXES, split_axis=0, concat_axis=0, tiled=True)  37.1 us
    pallas_call x9, Pallas kernels, call(): pl.pallas_call(kernel, out_shape=out_shapes, grid_spec=pltpu.PrefetchScal...  25.8 us
    all_to_all x3, starting transfers between devices, exchange(): return lax.all_to_all(array, AXES, split_axis=0, concat_axis=0, tiled=True)  20.7 us
  transfers between devices with their start and end apart: 3, of which 3 were waited for; matrix products, arithmetic and copies ran while one was open for 0% of the time, Pallas kernels for 6%

profile of v7, /device:TPU:1, one launch (start us, length us, event | category | flops | bytes accessed | tf_op | source)
XLA Modules:
  0.0 124.5 jit_solution(12622639231074816077)
XLA Ops:
  0.6 0.0 copy-start.1
  0.6 0.0 copy-start.4
  0.7 0.0 copy-start.5
  0.7 2.0 %shard_map.94 = (s32[2,128]{1,0:T(2,128)}, s32[2,128]{1,0:T(2,128)}, s32[128,128]{1,0:T(8,128)}) custom-call(s32[2,2,128]{2,1,0:T(2,128)} %bitcast.46, s32[2,2,128]{2,1,0:T(2,128)} %bitcast.47, s32[64,128]{1,0:T(8,128)} %bitcast.36), custom_call_target="tpu_custom_call" | custom-call | flops 67108864 | bytes 262144 | tf_op jit(solution)/shard_map/pallas_call | solution.py:334
  2.7 0.0 copy-start
  2.7 11.5 %all-to-all-start.2 = ((s32[128,1,128]{2,1,0:T(1,128)}), s32[128,1,128]{2,1,0:T(1,128)S(1)}, u32[]{:S(2)}, u32[]{:S(2)}) async-start(s32[128,1,128]{2,1,0:T(1,128)} %bitcast.44), calls=%async_computation.2 | async-start | bytes 131072 | tf_op jit(solution)/shard_map/all_to_all | solution.py:354
  14.2 0.0 copy-start.3
  14.2 0.0 copy-start.2
  14.2 0.0 copy-done.1
  14.3 0.0 copy-done.4
  14.3 0.0 copy-done.5
  14.3 0.0 copy-done
  14.3 0.6 copy-done.3
  14.9 0.0 copy-done.2
  14.9 1.4 %shard_map.95 = (f32[512,128]{1,0:T(8,128)S(1)}, f32[192,128]{1,0:T(8,128)S(1)}, f32[192,128]{1,0:T(8,128)S(1)}, s32[2,128]{1,0:T(2,128)S(1)}, s32[2,128]{1,0:T(...) custom-call(f32[3,8192]{1,0:T(4,128)S(1)} %copy-done, f32[3,8192]{1,0:T(4,128)S(1)} %copy-done.1, ...), custom_call_target="tpu_custom_call" | custom-call | flops 65536 | bytes 1048576 | tf_op jit(solution)/shard_map/pallas_call | solution.py:334
  16.3 7.3 %all-to-all-done.2 = s32[128,1,128]{2,1,0:T(1,128)S(1)} async-done(((s32[128,1,128]{2,1,0:T(1,128)}), s32[128,1,128]{2,1,0:T(1,128)S(1)}, u32[]{:S(2)}, u32[]{:S(2)}) %all-to-all-start.2) | async-done | bytes 65568 | tf_op jit(solution)/shard_map/all_to_all | solution.py:354
  23.6 1.5 %shard_map.96 = (f32[2048,128]{1,0:T(8,128)}, s32[8,128]{1,0:T(8,128)S(1)}, s32[1,1]{1,0:T(1,128)}) custom-call(s32[128,128]{1,0:T(8,128)S(1)} %bitcast.33, f32[512,128]{1,0:T(8,128)S(1)} %get-tuple-element.83.ordered), custom_call_target="tpu_custom_call" | custom-call | flops 65536 | bytes 2097152 | tf_op jit(solution)/shard_map/pallas_call | solution.py:334
  25.2 0.0 copy-start.6
  25.2 4.6 %all-to-all-start.3 = ((f32[128,16,128]{2,1,0:T(8,128)}), f32[128,16,128]{2,1,0:T(8,128)S(1)}, u32[]{:S(2)}, u32[]{:S(2)}) async-start(f32[128,16,128]{2,1,0:T(8,128)} %bitcast.12), calls=%async_computation.3 | async-start | bytes 2097152 | tf_op jit(solution)/shard_map/all_to_all | solution.py:354
  29.8 0.0 copy-done.6
  29.8 3.3 %shard_map.97 = f32[512,128]{1,0:T(8,128)S(1)} custom-call(s32[2,64]{1,0:T(2,128)S(1)} %get-tuple-element.98.pairs, f32[512,128]{1,0:T(8,128)S(1)} %get-tuple-element.89.state), custom_call_target="tpu_custom_call" | custom-call | flops 26214400 | bytes 1048576 | tf_op jit(solution)/shard_map/pallas_call | solution.py:334
  33.7 15.4 %all-to-all-done.3 = f32[128,16,128]{2,1,0:T(8,128)S(1)} async-done(((f32[128,16,128]{2,1,0:T(8,128)}), f32[128,16,128]{2,1,0:T(8,128)S(1)}, u32[]{:S(2)}, u32[]{:S(2)}) %all-to-all-start.3) | async-done | bytes 1048608 | tf_op jit(solution)/shard_map/all_to_all | solution.py:354
  49.1 24.1 %conditional.1 = ((f32[2048,128]{1,0:T(8,128)}, f32[512,128]{1,0:T(8,128)S(1)}, f32[192,128]{1,0:T(8,128)S(1)}, f32[192,128]{1,0:T(8,128)S(1)})) conditional(s32[]{:T(128)} %bitcast.11, (s32[2,128]{1,0:T(2,128)S(1)}, f32[2048,128]{1,0:T(8,128)S(1)}, s32[128,128]{1,0:T(8,128)S(1)}, s32[8,128]{1,0:T(8,128)S(1)}, f32[512,128]{1,0:T(8,128)S(1)}, ...), branch_computations={%region_0.0_spmd, %region_1.0_spmd} | conditional | flops 52494336 | bytes 7864328 | solution.py:483
  49.1 5.2 %branch_1_fun.2 = f32[768,128]{1,0:T(8,128)S(1)} custom-call(s32[2,128]{1,0:T(2,128)S(1)} %get-tuple-element.52.places, f32[2048,128]{1,0:T(8,128)S(1)} %get-tuple-element.53.arrived), custom_call_target="tpu_custom_call" | custom-call | flops 52428800 | bytes 2097152 | tf_op jit(solution)/shard_map/cond/branch_1_fun/pallas_call | solution.py:334
  54.3 16.5 %all_to_all.29 = f32[128,3,2,128]{3,2,1,0:T(2,128)S(1)} all-to-all(f32[128,3,2,128]{3,2,1,0:T(2,128)S(1)} %bitcast.30), channel_id=1, replica_groups=mesh['gx'=4,'gy'=4,'gz'=8] {'gx','gy','gz'}, dimensions={0} | all-to-all | bytes 786432 | tf_op jit(solution)/shard_map/cond/branch_1_fun/all_to_all | solution.py:354
  70.8 2.5 %branch_1_fun.3 = (f32[2048,128]{1,0:T(8,128)}, f32[512,128]{1,0:T(8,128)S(1)}, f32[192,128]{1,0:T(8,128)S(1)}, f32[192,128]{1,0:T(8,128)S(1)}) custom-call(s32[128,128]{1,0:T(8,128)S(1)} %get-tuple-element.50.wanted, s32[8,128]{1,0:T(8,128)S(1)} %get-tuple-element.51.asked, f32[768,128]{1,0:T(8,128)S(1)} %bitcast.29, ...), custom_call_target="tpu_custom_call" | custom-call | flops 65536 | bytes 4194304 | tf_op jit(solution)/shard_map/cond/branch_1_fun/pallas_call | solution.py:334
  73.3 4.6 %all-to-all-start.4 = ((f32[128,16,128]{2,1,0:T(8,128)}), f32[128,16,128]{2,1,0:T(8,128)S(1)}, u32[]{:S(2)}, u32[]{:S(2)}) async-start(f32[128,16,128]{2,1,0:T(8,128)} %bitcast.16), calls=%async_computation.4 | async-start | bytes 2097152 | tf_op jit(solution)/shard_map/all_to_all | solution.py:354
  77.8 3.3 %shard_map.98.refs_0_.local = f32[512,128]{1,0:T(8,128)S(1)} custom-call(s32[2,64]{1,0:T(2,128)S(1)} %get-tuple-element.97.pairs, f32[512,128]{1,0:T(8,128)S(1)} %get-tuple-element.94.state), custom_call_target="tpu_custom_call" | custom-call | flops 26214400 | bytes 1048576 | tf_op jit(solution)/shard_map/pallas_call | solution.py:334
  81.1 16.1 %all-to-all-done.4 = f32[128,16,128]{2,1,0:T(8,128)S(1)} async-done(((f32[128,16,128]{2,1,0:T(8,128)}), f32[128,16,128]{2,1,0:T(8,128)S(1)}, u32[]{:S(2)}, u32[]{:S(2)}) %all-to-all-start.4) | async-done | bytes 1048608 | tf_op jit(solution)/shard_map/all_to_all | solution.py:354
  97.2 5.2 %shard_map.99 = f32[1536,128]{1,0:T(8,128)S(1)} custom-call(s32[2,128]{1,0:T(2,128)S(1)} %get-tuple-element.85.places, f32[2048,128]{1,0:T(8,128)S(1)} %bitcast.24, f32[512,128]{1,0:T(8,128)S(1)} %shard_map.98.refs_0_.local), custom_call_target="tpu_custom_call" | custom-call | flops 52428800 | bytes 2097152 | tf_op jit(solution)/shard_map/pallas_call | solution.py:334
  102.4 20.7 %all_to_all.30 = f32[128,3,4,128]{3,2,1,0:T(4,128)S(1)} all-to-all(f32[128,3,4,128]{3,2,1,0:T(4,128)S(1)} %bitcast.28), channel_id=1, replica_groups=mesh['gx'=4,'gy'=4,'gz'=8] {'gx','gy','gz'}, dimensions={0} | all-to-all | bytes 1572864 | tf_op jit(solution)/shard_map/all_to_all | solution.py:354
  123.1 1.4 %shard_map.100 = (f32[3,8192]{1,0:T(4,128)}, f32[3,8192]{1,0:T(4,128)}, f32[3,8192]{1,0:T(4,128)}) custom-call(s32[8,128]{1,0:T(8,128)S(1)} %get-tuple-element.84.asked, f32[1536,128]{1,0:T(8,128)S(1)} %bitcast.25, f32[512,128]{1,0:T(8,128)S(1)} %shard_map.98.refs_0_.local, f32[192,128]{1,0:T(8,128)S(1)} %get-tuple-element.95.where, ...), custom_call_target="tpu_custom_call" | custom-call | flops 65536 | bytes 4194304 | tf_op jit(solution)/shard_map/pallas_call | solution.py:334
  (1 shorter events, 0.0 us)
Async XLA Ops:
  0.6 13.6 %copy-start.1 = (f32[3,8192]{1,0:T(4,128)S(1)}, f32[3,8192]{1,0:T(4,128)}, u32[]{:S(2)}) copy-start(f32[3,8192]{1,0:T(4,128)} %velocities.1) | copy-start | bytes 294916
  0.6 13.6 %copy-start.4 = (s32[8192]{0:T(1024)S(1)}, s32[8192]{0:T(1024)}, u32[]{:S(2)}) copy-start(s32[8192]{0:T(1024)} %param.12) | copy-start | bytes 98308
  0.7 13.6 %copy-start.5 = (f32[8192]{0:T(1024)S(1)}, f32[8192]{0:T(1024)}, u32[]{:S(2)}) copy-start(f32[8192]{0:T(1024)} %param.11) | copy-start | bytes 98308
  2.7 11.6 %copy-start = (f32[3,8192]{1,0:T(4,128)S(1)}, f32[3,8192]{1,0:T(4,128)}, u32[]{:S(2)}) copy-start(f32[3,8192]{1,0:T(4,128)} %positions.1) | copy-start | bytes 294916
  2.7 20.9 %all-to-all-start.2 = ((s32[128,1,128]{2,1,0:T(1,128)}), s32[128,1,128]{2,1,0:T(1,128)S(1)}, u32[]{:S(2)}, u32[]{:S(2)}) async-start(s32[128,1,128]{2,1,0:T(1,128)} %bitcast.44), calls=%async_computation.2 | async-start | bytes 131072 | tf_op jit(solution)/shard_map/all_to_all | solution.py:354
  14.2 0.7 copy-start.3
  14.2 0.7 copy-start.2
  25.2 4.6 %copy-start.6 = (s32[2,64,2]{1,2,0:T(2,128)S(1)}, s32[2,64,2]{1,2,0:T(2,128)}, u32[]{:S(2)}) copy-start(s32[2,64,2]{1,2,0:T(2,128)} %param.15) | copy-start | bytes 3076
  25.2 24.0 %all-to-all-start.3 = ((f32[128,16,128]{2,1,0:T(8,128)}), f32[128,16,128]{2,1,0:T(8,128)S(1)}, u32[]{:S(2)}, u32[]{:S(2)}) async-start(f32[128,16,128]{2,1,0:T(8,128)} %bitcast.12), calls=%async_computation.3 | async-start | bytes 2097152 | tf_op jit(solution)/shard_map/all_to_all | solution.py:354
  73.3 23.9 %all-to-all-start.4 = ((f32[128,16,128]{2,1,0:T(8,128)}), f32[128,16,128]{2,1,0:T(8,128)S(1)}, u32[]{:S(2)}, u32[]{:S(2)}) async-start(f32[128,16,128]{2,1,0:T(8,128)} %bitcast.16), calls=%async_computation.4 | async-start | bytes 2097152 | tf_op jit(solution)/shard_map/all_to_all | solution.py:354

commit v8 on v7

--- a/solution.py
+++ b/solution.py
@@ -317,19 +317,28 @@
     store_state(state, 3, masses[...])
 
 
-def finish_kernel(asked, returned, local, where, moving, bins, positions, velocities, accels, rows):
+def finish_kernel(
+    asked, returned, local, where, moving, bins, positions, velocities, accels, rows, *scratch
+):
+    staged, sems = scratch[:3], scratch[3]
     totals = summed(CAP, False, asked, returned)
     for index, *results in kick_drift(2, totals, local, where, moving, bins):
         for number, result in enumerate(results):
             rows[number, component(index), :] = result
-    for leaf in range(NLEAF):
-        lanes = slice(leaf * LEAF, (leaf + 1) * LEAF)
-        for number, out in enumerate((accels, velocities, positions)):
-            out[:, lanes] = rows[number, pl.ds(leaf, 3, stride=NLEAF), :]
+    copies = []
+    for number, out in enumerate((accels, velocities, positions)):
+        for leaf in range(NLEAF):
+            lanes = slice(leaf * LEAF, (leaf + 1) * LEAF)
+            staged[number][:, lanes] = rows[number, pl.ds(leaf, 3, stride=NLEAF), :]
+        copies.append(pltpu.make_async_copy(staged[number], out, sems.at[number]))
+        copies[-1].start()
+    for copy in copies:
+        copy.wait()
 
 
 def call(
-    kernel, out_shapes, arrays, flops, size, scratch=(), in_specs=None, scalars=(), vmem=40 * 2**20
+    kernel, out_shapes, arrays, flops, size, scratch=(), in_specs=None, scalars=(), vmem=40 * 2**20,
+    out_specs=None,
 ):
     return pl.pallas_call(
         kernel,
@@ -338,7 +347,7 @@
             num_scalar_prefetch=len(scalars),
             grid=(),
             in_specs=in_specs or [VMEM] * len(arrays),
-            out_specs=jax.tree.map(lambda _: VMEM, out_shapes),
+            out_specs=out_specs or jax.tree.map(lambda _: VMEM, out_shapes),
             scratch_shapes=scratch,
         ),
         compiler_params=pltpu.CompilerParams(vmem_limit_bytes=vmem),
@@ -494,7 +503,12 @@
         [asked, returned, local, where, moving, bins],
         2**16,
         2**22,
-        [pltpu.VMEM((3, 8 * NLEAF, LEAF), F32)],
+        [
+            pltpu.VMEM((3, 8 * NLEAF, LEAF), F32),
+            *[pltpu.VMEM((3, NLEAF * LEAF), F32)] * 3,
+            dma((3,)),
+        ],
+        out_specs=(anywhere,) * 3,
     )
 
 

time: 125 us -> 125 us (level)
  no operation moved by 1% of the time
where the time goes in v8:
time: 125 us
  waiting for transfers between devices  38.8 us (31%)
  blocking collectives  37.1 us (30%)
  Pallas kernels  25.8 us (21%)
  starting transfers between devices  20.7 us (17%)
  between operations  1.6 us (1%)
    all_to_all x3, waiting for transfers between devices, exchange(): return lax.all_to_all(array, AXES, split_axis=0, concat_axis=0, tiled=True)  38.8 us
    all_to_all x2, blocking collectives, exchange(): return lax.all_to_all(array, AXES, split_axis=0, concat_axis=0, tiled=True)  37.1 us
    pallas_call x9, Pallas kernels, call(): pl.pallas_call(kernel, out_shape=out_shapes, grid_spec=pltpu.PrefetchScal...  25.8 us
    all_to_all x3, starting transfers between devices, exchange(): return lax.all_to_all(array, AXES, split_axis=0, concat_axis=0, tiled=True)  20.7 us
  transfers between devices with their start and end apart: 3, of which 3 were waited for; matrix products, arithmetic and copies ran while one was open for 0% of the time, Pallas kernels for 6%

profile of v8, /device:TPU:1, one launch (start us, length us, event | category | flops | bytes accessed | tf_op | source)
XLA Modules:
  0.0 124.6 jit_solution(2003550662517437598)
XLA Ops:
  0.6 0.0 copy-start.1
  0.6 0.0 copy-start.4
  0.7 0.0 copy-start.5
  0.7 2.0 %shard_map.94 = (s32[2,128]{1,0:T(2,128)}, s32[2,128]{1,0:T(2,128)}, s32[128,128]{1,0:T(8,128)}) custom-call(s32[2,2,128]{2,1,0:T(2,128)} %bitcast.46, s32[2,2,128]{2,1,0:T(2,128)} %bitcast.47, s32[64,128]{1,0:T(8,128)} %bitcast.36), custom_call_target="tpu_custom_call" | custom-call | flops 67108864 | bytes 262144 | tf_op jit(solution)/shard_map/pallas_call | solution.py:343
  2.7 0.0 copy-start
  2.7 11.5 %all-to-all-start.2 = ((s32[128,1,128]{2,1,0:T(1,128)}), s32[128,1,128]{2,1,0:T(1,128)S(1)}, u32[]{:S(2)}, u32[]{:S(2)}) async-start(s32[128,1,128]{2,1,0:T(1,128)} %bitcast.44), calls=%async_computation.2 | async-start | bytes 131072 | tf_op jit(solution)/shard_map/all_to_all | solution.py:363
  14.2 0.0 copy-start.3
  14.2 0.0 copy-start.2
  14.2 0.0 copy-done.1
  14.3 0.0 copy-done.4
  14.3 0.0 copy-done.5
  14.3 0.0 copy-done
  14.3 0.6 copy-done.3
  14.9 0.0 copy-done.2
  14.9 1.4 %shard_map.95 = (f32[512,128]{1,0:T(8,128)S(1)}, f32[192,128]{1,0:T(8,128)S(1)}, f32[192,128]{1,0:T(8,128)S(1)}, s32[2,128]{1,0:T(2,128)S(1)}, s32[2,128]{1,0:T(...) custom-call(f32[3,8192]{1,0:T(4,128)S(1)} %copy-done, f32[3,8192]{1,0:T(4,128)S(1)} %copy-done.1, ...), custom_call_target="tpu_custom_call" | custom-call | flops 65536 | bytes 1048576 | tf_op jit(solution)/shard_map/pallas_call | solution.py:343
  16.3 7.3 %all-to-all-done.2 = s32[128,1,128]{2,1,0:T(1,128)S(1)} async-done(((s32[128,1,128]{2,1,0:T(1,128)}), s32[128,1,128]{2,1,0:T(1,128)S(1)}, u32[]{:S(2)}, u32[]{:S(2)}) %all-to-all-start.2) | async-done | bytes 65568 | tf_op jit(solution)/shard_map/all_to_all | solution.py:363
  23.6 1.5 %shard_map.96 = (f32[2048,128]{1,0:T(8,128)}, s32[8,128]{1,0:T(8,128)S(1)}, s32[1,1]{1,0:T(1,128)}) custom-call(s32[128,128]{1,0:T(8,128)S(1)} %bitcast.33, f32[512,128]{1,0:T(8,128)S(1)} %get-tuple-element.83.ordered), custom_call_target="tpu_custom_call" | custom-call | flops 65536 | bytes 2097152 | tf_op jit(solution)/shard_map/pallas_call | solution.py:343
  25.2 0.0 copy-start.6
  25.2 4.6 %all-to-all-start.3 = ((f32[128,16,128]{2,1,0:T(8,128)}), f32[128,16,128]{2,1,0:T(8,128)S(1)}, u32[]{:S(2)}, u32[]{:S(2)}) async-start(f32[128,16,128]{2,1,0:T(8,128)} %bitcast.12), calls=%async_computation.3 | async-start | bytes 2097152 | tf_op jit(solution)/shard_map/all_to_all | solution.py:363
  29.8 0.0 copy-done.6
  29.8 3.3 %shard_map.97 = f32[512,128]{1,0:T(8,128)S(1)} custom-call(s32[2,64]{1,0:T(2,128)S(1)} %get-tuple-element.98.pairs, f32[512,128]{1,0:T(8,128)S(1)} %get-tuple-element.89.state), custom_call_target="tpu_custom_call" | custom-call | flops 26214400 | bytes 1048576 | tf_op jit(solution)/shard_map/pallas_call | solution.py:343
  33.7 15.4 %all-to-all-done.3 = f32[128,16,128]{2,1,0:T(8,128)S(1)} async-done(((f32[128,16,128]{2,1,0:T(8,128)}), f32[128,16,128]{2,1,0:T(8,128)S(1)}, u32[]{:S(2)}, u32[]{:S(2)}) %all-to-all-start.3) | async-done | bytes 1048608 | tf_op jit(solution)/shard_map/all_to_all | solution.py:363
  49.1 24.1 %conditional.1 = ((f32[2048,128]{1,0:T(8,128)}, f32[512,128]{1,0:T(8,128)S(1)}, f32[192,128]{1,0:T(8,128)S(1)}, f32[192,128]{1,0:T(8,128)S(1)})) conditional(s32[]{:T(128)} %bitcast.11, (s32[2,128]{1,0:T(2,128)S(1)}, f32[2048,128]{1,0:T(8,128)S(1)}, s32[128,128]{1,0:T(8,128)S(1)}, s32[8,128]{1,0:T(8,128)S(1)}, f32[512,128]{1,0:T(8,128)S(1)}, ...), branch_computations={%region_0.0_spmd, %region_1.0_spmd} | conditional | flops 52494336 | bytes 7864328 | solution.py:492
  49.1 5.2 %branch_1_fun.2 = f32[768,128]{1,0:T(8,128)S(1)} custom-call(s32[2,128]{1,0:T(2,128)S(1)} %get-tuple-element.52.places, f32[2048,128]{1,0:T(8,128)S(1)} %get-tuple-element.53.arrived), custom_call_target="tpu_custom_call" | custom-call | flops 52428800 | bytes 2097152 | tf_op jit(solution)/shard_map/cond/branch_1_fun/pallas_call | solution.py:343
  54.3 16.5 %all_to_all.29 = f32[128,3,2,128]{3,2,1,0:T(2,128)S(1)} all-to-all(f32[128,3,2,128]{3,2,1,0:T(2,128)S(1)} %bitcast.30), channel_id=1, replica_groups=mesh['gx'=4,'gy'=4,'gz'=8] {'gx','gy','gz'}, dimensions={0} | all-to-all | bytes 786432 | tf_op jit(solution)/shard_map/cond/branch_1_fun/all_to_all | solution.py:363
  70.8 2.5 %branch_1_fun.3 = (f32[2048,128]{1,0:T(8,128)}, f32[512,128]{1,0:T(8,128)S(1)}, f32[192,128]{1,0:T(8,128)S(1)}, f32[192,128]{1,0:T(8,128)S(1)}) custom-call(s32[128,128]{1,0:T(8,128)S(1)} %get-tuple-element.50.wanted, s32[8,128]{1,0:T(8,128)S(1)} %get-tuple-element.51.asked, f32[768,128]{1,0:T(8,128)S(1)} %bitcast.29, ...), custom_call_target="tpu_custom_call" | custom-call | flops 65536 | bytes 4194304 | tf_op jit(solution)/shard_map/cond/branch_1_fun/pallas_call | solution.py:343
  73.3 4.6 %all-to-all-start.4 = ((f32[128,16,128]{2,1,0:T(8,128)}), f32[128,16,128]{2,1,0:T(8,128)S(1)}, u32[]{:S(2)}, u32[]{:S(2)}) async-start(f32[128,16,128]{2,1,0:T(8,128)} %bitcast.16), calls=%async_computation.4 | async-start | bytes 2097152 | tf_op jit(solution)/shard_map/all_to_all | solution.py:363
  77.8 3.3 %shard_map.98.refs_0_.local = f32[512,128]{1,0:T(8,128)S(1)} custom-call(s32[2,64]{1,0:T(2,128)S(1)} %get-tuple-element.97.pairs, f32[512,128]{1,0:T(8,128)S(1)} %get-tuple-element.94.state), custom_call_target="tpu_custom_call" | custom-call | flops 26214400 | bytes 1048576 | tf_op jit(solution)/shard_map/pallas_call | solution.py:343
  81.1 16.1 %all-to-all-done.4 = f32[128,16,128]{2,1,0:T(8,128)S(1)} async-done(((f32[128,16,128]{2,1,0:T(8,128)}), f32[128,16,128]{2,1,0:T(8,128)S(1)}, u32[]{:S(2)}, u32[]{:S(2)}) %all-to-all-start.4) | async-done | bytes 1048608 | tf_op jit(solution)/shard_map/all_to_all | solution.py:363
  97.2 5.3 %shard_map.99 = f32[1536,128]{1,0:T(8,128)S(1)} custom-call(s32[2,128]{1,0:T(2,128)S(1)} %get-tuple-element.85.places, f32[2048,128]{1,0:T(8,128)S(1)} %bitcast.24, f32[512,128]{1,0:T(8,128)S(1)} %shard_map.98.refs_0_.local), custom_call_target="tpu_custom_call" | custom-call | flops 52428800 | bytes 2097152 | tf_op jit(solution)/shard_map/pallas_call | solution.py:343
  102.4 20.7 %all_to_all.30 = f32[128,3,4,128]{3,2,1,0:T(4,128)S(1)} all-to-all(f32[128,3,4,128]{3,2,1,0:T(4,128)S(1)} %bitcast.28), channel_id=1, replica_groups=mesh['gx'=4,'gy'=4,'gz'=8] {'gx','gy','gz'}, dimensions={0} | all-to-all | bytes 1572864 | tf_op jit(solution)/shard_map/all_to_all | solution.py:363
  123.1 1.4 %shard_map.100 = (f32[3,8192]{1,0:T(4,128)}, f32[3,8192]{1,0:T(4,128)}, f32[3,8192]{1,0:T(4,128)}) custom-call(s32[8,128]{1,0:T(8,128)S(1)} %get-tuple-element.84.asked, f32[1536,128]{1,0:T(8,128)S(1)} %bitcast.25, f32[512,128]{1,0:T(8,128)S(1)} %shard_map.98.refs_0_.local, f32[192,128]{1,0:T(8,128)S(1)} %get-tuple-element.95.where, ...), custom_call_target="tpu_custom_call" | custom-call | flops 65536 | bytes 4194304 | tf_op jit(solution)/shard_map/pallas_call | solution.py:343
  (1 shorter events, 0.0 us)
Async XLA Ops:
  0.6 13.6 %copy-start.1 = (f32[3,8192]{1,0:T(4,128)S(1)}, f32[3,8192]{1,0:T(4,128)}, u32[]{:S(2)}) copy-start(f32[3,8192]{1,0:T(4,128)} %velocities.1) | copy-start | bytes 294916
  0.6 13.6 %copy-start.4 = (s32[8192]{0:T(1024)S(1)}, s32[8192]{0:T(1024)}, u32[]{:S(2)}) copy-start(s32[8192]{0:T(1024)} %param.12) | copy-start | bytes 98308
  0.7 13.6 %copy-start.5 = (f32[8192]{0:T(1024)S(1)}, f32[8192]{0:T(1024)}, u32[]{:S(2)}) copy-start(f32[8192]{0:T(1024)} %param.11) | copy-start | bytes 98308
  2.7 11.6 %copy-start = (f32[3,8192]{1,0:T(4,128)S(1)}, f32[3,8192]{1,0:T(4,128)}, u32[]{:S(2)}) copy-start(f32[3,8192]{1,0:T(4,128)} %positions.1) | copy-start | bytes 294916
  2.7 20.9 %all-to-all-start.2 = ((s32[128,1,128]{2,1,0:T(1,128)}), s32[128,1,128]{2,1,0:T(1,128)S(1)}, u32[]{:S(2)}, u32[]{:S(2)}) async-start(s32[128,1,128]{2,1,0:T(1,128)} %bitcast.44), calls=%async_computation.2 | async-start | bytes 131072 | tf_op jit(solution)/shard_map/all_to_all | solution.py:363
  14.2 0.7 copy-start.3
  14.2 0.7 copy-start.2
  25.2 4.6 %copy-start.6 = (s32[2,64,2]{1,2,0:T(2,128)S(1)}, s32[2,64,2]{1,2,0:T(2,128)}, u32[]{:S(2)}) copy-start(s32[2,64,2]{1,2,0:T(2,128)} %param.15) | copy-start | bytes 3076
  25.2 24.0 %all-to-all-start.3 = ((f32[128,16,128]{2,1,0:T(8,128)}), f32[128,16,128]{2,1,0:T(8,128)S(1)}, u32[]{:S(2)}, u32[]{:S(2)}) async-start(f32[128,16,128]{2,1,0:T(8,128)} %bitcast.12), calls=%async_computation.3 | async-start | bytes 2097152 | tf_op jit(solution)/shard_map/all_to_all | solution.py:363
  73.3 23.9 %all-to-all-start.4 = ((f32[128,16,128]{2,1,0:T(8,128)}), f32[128,16,128]{2,1,0:T(8,128)S(1)}, u32[]{:S(2)}, u32[]{:S(2)}) async-start(f32[128,16,128]{2,1,0:T(8,128)} %bitcast.16), calls=%async_computation.4 | async-start | bytes 2097152 | tf_op jit(solution)/shard_map/all_to_all | solution.py:363
